TPU v7x, 32 devices: a whole 2x2x4 slice. The times are simulated.
32 devices in a mesh: rep: 16 (over z, y, x), tp: 2 (over core).
Axes of the slice: x: 2, y: 2, z: 4, core: 2. Of those that a mesh axis runs over, the one named last changes fastest.
Arguments:
- kv_pool: bfloat16 [256, 128, 1024], P('rep', None, 'tp'), may hold values from -6 to 6
- page_table: int32 [64, 4], P('rep'), may hold values from 0 to 15, as said below
- req_lengths: int32 [64], P('rep'), may hold values from 1 to 511, as said below
- leave_slot: int32 [16], P('rep'), may hold values from 0 to 3
- target_rep: int32 [16], P('rep'), may hold values from 0 to 15, as said below
- qkv_new: bfloat16 [64, 2560], P('rep', 'tp'), may hold values from -8.2 to 8.2
- residual_in: bfloat16 [64, 1536], P('rep'), may hold values from -6 to 6
- expert_ids: int32 [64, 1], P('rep'), may hold values from 0 to 1
- gate_weights: bfloat16 [64, 1], P('rep'), may hold values from 0.099609375 to 0.69921875
- norm_gain: float32 [1536], replicated, may hold values from 0.1 to 1.9
- out_proj: bfloat16 [1536, 1536], P('tp'), may hold values from -0.15625 to 0.15625
- expert_in: bfloat16 [2, 1536, 512], P('tp'), may hold values from -0.15625 to 0.15625
- expert_down: bfloat16 [2, 256, 1536], P('tp'), may hold values from -0.375 to 0.375
Outputs:
- hidden_out: bfloat16 [64, 1536], P('rep', 'tp')
- new_pages: bfloat16 [64, 128, 1024], P('rep', None, 'tp')
- arrived: bfloat16 [64, 128, 1024], P('rep', None, 'tp')
Inputs may be any that keep to these rules, and one draw needn't show every extreme that they name: `req_lengths`: in every draw the request that leaves some replica has length 511. `page_table`: the 4 rows of one replica hold each of its 16 pool pages once. `target_rep`: the targets form one cycle through all replicas: every replica receives exactly one request and none keeps its own; in every draw some replica sends to the replica half the axis of replicas away.
All inputs are finite; a program needn't handle non-finite values.
Results may differ from a plain program's by a relative error of at most 0.005.
Values may be sent and summed in bfloat16 or wider, within the bound.
No kernel may reach another device: no remote copies, remote signals or barrier semaphores. Data moves between devices by JAX's collectives and lax.ppermute only.
A program may use at most 64 MiB of HBM per device.

v0:
```python
import math

import jax
import jax.numpy as jnp
from jax import lax
from jax.sharding import PartitionSpec as P

QH = 24
KVH = 8
HD = 64
FF = 256
PAGE = 128
MAXP = 4


def spread_slot(member, slot_mask):
    out_shape = (slot_mask.shape[0],) + (1,) * (member.ndim - 1)
    return jnp.where(slot_mask.reshape(out_shape), member, jnp.zeros((), member.dtype))


def fold_sum(member):
    if member.dtype == jnp.int32:
        return jnp.sum(member, axis=0, keepdims=True)
    return jnp.sum(member.astype(jnp.float32), axis=0, keepdims=True).astype(member.dtype)


def migrate(pages_out, row_data, resid_row, gate_row, int_row):
    slot_mask = jnp.arange(lax.axis_size("rep"), dtype=jnp.int32) == int_row[0, 1]
    landed = (
        lax.all_to_all(
            spread_slot(pages_out, slot_mask), "rep", split_axis=0, concat_axis=0, tiled=True
        ),
        lax.all_to_all(
            spread_slot(row_data, slot_mask), "rep", split_axis=0, concat_axis=0, tiled=True
        ),
        lax.all_to_all(
            spread_slot(resid_row, slot_mask), "rep", split_axis=0, concat_axis=0, tiled=True
        ),
        lax.all_to_all(
            spread_slot(gate_row, slot_mask), "rep", split_axis=0, concat_axis=0, tiled=True
        ),
        lax.all_to_all(
            spread_slot(int_row, slot_mask), "rep", split_axis=0, concat_axis=0, tiled=True
        ),
    )
    return tuple((fold_sum(member) for member in landed))


def write_token(cache_rows, new_kv, lengths):
    positions = jnp.arange(cache_rows.shape[1], dtype=jnp.int32)
    at_token = positions[None, :] == lengths[:, None]
    return jnp.where(at_token[:, :, None], new_kv[:, None, :], cache_rows)


def attend(queries, cache_rows, lengths):
    num_req, span_len, col_count = cache_rows.shape
    head_count = queries.shape[1]
    split_cache = cache_rows.reshape(num_req, span_len, head_count, 2, HD)
    scores = jnp.einsum(
        "rhgd,rlhd->rhgl", queries, split_cache[:, :, :, 0, :], preferred_element_type=jnp.float32
    ) * (1.0 / math.sqrt(HD))
    positions = jnp.arange(span_len, dtype=jnp.int32)
    visible = positions[None, :] <= lengths[:, None]
    scores = jnp.where(visible[:, None, None, :], scores, -jnp.inf)
    top_score = jnp.max(scores, axis=-1, keepdims=True)
    weights = jnp.exp(scores - top_score)
    probs = (weights / jnp.sum(weights, axis=-1, keepdims=True)).astype(jnp.bfloat16)
    attn_rows = jnp.einsum(
        "rhgl,rlhd->rhgd", probs, split_cache[:, :, :, 1, :], preferred_element_type=jnp.float32
    )
    return attn_rows.astype(jnp.bfloat16).reshape(num_req, -1)


def page_at(cache_rows, lengths):
    num_req, span_len, col_count = cache_rows.shape
    paged = cache_rows.reshape(num_req, span_len // PAGE, PAGE, col_count)
    return jnp.take_along_axis(paged, (lengths // PAGE)[:, None, None, None], axis=1)[:, 0]


def local(
    kv_pool,
    page_table,
    req_lengths,
    leave_slot,
    target_rep,
    qkv_new,
    residual_in,
    expert_ids,
    gate_weights,
    norm_gain,
    out_proj,
    expert_in,
    expert_down,
):
    num_req = residual_in.shape[0]
    group = QH // KVH
    head_local = kv_pool.shape[2] // (2 * HD)
    slot_hit = jnp.arange(num_req, dtype=jnp.int32) == leave_slot[0]
    own_cache = kv_pool[page_table].reshape(num_req, MAXP * PAGE, -1)
    int_row = jnp.concatenate(
        [req_lengths[leave_slot][:, None], target_rep[:, None], expert_ids[leave_slot]], axis=1
    )
    resid_row = residual_in[leave_slot]
    gate_row = gate_weights[leave_slot]
    pages_out = kv_pool[page_table[leave_slot[0]]][None]
    got_pages, got_qkv, got_resid, got_gates, got_ints = migrate(
        pages_out, qkv_new[leave_slot], resid_row, gate_row, int_row
    )
    cache_now = jnp.where(slot_hit[:, None, None], got_pages.reshape(1, MAXP * PAGE, -1), own_cache)
    qkv_now = jnp.where(slot_hit[:, None], got_qkv, qkv_new).reshape(
        num_req, head_local, group + 2, HD
    )
    len_now = jnp.where(slot_hit, got_ints[0, 0], req_lengths)
    cache_now = write_token(cache_now, qkv_now[:, :, group:, :].reshape(num_req, -1), len_now)
    attn_rows = attend(qkv_now[:, :, :group, :], cache_now, len_now)
    new_pages = page_at(cache_now, len_now)
    arrived_pages = cache_now[leave_slot[0]].reshape(MAXP, PAGE, -1)
    resid_now = jnp.where(slot_hit[:, None], got_resid, residual_in)
    gates_now = jnp.where(slot_hit[:, None], got_gates, gate_weights)
    ids_now = jnp.where(slot_hit[:, None], got_ints[:, 2:], expert_ids)
    head_part = jnp.dot(attn_rows, out_proj, preferred_element_type=jnp.float32)
    tp_index = lax.axis_index("tp")
    col_count = norm_gain.shape[0] // lax.axis_size("tp")
    stream_full = resid_now.astype(jnp.float32) + lax.psum(head_part, "tp")
    mean_sq = jnp.mean(stream_full * stream_full, axis=1, keepdims=True)
    normed = (stream_full * lax.rsqrt(mean_sq + 1e-05) * norm_gain).astype(jnp.bfloat16)
    stream_share = lax.dynamic_slice_in_dim(stream_full, tp_index * col_count, col_count, 1)
    expert_local = expert_in.shape[0]
    expert_number = tp_index * expert_local + 0
    route_share = jnp.sum(
        jnp.where(ids_now == expert_number, gates_now.astype(jnp.float32), 0.0), axis=1
    )
    up_both = jnp.dot(normed, expert_in[0], preferred_element_type=jnp.float32)
    acted = (jax.nn.silu(up_both[:, :FF]) * up_both[:, FF:]).astype(jnp.bfloat16)
    expert_total = route_share[:, None] * jnp.dot(
        acted, expert_down[0], preferred_element_type=jnp.float32
    )
    moe_share = lax.psum_scatter(expert_total, "tp", scatter_dimension=1, tiled=True)
    hidden_out = (stream_share + moe_share).astype(jnp.bfloat16)
    return (hidden_out, new_pages, arrived_pages)


def solution(mesh):
    return jax.shard_map(
        local,
        mesh=mesh,
        in_specs=(
            P("rep", None, "tp"),
            P("rep", None),
            P("rep"),
            P("rep"),
            P("rep"),
            P("rep", "tp"),
            P("rep", None),
            P("rep", None),
            P("rep", None),
            P(),
            P("tp", None),
            P("tp", None, None),
            P("tp", None, None),
        ),
        out_specs=(P("rep", "tp"), P("rep", None, "tp"), P("rep", None, "tp")),
        check_vma=False,
    )
```

profile of v0, /device:TPU:0, one launch (start us, length us, event | category | flops | bytes accessed | tf_op | source)
XLA Modules:
  0.0 286.3 jit_solution(13827431698050089674)
XLA Ops:
  8.6 1.2 constant_dynamic-slice_fusion.1
  9.9 1.2 compare_select_fusion
  11.0 8.3 %all-to-all-start.4 = ((bf16[16,1,1]{2,1,0:T(2,128)(2,1)}), bf16[16,1,1]{2,1,0:T(2,128)(2,1)S(1)}, u32[]{:S(2)}, u32[]{:S(2)}) async-start(bf16[16,1,1]{2,1,0:T(2,128)(2,1)} %compare_select_fusion), calls=%async_computation.4 | async-start | bytes 16384 | tf_op jit(solution)/shard_map/all_to_all | solution.py:39
  19.3 1.2 constant_dynamic-slice_fusion.2
  20.6 1.3 dynamic-slice.15
  21.9 0.7 dynamic-slice_reduce_fusion.1
  22.6 1.3 add_bitcast_fusion.1
  23.8 0.7 broadcast_select_fusion.4
  24.5 0.1 broadcast_select_fusion.3
  24.7 0.7 dynamic-slice_reduce_fusion
  25.4 0.1 broadcast_select_fusion.2
  25.6 1.0 all-to-all-done.4
  26.5 6.0 %all-to-all-start.1 = ((s32[16,1,3]{2,1,0:T(1,128)}), s32[16,1,3]{2,1,0:T(1,128)S(1)}, u32[]{:S(2)}, u32[]{:S(2)}) async-start(s32[16,1,3]{2,1,0:T(1,128)} %broadcast_select_fusion.4), calls=%async_computation.1 | async-start | bytes 16384 | tf_op jit(solution)/shard_map/all_to_all | solution.py:42
  32.5 0.7 fusion.19
  33.2 0.5 broadcast.403
  33.7 0.9 reduce.13
  34.6 0.6 reshape.502
  35.2 0.9 reduce.14
  36.1 0.6 reshape.504
  36.8 3.0 %all-to-all-done.1 = s32[16,1,3]{2,1,0:T(1,128)S(1)} async-done(((s32[16,1,3]{2,1,0:T(1,128)}), s32[16,1,3]{2,1,0:T(1,128)S(1)}, u32[]{:S(2)}, u32[]{:S(2)}) %all-to-all-start.1) | async-done | bytes 224 | tf_op jit(solution)/shard_map/all_to_all | solution.py:42
  39.8 3.9 %all-to-all-start.2 = ((bf16[16,2,640]{2,1,0:T(2,128)(2,1)}), bf16[16,2,640]{2,1,0:T(2,128)(2,1)S(1)}, u32[]{:S(2)}, u32[]{:S(2)}) async-start(bf16[16,2,640]{2,1,0:T(2,128)(2,1)} %reshape.502), calls=%async_computation.2 | async-start | bytes 81920 | tf_op jit(solution)/shard_map/all_to_all | solution.py:33
  43.7 2.2 gather_fusion
  45.9 5.2 %all-to-all-done.2 = bf16[16,2,640]{2,1,0:T(2,128)(2,1)S(1)} async-done(((bf16[16,2,640]{2,1,0:T(2,128)(2,1)}), bf16[16,2,640]{2,1,0:T(2,128)(2,1)S(1)}, u32[]{:S(2)}, u32[]{:S(2)}) %all-to-all-start.2) | async-done | bytes 40992 | tf_op jit(solution)/shard_map/all_to_all | solution.py:33
  51.1 3.5 %all-to-all-start = ((bf16[16,2,768]{2,1,0:T(2,128)(2,1)}), bf16[16,2,768]{2,1,0:T(2,128)(2,1)S(1)}, u32[]{:S(2)}, u32[]{:S(2)}) async-start(bf16[16,2,768]{2,1,0:T(2,128)(2,1)} %reshape.504), calls=%async_computation | async-start | bytes 98304 | tf_op jit(solution)/shard_map/all_to_all | solution.py:36
  54.6 4.0 %broadcast_select_fusion = bf16[16,4,128,512]{3,2,1,0:T(8,128)(2,1)} fusion(pred[16]{0:T(512)(128)(4,1)S(1)} %iota_compare_fusion.2, bf16[4,128,512]{2,1,0:T(8,128)(2,1)S(1)} %gather_fusion), kind=kLoop, calls=%fused_computation.4 | loop fusion | flops 4194304 | bytes 8912912 | tf_op jit(solution)/shard_map/jit(_where)/select_n | solution.py:18
  58.6 3.5 %all-to-all-done = bf16[16,2,768]{2,1,0:T(2,128)(2,1)S(1)} async-done(((bf16[16,2,768]{2,1,0:T(2,128)(2,1)}), bf16[16,2,768]{2,1,0:T(2,128)(2,1)S(1)}, u32[]{:S(2)}, u32[]{:S(2)}) %all-to-all-start) | async-done | bytes 49184 | tf_op jit(solution)/shard_map/all_to_all | solution.py:36
  62.1 4.7 %all-to-all-start.3 = ((bf16[16,4,128,512]{3,2,1,0:T(8,128)(2,1)}), bf16[16,4,128,512]{3,2,1,0:T(8,128)(2,1)}, u32[]{:S(2)}, u32[]{:S(2)}) async-start(bf16[16,4,128,512]{3,2,1,0:T(8,128)(2,1)} %broadcast_select_fusion), calls=%async_computation.3 | async-start | bytes 16777216 | tf_op jit(solution)/shard_map/all_to_all | solution.py:30
  66.9 0.1 reshape.477
  67.0 3.6 %gather_fusion.1 = bf16[16,128,512]{2,1,0:T(8,128)(2,1)} fusion(bf16[16,128,512]{2,1,0:T(8,128)(2,1)} %param.13, s32[1024]{0:T(1024)S(1)} %pad_clamp_fusion), kind=kCustom, calls=%fused_computation.1 | custom fusion | bytes 4194368 | tf_op jit(solution)/shard_map/gather | solution.py:99
  70.6 8.9 %reshape.497 = bf16[4,512,4,2,64]{4,3,2,1,0:T(2,128)(2,1)} reshape(bf16[16,128,512]{2,1,0:T(8,128)(2,1)} %gather_fusion.1) | data formatting | bytes 4194304 | tf_op jit(solution)/shard_map/reshape | solution.py:99
  79.5 10.6 %copy.54 = bf16[4,512,4,2,64]{1,4,2,0,3:T(8,128)(2,1)} copy(bf16[4,512,4,2,64]{4,3,2,1,0:T(2,128)(2,1)} %reshape.497) | data formatting | bytes 4194304 | tf_op jit(solution)/shard_map/reshape | solution.py:99
  90.1 0.6 dynamic-slice.19
  90.7 0.6 reduce_sum.81
  91.4 0.7 fusion.21
  92.0 0.7 compare_and_fusion
  92.8 1.3 fusion.18
  94.3 0.1 reduce_sum.78
  94.4 0.1 broadcast_select_fusion.5
  94.5 0.1 reshape.359
  94.6 0.1 broadcast_in_dim.301
  94.7 0.1 reduce_sum.76
  94.8 120.9 %all-to-all-done.3 = bf16[16,4,128,512]{3,2,1,0:T(8,128)(2,1)} async-done(((bf16[16,4,128,512]{3,2,1,0:T(8,128)(2,1)}), bf16[16,4,128,512]{3,2,1,0:T(8,128)(2,1)}, u32[]{:S(2)}, u32[]{:S(2)}) %all-to-all-start.3) | async-done | bytes 8388640 | tf_op jit(solution)/shard_map/all_to_all | solution.py:30
  215.7 5.0 %reduce.8 = bf16[4,128,512]{2,1,0:T(8,128)(2,1)S(1)} reduce(bf16[16,4,128,512]{3,2,1,0:T(8,128)(2,1)} %all-to-all-done.3, bf16[]{:T(256)} %constant.25.clone.1), dimensions={0}, to_apply=%region_3.4.clone | reduce | flops 3932160 | bytes 8912898 | tf_op jit(solution)/shard_map/reduce_sum | solution.py:24
  220.7 1.5 reshape.496
  222.3 2.4 copy.52
  224.7 1.9 select_select_fusion.1
  226.6 1.3 copy-done.1
  228.0 0.2 fusion.5
  228.2 0.2 fusion.22
  228.4 1.7 convolution_convert_fusion
  230.1 0.1 reshape.361
  230.2 0.4 fusion.23
  230.6 3.4 %psum.7 = f32[4,1536]{1,0:T(4,128)S(1)} all-reduce(f32[4,1536]{1,0:T(4,128)S(1)} %fusion.23), channel_id=1, replica_groups=mesh['rep'=16,'tp'=2] {'tp'}, use_global_device_ids=true, to_apply=%region_6.7 | all-reduce | flops 6144 | bytes 49152 | tf_op jit(solution)/shard_map/psum | solution.py:124
  234.1 0.2 multiply_reduce_fusion
  234.3 1.8 fusion.1
  236.1 1.3 convolution_multiply_fusion
  237.4 1.2 copy.60
  238.6 2.8 select_select_fusion
  241.4 2.2 gather_fusion.2
  243.6 2.5 fusion.7
  246.2 0.9 broadcast_select_fusion.1
  247.1 30.7 %reduce-scatter.4.cloned.1.call-done = f32[768,4]{1,0:T(8,128)} async-done(((f32[1536,4]{1,0:T(8,128)}), f32[768,4]{1,0:T(8,128)}) %reduce-scatter.4.cloned.1.call-update) | async-done | bytes 12304
  277.7 1.1 copy.61
  278.9 0.6 add_convert_fusion
  (38 shorter events, 0.5 us)
Async XLA Ops:
  7.2 223.1 %copy-start = (bf16[768,1536]{1,0:T(8,128)(2,1)S(1)}, bf16[768,1536]{1,0:T(8,128)(2,1)}, u32[]{:S(2)}) copy-start(bf16[768,1536]{1,0:T(8,128)(2,1)} %param.23) | copy-start | bytes 7077892
  11.0 15.5 %all-to-all-start.4 = ((bf16[16,1,1]{2,1,0:T(2,128)(2,1)}), bf16[16,1,1]{2,1,0:T(2,128)(2,1)S(1)}, u32[]{:S(2)}, u32[]{:S(2)}) async-start(bf16[16,1,1]{2,1,0:T(2,128)(2,1)} %compare_select_fusion), calls=%async_computation.4 | async-start | bytes 16384 | tf_op jit(solution)/shard_map/all_to_all | solution.py:39
  26.5 13.2 %all-to-all-start.1 = ((s32[16,1,3]{2,1,0:T(1,128)}), s32[16,1,3]{2,1,0:T(1,128)S(1)}, u32[]{:S(2)}, u32[]{:S(2)}) async-start(s32[16,1,3]{2,1,0:T(1,128)} %broadcast_select_fusion.4), calls=%async_computation.1 | async-start | bytes 16384 | tf_op jit(solution)/shard_map/all_to_all | solution.py:42
  39.8 11.3 %all-to-all-start.2 = ((bf16[16,2,640]{2,1,0:T(2,128)(2,1)}), bf16[16,2,640]{2,1,0:T(2,128)(2,1)S(1)}, u32[]{:S(2)}, u32[]{:S(2)}) async-start(bf16[16,2,640]{2,1,0:T(2,128)(2,1)} %reshape.502), calls=%async_computation.2 | async-start | bytes 81920 | tf_op jit(solution)/shard_map/all_to_all | solution.py:33
  51.1 10.9 %all-to-all-start = ((bf16[16,2,768]{2,1,0:T(2,128)(2,1)}), bf16[16,2,768]{2,1,0:T(2,128)(2,1)S(1)}, u32[]{:S(2)}, u32[]{:S(2)}) async-start(bf16[16,2,768]{2,1,0:T(2,128)(2,1)} %reshape.504), calls=%async_computation | async-start | bytes 98304 | tf_op jit(solution)/shard_map/all_to_all | solution.py:36
  58.6 8.3 %copy-start.5 = (s32[4,4]{1,0:T(4,128)S(1)}, s32[4,4]{1,0:T(4,128)}, u32[]{:S(2)}) copy-start(s32[4,4]{1,0:T(4,128)} %param.14) | copy-start | bytes 196
  62.1 153.7 %all-to-all-start.3 = ((bf16[16,4,128,512]{3,2,1,0:T(8,128)(2,1)}), bf16[16,4,128,512]{3,2,1,0:T(8,128)(2,1)}, u32[]{:S(2)}, u32[]{:S(2)}) async-start(bf16[16,4,128,512]{3,2,1,0:T(8,128)(2,1)} %broadcast_select_fusion), calls=%async_computation.3 | async-start | bytes 16777216 | tf_op jit(solution)/shard_map/all_to_all | solution.py:30
  66.8 210.9 %reduce-scatter.4.cloned.1.call-start = ((), (), s32[]{:S(2)}) async-start(), calls=%async_computation.6 | async-start | bytes 1179648
  79.5 12.6 %copy-start.8 = (s32[4]{0:T(128)S(1)}, s32[4]{0:T(128)}, u32[]{:S(2)}) copy-start(s32[4]{0:T(128)} %param.15) | copy-start | bytes 52
  79.5 13.4 %copy-start.6 = (bf16[4,1]{0,1:T(2,128)(2,1)S(1)}, bf16[4,1]{0,1:T(2,128)(2,1)}, u32[]{:S(2)}) copy-start(bf16[4,1]{0,1:T(2,128)(2,1)} %param.21) | copy-start | bytes 28
  79.5 13.4 %copy-start.7 = (s32[4,1]{0,1:T(1,128)S(1)}, s32[4,1]{0,1:T(1,128)}, u32[]{:S(2)}) copy-start(s32[4,1]{0,1:T(1,128)} %param.20) | copy-start | bytes 52
  79.5 14.9 %copy-start.3 = (bf16[4,1280]{1,0:T(4,128)(2,1)S(1)}, bf16[4,1280]{1,0:T(4,128)(2,1)}, u32[]{:S(2)}) copy-start(bf16[4,1280]{1,0:T(4,128)(2,1)} %param.18) | copy-start | bytes 30724
  226.6 1.4 copy-start.1
  228.4 5.7 %copy-start.2 = (bf16[4,1536]{1,0:T(4,128)(2,1)S(1)}, bf16[4,1536]{1,0:T(4,128)(2,1)}, u32[]{:S(2)}) copy-start(bf16[4,1536]{1,0:T(4,128)(2,1)} %param.19) | copy-start | bytes 36868
  228.4 5.9 %copy-start.4 = (f32[1536]{0:T(1024)S(1)}, f32[1536]{0:T(1024)}, u32[]{:S(2)}) copy-start(f32[1536]{0:T(1024)} %param.22) | copy-start | bytes 18436
Sparse Core Ops, SparseCore 0:
  238.8 38.9 reduce-scatter.3
where the time goes:
time: 288 us; the launch traced here: 286 us
  waiting for transfers between devices  164 us (57%)
  local copies, waits for them, and re-layouts  43.8 us (15%)
  other arithmetic  27.2 us (9%)
  starting transfers between devices  26.5 us (9%)
  between operations  15.8 us (5%)
  matrix products  5.44 us (2%)
  blocking collectives  3.42 us (1%)
    all_to_all x1, waiting for transfers between devices, migrate(): lax.all_to_all(spread_slot(pages_out, slot_mask), 'rep', split_axis=0, co...  121 us
    unnamed x2, waiting for transfers between devices  30.7 us
    reshape x2, local copies, waits for them, and re-layouts, local(): own_cache = kv_pool[page_table].reshape(num_req, MAXP * PAGE, -1)  19.5 us
    all_to_all x1, starting transfers between devices, migrate(): lax.all_to_all(spread_slot(gate_row, slot_mask), 'rep', split_axis=0, con...  8.31 us
    select_n x7, other arithmetic, spread_slot(): jnp.where(slot_mask.reshape(out_shape), member, jnp.zeros((), member.dtype))  7.87 us
    select_n x3, other arithmetic, write_token(): return jnp.where(at_token[:, :, None], new_kv[:, None, :], cache_rows)  7.26 us
    all_to_all x1, starting transfers between devices, migrate(): lax.all_to_all(spread_slot(int_row, slot_mask), 'rep', split_axis=0, conc...  5.95 us
    reduce_sum x4, other arithmetic, fold_sum(): jnp.sum(member.astype(jnp.float32), axis=0, keepdims=True)  5.81 us
  transfers between devices with their start and end apart: 6, of which 6 were waited for; matrix products, arithmetic and copies ran while one was open for 18% of the time, Pallas kernels for 0%

commit v1 on v0

v1 whole, which is shorter than its diff:
```python
import math

import jax
import jax.numpy as jnp
from jax import lax
from jax.experimental import pallas as pl
from jax.experimental.pallas import tpu as pltpu
from jax.sharding import PartitionSpec as P

QH = 24
KVH = 8
HD = 64
FF = 256
PAGE = 128
MAXP = 4
GROUP = QH // KVH
SPAN = MAXP * PAGE
LANES = 128
EXTRA = 8
VMEM_BYTES = 32 * 1024 * 1024

SMEM = pl.BlockSpec(memory_space=pltpu.SMEM)
VMEM = pl.BlockSpec(memory_space=pltpu.VMEM)
ANY = pl.BlockSpec(memory_space=pl.ANY)


def row_of(values, index):
    at_row = lax.broadcasted_iota(jnp.int32, values.shape, 0) == index
    return jnp.sum(jnp.where(at_row, values, 0.0), axis=0, keepdims=True)


def put_row(ref, lead, row, fresh):
    start = pl.multiple_of(row // 16 * 16, 16)
    block = ref[lead, pl.ds(start, 16), :].astype(jnp.float32)
    at_row = lax.broadcasted_iota(jnp.int32, block.shape, 0) == row - start
    ref[lead, pl.ds(start, 16), :] = jnp.where(at_row, fresh, block).astype(ref.dtype)


def pack_kernel(leave_ref, target_ref, table_ref, lens_ref, qkv_ref, pool_ref, send_ref, pages, sems):
    leave = leave_ref[0]
    copies = [
        pltpu.make_async_copy(pool_ref.at[table_ref[leave, p]], pages.at[p], sems.at[p])
        for p in range(MAXP)
    ]
    for copy in copies:
        copy.start()
    pieces, _, _ = send_ref.shape
    cols = pages.shape[2]
    rows = SPAN // pieces
    body = cols // LANES * rows
    ticket = jnp.full((pieces, EXTRA, LANES), target_ref[0].astype(jnp.float32), jnp.float32)
    send_ref[:, body:, :] = ticket.astype(send_ref.dtype)
    qkv = row_of(qkv_ref[...].astype(jnp.float32), leave)
    width = (GROUP + 2) * HD
    fresh = jnp.concatenate(
        [qkv[:, h * width + GROUP * HD : (h + 1) * width] for h in range(cols // LANES)], axis=1
    )
    for copy in copies:
        copy.wait()
    length = lens_ref[leave]
    put_row(pages, length // PAGE, length % PAGE, fresh)
    for j in range(pieces):
        page, start = j * rows // PAGE, j * rows % PAGE
        for c in range(cols // LANES):
            send_ref[j, c * rows : (c + 1) * rows, :] = pages[
                page, start : start + rows, c * LANES : (c + 1) * LANES
            ]


def pack(leave_slot, target_rep, page_table, req_lengths, qkv_new, kv_pool, pieces):
    cols = kv_pool.shape[2]
    slot_rows = SPAN // pieces * (cols // LANES) + EXTRA
    return pl.pallas_call(
        pack_kernel,
        out_shape=jax.ShapeDtypeStruct((pieces, slot_rows, LANES), kv_pool.dtype),
        in_specs=[SMEM, SMEM, SMEM, SMEM, VMEM, ANY],
        out_specs=VMEM,
        scratch_shapes=[
            pltpu.VMEM((MAXP, PAGE, cols), kv_pool.dtype),
            pltpu.SemaphoreType.DMA((MAXP,)),
        ],
        compiler_params=pltpu.CompilerParams(vmem_limit_bytes=VMEM_BYTES),
        name="pack",
    )(leave_slot, target_rep, page_table, req_lengths, qkv_new, kv_pool)


def attend_kernel(
    table_ref, lens_ref, query_ref, fresh_ref, pool_ref, proj_ref, head_ref, new_ref,
    cache, proj, rows, page_sems, proj_sem, new_sems,
):
    num_req, heads, cols = query_ref.shape
    used = cols // LANES * GROUP
    reads = [
        [
            pltpu.make_async_copy(
                pool_ref.at[table_ref[r, p]], cache.at[r, pl.ds(p * PAGE, PAGE)], page_sems.at[r, p]
            )
            for p in range(MAXP)
        ]
        for r in range(num_req)
    ]
    for request in reads:
        for copy in request:
            copy.start()
    proj_read = pltpu.make_async_copy(proj_ref, proj, proj_sem)
    proj_read.start()
    fresh = fresh_ref[...].astype(jnp.float32)
    writes = []
    for r in range(num_req):
        for copy in reads[r]:
            copy.wait()
        length = lens_ref[r]
        put_row(cache, r, length, fresh[r : r + 1, :])
        start = pl.multiple_of(length // PAGE * PAGE, PAGE)
        write = pltpu.make_async_copy(cache.at[r, pl.ds(start, PAGE)], new_ref.at[r], new_sems.at[r])
        write.start()
        writes.append(write)
        held = cache[r]
        scores = lax.dot_general(
            query_ref[r], held, (((1,), (1,)), ((), ())), preferred_element_type=jnp.float32
        ) * (1.0 / math.sqrt(HD))
        positions = lax.broadcasted_iota(jnp.int32, scores.shape, 1)
        scores = jnp.where(positions <= length, scores, -jnp.inf)
        weights = jnp.exp(scores - jnp.max(scores, axis=1, keepdims=True))
        probs = (weights / jnp.sum(weights, axis=1, keepdims=True)).astype(held.dtype)
        rows[r] = jnp.dot(probs, held, preferred_element_type=jnp.float32)
    attn = jnp.concatenate(
        [
            jnp.concatenate(
                [
                    rows[r, i : i + 1, i // GROUP * LANES + HD : (i // GROUP + 1) * LANES]
                    for i in range(used)
                ],
                axis=1,
            )
            for r in range(num_req)
        ],
        axis=0,
    ).astype(proj.dtype)
    proj_read.wait()
    head_ref[...] = jnp.dot(attn, proj[...], preferred_element_type=jnp.float32)
    for write in writes:
        write.wait()


def attend(page_table, req_lengths, qkv_new, kv_pool, out_proj):
    num_req = qkv_new.shape[0]
    cols = kv_pool.shape[2]
    head_local = cols // LANES
    split = qkv_new.reshape(num_req, head_local, GROUP + 2, HD)
    fresh = split[:, :, GROUP:, :].reshape(num_req, cols)
    own_head = jnp.arange(head_local)[:, None] == jnp.arange(head_local)[None, :]
    queries = jnp.where(
        own_head[None, :, None, :, None], split[:, :, :GROUP, None, :], jnp.zeros((), qkv_new.dtype)
    )
    queries = jnp.pad(queries, ((0, 0), (0, 0), (0, 0), (0, 0), (0, HD)))
    queries = queries.reshape(num_req, head_local * GROUP, cols)
    heads = -(-head_local * GROUP // 16) * 16
    queries = jnp.pad(queries, ((0, 0), (0, heads - head_local * GROUP), (0, 0)))
    width = out_proj.shape[1]
    return pl.pallas_call(
        attend_kernel,
        out_shape=(
            jax.ShapeDtypeStruct((num_req, width), jnp.float32),
            jax.ShapeDtypeStruct((num_req, PAGE, cols), kv_pool.dtype),
        ),
        in_specs=[SMEM, SMEM, VMEM, VMEM, ANY, ANY],
        out_specs=(VMEM, ANY),
        scratch_shapes=[
            pltpu.VMEM((num_req, SPAN, cols), kv_pool.dtype),
            pltpu.VMEM(out_proj.shape, out_proj.dtype),
            pltpu.VMEM((num_req, heads, cols), jnp.float32),
            pltpu.SemaphoreType.DMA((num_req, MAXP)),
            pltpu.SemaphoreType.DMA,
            pltpu.SemaphoreType.DMA((num_req,)),
        ],
        compiler_params=pltpu.CompilerParams(vmem_limit_bytes=VMEM_BYTES),
        cost_estimate=pl.CostEstimate(
            flops=2 * num_req * (2 * heads * SPAN * cols + out_proj.size),
            bytes_accessed=2 * (num_req * SPAN * cols + out_proj.size),
            transcendentals=num_req * heads * SPAN,
        ),
        name="attend",
    )(page_table, req_lengths, queries, fresh, kv_pool, out_proj)


def experts_kernel(parts_ref, resid_ref, route_ref, gain_ref, in_ref, down_ref, stream_ref, total_ref):
    head = parts_ref[0]
    for k in range(1, parts_ref.shape[0]):
        head = head + parts_ref[k]
    stream = resid_ref[...].astype(jnp.float32) + head
    stream_ref[...] = stream
    mean_sq = jnp.mean(stream * stream, axis=1, keepdims=True)
    normed = (stream * lax.rsqrt(mean_sq + 1e-05) * gain_ref[...]).astype(in_ref.dtype)
    both = jnp.dot(normed, in_ref[0], preferred_element_type=jnp.float32)
    gate = both[:, :FF]
    acted = (gate / (1.0 + jnp.exp(-gate)) * both[:, FF:]).astype(down_ref.dtype)
    total_ref[...] = route_ref[...] * jnp.dot(
        acted, down_ref[0], preferred_element_type=jnp.float32
    )


def experts(parts, resid, route, norm_gain, expert_in, expert_down):
    shape = jax.ShapeDtypeStruct(resid.shape, jnp.float32)
    return pl.pallas_call(
        experts_kernel,
        out_shape=(shape, shape),
        in_specs=[VMEM] * 6,
        out_specs=(VMEM, VMEM),
        compiler_params=pltpu.CompilerParams(vmem_limit_bytes=VMEM_BYTES),
        cost_estimate=pl.CostEstimate(
            flops=2 * resid.shape[0] * (expert_in.size + expert_down.size),
            bytes_accessed=2 * (expert_in.size + expert_down.size),
            transcendentals=resid.shape[0] * FF,
        ),
        name="experts",
    )(parts, resid, route, norm_gain[None, :], expert_in, expert_down)


def forward_kernel(target_ref, landed_ref, extra_ref, send_ref):
    pieces, slot_rows, _ = landed_ref.shape
    body = slot_rows - EXTRA
    send_ref[:, body:, :] = jnp.zeros((pieces, EXTRA, LANES), send_ref.dtype)
    for s in range(pieces):
        ticket = landed_ref[s, body:, :].astype(jnp.float32)
        target = jnp.max(ticket).astype(jnp.int32)
        send_ref[target, :body, :] = landed_ref[s, :body, :]
    send_ref[target_ref[0], body:, :] = extra_ref[...]


def forward(target_rep, landed, extra):
    return pl.pallas_call(
        forward_kernel,
        out_shape=jax.ShapeDtypeStruct(landed.shape, landed.dtype),
        in_specs=[SMEM, VMEM, VMEM],
        out_specs=VMEM,
        compiler_params=pltpu.CompilerParams(vmem_limit_bytes=VMEM_BYTES),
        name="forward",
    )(target_rep, landed, extra)


def settle_kernel(leave_ref, landed_ref, hidden_ref, new_in_ref, hidden_out_ref, new_ref, arrived_ref, sem):
    del new_in_ref
    pieces, slot_rows, _ = landed_ref.shape
    body = slot_rows - EXTRA
    cols = arrived_ref.shape[2]
    rows = SPAN // pieces
    leave = leave_ref[0]
    for j in range(pieces):
        page, start = j * rows // PAGE, j * rows % PAGE
        for c in range(cols // LANES):
            arrived_ref[page, start : start + rows, c * LANES : (c + 1) * LANES] = landed_ref[
                j, c * rows : (c + 1) * rows, :
            ]
    extra = jnp.sum(landed_ref[:, body:, :].astype(jnp.float32), axis=0)
    page = jnp.max(extra[EXTRA - 1 :, :]).astype(jnp.int32)
    write = pltpu.make_async_copy(arrived_ref.at[page], new_ref.at[leave], sem)
    write.start()
    width = hidden_ref.shape[1]
    row = jnp.concatenate([extra[k : k + 1, :] for k in range(-(-width // LANES))], axis=1)
    hidden = hidden_ref[...].astype(jnp.float32)
    at_row = lax.broadcasted_iota(jnp.int32, hidden.shape, 0) == leave
    hidden_out_ref[...] = jnp.where(at_row, row[:, :width], hidden).astype(hidden_out_ref.dtype)
    write.wait()


def settle(leave_slot, landed, hidden, new_pages):
    arrived = jax.ShapeDtypeStruct((MAXP,) + new_pages.shape[1:], new_pages.dtype)
    return pl.pallas_call(
        settle_kernel,
        out_shape=(
            jax.ShapeDtypeStruct(hidden.shape, hidden.dtype),
            jax.ShapeDtypeStruct(new_pages.shape, new_pages.dtype),
            arrived,
        ),
        in_specs=[SMEM, VMEM, VMEM, ANY],
        out_specs=(VMEM, ANY, VMEM),
        scratch_shapes=[pltpu.SemaphoreType.DMA],
        input_output_aliases={3: 1},
        compiler_params=pltpu.CompilerParams(vmem_limit_bytes=VMEM_BYTES),
        name="settle",
    )(leave_slot, landed, hidden, new_pages)


def local(
    kv_pool,
    page_table,
    req_lengths,
    leave_slot,
    target_rep,
    qkv_new,
    residual_in,
    expert_ids,
    gate_weights,
    norm_gain,
    out_proj,
    expert_in,
    expert_down,
):
    pieces = lax.axis_size("rep")
    tp_size = lax.axis_size("tp")
    tp_index = lax.axis_index("tp")
    assert pieces <= 256
    send = pack(leave_slot, target_rep, page_table, req_lengths, qkv_new, kv_pool, pieces)
    landed = lax.all_to_all(send, "rep", split_axis=0, concat_axis=0, tiled=True)

    head_part, new_pages = attend(page_table, req_lengths, qkv_new, kv_pool, out_proj)
    shifts = [[(i, (i + k) % tp_size) for i in range(tp_size)] for k in range(1, tp_size)]
    parts = jnp.stack([head_part] + [lax.ppermute(head_part, "tp", shift) for shift in shifts])
    assert expert_in.shape[0] == 1
    route = jnp.sum(
        jnp.where(expert_ids == tp_index, gate_weights.astype(jnp.float32), 0.0),
        axis=1,
        keepdims=True,
    )
    stream, total = experts(parts, residual_in, route, norm_gain, expert_in, expert_down)
    width = stream.shape[1] // tp_size

    def share(values, index):
        return lax.dynamic_slice_in_dim(values, index * width, width, 1)

    mix = share(total, tp_index)
    for k, shift in enumerate(shifts, 1):
        mix = mix + lax.ppermute(share(total, (tp_index + k) % tp_size), "tp", shift)
    hidden = (share(stream, tp_index) + mix).astype(jnp.bfloat16)
    row = lax.dynamic_slice_in_dim(hidden, leave_slot[0], 1, 0)[0]
    page_number = req_lengths[leave_slot[0]] // PAGE
    row = jnp.pad(row, (0, (EXTRA - 1) * LANES - width)).reshape(EXTRA - 1, LANES)
    note = jnp.full((1, LANES), page_number.astype(hidden.dtype))
    extra = jnp.concatenate([row, note], axis=0)

    landed = lax.all_to_all(
        forward(target_rep, landed, extra), "rep", split_axis=0, concat_axis=0, tiled=True
    )
    return settle(leave_slot, landed, hidden, new_pages)


def solution(mesh):
    return jax.shard_map(
        local,
        mesh=mesh,
        in_specs=(
            P("rep", None, "tp"),
            P("rep", None),
            P("rep"),
            P("rep"),
            P("rep"),
            P("rep", "tp"),
            P("rep", None),
            P("rep", None),
            P("rep", None),
            P(),
            P("tp", None),
            P("tp", None, None),
            P("tp", None, None),
        ),
        out_specs=(P("rep", "tp"), P("rep", None, "tp"), P("rep", None, "tp")),
        check_vma=False,
    )
```

time: 288 us -> 63.6 us (0.22)
  waiting for transfers between devices: 164 us -> 11.7 us
  local copies, waits for them, and re-layouts: 43.8 us -> 6.48 us
  other arithmetic: 27.2 us -> 0.14 us
  starting transfers between devices: 26.5 us -> 8.47 us
  blocking collectives: 3.42 us -> 20.1 us
  Pallas kernels: 0 us -> 11.2 us
  between operations: 15.8 us -> 5 us
  matrix products: 5.44 us -> 0 us
    all_to_all x5 -> x1, waiting for transfers between devices: 134 us -> 11.7 us  [local(): lax.all_to_all(send, 'rep', split_axis=0, concat_axis=0, tiled=True)]
    unnamed x2 -> x0, waiting for transfers between devices: 30.7 us -> none
    all_to_all x0 -> x1, blocking collectives: none -> 20.1 us  [local(): lax.all_to_all(forward(target_rep, landed, extra), 'rep', split_axis=0, c...]
    reshape x4 -> x5, local copies, waits for them, and re-layouts: 19.7 us -> 0.93 us  [the longest x1 0.8 us: attend(): split = qkv_new.reshape(num_req, head_local, GROUP + 2, HD)]
    all_to_all x5 -> x1, starting transfers between devices: 26.4 us -> 7.84 us  [local(): lax.all_to_all(send, 'rep', split_axis=0, concat_axis=0, tiled=True)]
    select_n x14 -> x2, other arithmetic: 16.8 us -> 0.1 us  [the longest x1 0.09 us: attend(): jnp.where(own_head[None, :, None, :, None], split[:, :, :GROUP, None, :],...]
    gather x8 -> x0, local copies, waits for them, and re-layouts: 13.1 us -> none  [the longest x1 3.6 us: local(): own_cache = kv_pool[page_table].reshape(num_req, MAXP * PAGE, -1)]
    pallas_call x0 -> x5, Pallas kernels: none -> 11.2 us  [the longest x1 6.49 us: attend(): pl.pallas_call(attend_kernel, out_shape=(jax.ShapeDtypeStruct((num_req, w...]
  transfers between devices with their start and end apart: 6 -> 3, of which waited for: 6 -> 1; matrix products, arithmetic and copies ran while one was open for 18% -> 1% of each run, Pallas kernels for 0% -> 5%
where the time goes in v1:
time: 63.6 us; the launch traced here: 63.1 us
  blocking collectives  20.1 us (32%)
  waiting for transfers between devices  11.7 us (18%)
  Pallas kernels  11.2 us (18%)
  starting transfers between devices  8.47 us (13%)
  local copies, waits for them, and re-layouts  6.48 us (10%)
  between operations  5 us (8%)
    all_to_all x1, blocking collectives, local(): lax.all_to_all(forward(target_rep, landed, extra), 'rep', split_axis=0, c...  20.1 us
    all_to_all x1, waiting for transfers between devices, local(): lax.all_to_all(send, 'rep', split_axis=0, concat_axis=0, tiled=True)  11.7 us
    all_to_all x1, starting transfers between devices, local(): lax.all_to_all(send, 'rep', split_axis=0, concat_axis=0, tiled=True)  7.84 us
    pallas_call x1, Pallas kernels, attend(): pl.pallas_call(attend_kernel, out_shape=(jax.ShapeDtypeStruct((num_req, w...  6.49 us
    unnamed x27, local copies, waits for them, and re-layouts  4.74 us
    pallas_call x1, Pallas kernels, pack(): pl.pallas_call(pack_kernel, out_shape=jax.ShapeDtypeStruct((pieces, slot_...  2.28 us
    pallas_call x1, Pallas kernels, settle(): pl.pallas_call(settle_kernel, out_shape=(jax.ShapeDtypeStruct(hidden.shap...  1.68 us
  transfers between devices with their start and end apart: 3, of which 1 were waited for; matrix products, arithmetic and copies ran while one was open for 1% of the time, Pallas kernels for 5%

profile of v1, /device:TPU:0, one launch (start us, length us, event | category | flops | bytes accessed | tf_op | source)
XLA Modules:
  0.0 63.1 jit_solution(2101615843646284923)
XLA Ops:
  0.6 0.8 %reshape.34 = bf16[4,4,5,64]{3,2,1,0:T(8,128)(2,1)S(1)} reshape(bf16[4,1280]{1,0:T(4,128)(2,1)} %qkv_ref.1) | data formatting | bytes 20480 | tf_op jit(solution)/shard_map/reshape | solution.py:150
  1.5 0.1 reshape.36.fresh_ref
  1.6 0.1 broadcast_select_fusion
  1.8 0.0 copy-start
  1.8 1.6 %copy-done = bf16[16,128,512]{2,1,0:T(8,128)(2,1)S(1)} copy-done((bf16[16,128,512]{2,1,0:T(8,128)(2,1)S(1)}, bf16[16,128,512]{2,1,0:T(8,128)(2,1)}, u32[]{:S(2)}) %copy-start) | copy-done | bytes 2097176
  3.4 0.0 copy-start.2
  3.4 1.7 %copy-done.2 = bf16[768,1536]{1,0:T(8,128)(2,1)S(1)} copy-done((bf16[768,1536]{1,0:T(8,128)(2,1)S(1)}, bf16[768,1536]{1,0:T(8,128)(2,1)}, u32[]{:S(2)}) %copy-start.2) | copy-done | bytes 2359320
  5.0 0.0 copy-start.7
  5.0 0.7 %copy-done.7 = s32[4,4]{1,0:T(4,128)S(1)} copy-done((s32[4,4]{1,0:T(4,128)S(1)}, s32[4,4]{1,0:T(4,128)}, u32[]{:S(2)}) %copy-start.7) | copy-done | bytes 88
  5.7 0.0 copy-start.8
  5.7 0.7 %copy-done.8 = s32[4]{0:T(128)S(1)} copy-done((s32[4]{0:T(128)S(1)}, s32[4]{0:T(128)}, u32[]{:S(2)}) %copy-start.8) | copy-done | bytes 40
  6.4 0.0 copy-start.1
  6.4 0.0 copy-start.5
  6.4 6.5 %attend.1 = (f32[4,1536]{1,0:T(4,128)S(1)}, bf16[4,128,512]{2,1,0:T(8,128)(2,1)}) custom-call(s32[4,4]{1,0:T(4,128)S(1)} %copy-done.7, s32[4]{0:T(128)S(1)} %copy-done.8, bf16[4,16,512]{2,1,0:T(8,128)(2,1)S(1)} %pad.14.query_ref, bf16[4,512]{1,0:T(4,128)(2,1)S(1)} %reshape.36.fresh_ref, bf16[16,128,512]{2,1,0:T(8,128)(2,1)S(1)} %copy-done, ...), custom_call_target="tpu_custom_call" | custom-call | flops 76546048 | bytes 4456448 | tf_op jit(solution)/shard_map/attend/pallas_call | solution.py:161
  12.9 0.0 copy-start.11
  12.9 0.0 copy-start.12
  12.9 0.0 copy-start.10
  12.9 0.0 copy-start.3
  12.9 0.0 copy-start.4
  12.9 0.0 copy-start.6
  13.0 0.5 collective-permute-start
  15.0 0.0 copy-done.1
  15.0 0.0 copy-done.5
  15.0 2.3 %pack.1 = bf16[16,136,128]{2,1,0:T(8,128)(2,1)} custom-call(s32[1]{0:T(128)} %copy.28.leave_ref, s32[1]{0:T(128)S(6)} %copy.29.target_ref, s32[4,4]{1,0:T(4,128)S(1)} %copy-done.7, s32[4]{0:T(128)S(1)} %copy-done.8, bf16[4,1280]{1,0:T(4,128)(2,1)S(1)} %copy-done.5, bf16[16,128,512]{2,1,0:T(8,128)(2,1)S(1)} %copy-done.1), custom_call_target="tpu_custom_call" | custom-call | tf_op jit(solution)/shard_map/pack/pallas_call | solution.py:73
  17.3 0.0 copy-start.9
  17.3 7.8 %all-to-all-start = ((bf16[16,136,128]{2,1,0:T(8,128)(2,1)}), bf16[16,136,128]{2,1,0:T(8,128)(2,1)S(1)}, u32[]{:S(2)}, u32[]{:S(2)}) async-start(bf16[16,136,128]{2,1,0:T(8,128)(2,1)} %pack.1), calls=%async_computation | async-start | bytes 1114112 | tf_op jit(solution)/shard_map/all_to_all | solution.py:305
  25.1 0.0 copy-done.11
  25.2 0.1 copy.24
  25.3 0.0 copy-done.12
  25.3 0.1 copy.23
  25.4 0.0 copy-done.10
  25.4 0.0 collective-permute-done
  25.4 0.0 copy-done.3
  25.4 0.0 copy-done.4
  25.5 0.0 copy-done.6
  25.5 0.6 experts.1
  26.1 0.1 collective-permute-start.1
  26.2 0.0 copy-done.9
  26.2 0.6 dynamic_slice.19
  29.4 0.0 collective-permute-done.1
  29.5 11.7 %all-to-all-done.landed_ref = bf16[16,136,128]{2,1,0:T(8,128)(2,1)S(1)} async-done(((bf16[16,136,128]{2,1,0:T(8,128)(2,1)}), bf16[16,136,128]{2,1,0:T(8,128)(2,1)S(1)}, u32[]{:S(2)}, u32[]{:S(2)}) %all-to-all-start) | async-done | bytes 557088 | tf_op jit(solution)/shard_map/all_to_all | solution.py:305
  41.2 0.2 forward.1
  41.3 20.1 %all_to_all.10.landed_ref = bf16[16,136,128]{2,1,0:T(8,128)(2,1)S(1)} all-to-all(bf16[16,136,128]{2,1,0:T(8,128)(2,1)S(1)} %forward.1), channel_id=1, replica_groups=mesh['rep'=16,'tp'=2] {'rep'}, dimensions={0} | all-to-all | bytes 1114112 | tf_op jit(solution)/shard_map/all_to_all | solution.py:332
  61.4 1.7 %settle.1 = (bf16[4,768]{1,0:T(4,128)(2,1)}, bf16[4,128,512]{2,1,0:T(8,128)(2,1)}, bf16[4,128,512]{2,1,0:T(8,128)(2,1)}) custom-call(s32[1]{0:T(128)} %copy.28.leave_ref, bf16[16,136,128]{2,1,0:T(8,128)(2,1)S(1)} %all_to_all.10.landed_ref, bf16[4,768]{1,0:T(4,128)(2,1)S(1)} %add_convert_fusion.hidden_ref, ...), custom_call_target="tpu_custom_call", output_to_operand_aliasing={{1}: (3, {})} | custom-call | tf_op jit(solution)/shard_map/settle/pallas_call | solution.py:269
  (17 shorter events, 0.2 us)
Async XLA Ops:
  1.8 1.6 %copy-start = (bf16[16,128,512]{2,1,0:T(8,128)(2,1)S(1)}, bf16[16,128,512]{2,1,0:T(8,128)(2,1)}, u32[]{:S(2)}) copy-start(bf16[16,128,512]{2,1,0:T(8,128)(2,1)} %pool_ref.3) | copy-start | bytes 6291460
  3.4 1.7 %copy-start.2 = (bf16[768,1536]{1,0:T(8,128)(2,1)S(1)}, bf16[768,1536]{1,0:T(8,128)(2,1)}, u32[]{:S(2)}) copy-start(bf16[768,1536]{1,0:T(8,128)(2,1)} %proj_ref.1) | copy-start | bytes 7077892
  5.0 0.7 %copy-start.7 = (s32[4,4]{1,0:T(4,128)S(1)}, s32[4,4]{1,0:T(4,128)}, u32[]{:S(2)}) copy-start(s32[4,4]{1,0:T(4,128)} %table_ref.3) | copy-start | bytes 196
  5.7 0.7 %copy-start.8 = (s32[4]{0:T(128)S(1)}, s32[4]{0:T(128)}, u32[]{:S(2)}) copy-start(s32[4]{0:T(128)} %lens_ref.3) | copy-start | bytes 52
  6.4 8.6 %copy-start.1 = (bf16[16,128,512]{2,1,0:T(8,128)(2,1)S(1)}, bf16[16,128,512]{2,1,0:T(8,128)(2,1)}, u32[]{:S(2)}) copy-start(bf16[16,128,512]{2,1,0:T(8,128)(2,1)} %pool_ref.3) | copy-start | bytes 6291460
  6.4 8.6 %copy-start.5 = (bf16[4,1280]{1,0:T(4,128)(2,1)S(1)}, bf16[4,1280]{1,0:T(4,128)(2,1)}, u32[]{:S(2)}) copy-start(bf16[4,1280]{1,0:T(4,128)(2,1)} %qkv_ref.1) | copy-start | bytes 30724
  12.9 12.3 %copy-start.11 = (s32[4,1]{0,1:T(1,128)S(1)}, s32[4,1]{0,1:T(1,128)}, u32[]{:S(2)}) copy-start(s32[4,1]{0,1:T(1,128)} %param.20) | copy-start | bytes 52
  12.9 12.4 %copy-start.12 = (bf16[4,1]{0,1:T(2,128)(2,1)S(1)}, bf16[4,1]{0,1:T(2,128)(2,1)}, u32[]{:S(2)}) copy-start(bf16[4,1]{0,1:T(2,128)(2,1)} %param.21) | copy-start | bytes 28
  12.9 12.5 %copy-start.10 = (f32[1536]{0:T(1024)S(1)}, f32[1536]{0:T(1024)}, u32[]{:S(2)}) copy-start(f32[1536]{0:T(1024)} %param.22) | copy-start | bytes 18436
  12.9 12.5 %copy-start.3 = (bf16[1,1536,512]{2,1,0:T(8,128)(2,1)S(1)}, bf16[1,1536,512]{2,1,0:T(8,128)(2,1)}, u32[]{:S(2)}) copy-start(bf16[1,1536,512]{2,1,0:T(8,128)(2,1)} %in_ref.1) | copy-start | bytes 4718596
  12.9 12.5 %copy-start.4 = (bf16[1,256,1536]{2,1,0:T(8,128)(2,1)S(1)}, bf16[1,256,1536]{2,1,0:T(8,128)(2,1)}, u32[]{:S(2)}) copy-start(bf16[1,256,1536]{2,1,0:T(8,128)(2,1)} %down_ref.1) | copy-start | bytes 2359300
  12.9 12.5 %copy-start.6 = (bf16[4,1536]{1,0:T(4,128)(2,1)S(1)}, bf16[4,1536]{1,0:T(4,128)(2,1)}, u32[]{:S(2)}) copy-start(bf16[4,1536]{1,0:T(4,128)(2,1)} %resid_ref.1) | copy-start | bytes 36868
  13.0 12.4 %collective-permute-start = (f32[4,1536]{1,0:T(4,128)S(1)}, f32[4,1536]{1,0:T(4,128)S(1)}, u32[]{:S(2)}, u32[]{:S(2)}) collective-permute-start(f32[4,1536]{1,0:T(4,128)S(1)} %get-tuple-element.7), channel_id=1, source_target_pairs={{0,1},{1,0},{2,3},{3,2},{4,5},{5,4},{6,7},{7,6},{8,9},{9,8},{10,11... | collective-permute-start | bytes 73736 | tf_op jit(solution)/shard_map/ppermute | solution.py:309
  17.3 8.9 %copy-start.9 = (s32[4]{0:T(128)S(1)}, s32[4]{0:T(128)}, u32[]{:S(2)}) copy-start(s32[4]{0:T(128)} %lens_ref.3) | copy-start | bytes 52
  17.3 23.9 %all-to-all-start = ((bf16[16,136,128]{2,1,0:T(8,128)(2,1)}), bf16[16,136,128]{2,1,0:T(8,128)(2,1)S(1)}, u32[]{:S(2)}, u32[]{:S(2)}) async-start(bf16[16,136,128]{2,1,0:T(8,128)(2,1)} %pack.1), calls=%async_computation | async-start | bytes 1114112 | tf_op jit(solution)/shard_map/all_to_all | solution.py:305
  26.1 3.3 %collective-permute-start.1 = (f32[4,768]{1,0:T(4,128)S(1)}, f32[4,768]{1,0:T(4,128)S(1)}, u32[]{:S(2)}, u32[]{:S(2)}) collective-permute-start(f32[4,768]{1,0:T(4,128)S(1)} %constant_dynamic-slice_fusion), channel_id=1, source_target_pairs={{0,1},{1,0},{2,3},{3,2},{4,5},{5,4},{6,7},{7,6},{8,9},{9,8},{10,11... | collective-permute-start | bytes 36872 | tf_op jit(solution)/shard_map/ppermute | solution.py:324

commit v2 on v1

v2 whole, which is shorter than its diff:
```python
import math

import jax
import jax.numpy as jnp
from jax import lax
from jax.experimental import pallas as pl
from jax.experimental.pallas import tpu as pltpu
from jax.sharding import PartitionSpec as P

QH = 24
KVH = 8
HD = 64
FF = 256
PAGE = 128
MAXP = 4
GROUP = QH // KVH
SPAN = MAXP * PAGE
LANES = 128
EXTRA = 8
VMEM_BYTES = 16 * 1024 * 1024

SMEM = pl.BlockSpec(memory_space=pltpu.SMEM)
VMEM = pl.BlockSpec(memory_space=pltpu.VMEM)
HBM = pl.BlockSpec(memory_space=pltpu.HBM)


def in_hbm(array):
    return pltpu.with_memory_space_constraint(array, pltpu.HBM)


def params():
    return pltpu.CompilerParams(vmem_limit_bytes=VMEM_BYTES)


def fresh_of(qkv, cols):
    width = (GROUP + 2) * HD
    return jnp.concatenate(
        [qkv[:, h * width + GROUP * HD : (h + 1) * width] for h in range(cols // LANES)], axis=1
    )


def blocks_of(pieces, cols):
    rows = SPAN // pieces
    return rows, [
        (j, c * rows, j * rows // PAGE, j * rows % PAGE, c * LANES)
        for j in range(pieces)
        for c in range(cols // LANES)
    ]


def put_row(ref, lead, row, fresh):
    start = pl.multiple_of(row // 16 * 16, 16)
    block = ref[lead, pl.ds(start, 16), :].astype(jnp.float32)
    at_row = lax.broadcasted_iota(jnp.int32, block.shape, 0) == row - start
    ref[lead, pl.ds(start, 16), :] = jnp.where(at_row, fresh, block).astype(ref.dtype)


def pack_kernel(
    leave_ref, target_ref, table_hbm, lens_hbm, qkv_hbm, pool_ref, send_ref,
    table_ref, lens_ref, qkv_ref, pages, small_sems, page_sems,
):
    smalls = [
        pltpu.make_async_copy(source, target, small_sems.at[i])
        for i, (source, target) in enumerate(
            [(table_hbm, table_ref), (lens_hbm, lens_ref), (qkv_hbm, qkv_ref)]
        )
    ]
    for copy in smalls:
        copy.start()
    pieces, slot_rows, _ = send_ref.shape
    body = slot_rows - EXTRA
    ticket = jnp.full((pieces, EXTRA, LANES), target_ref[0].astype(jnp.float32), jnp.float32)
    send_ref[:, body:, :] = ticket.astype(send_ref.dtype)
    smalls[0].wait()
    leave = leave_ref[0]
    copies = [
        pltpu.make_async_copy(pool_ref.at[table_ref[leave, p]], pages.at[p], page_sems.at[p])
        for p in range(MAXP)
    ]
    for copy in copies:
        copy.start()
    smalls[1].wait()
    smalls[2].wait()
    qkv = qkv_ref[...].astype(jnp.float32)
    at_row = lax.broadcasted_iota(jnp.int32, qkv.shape, 0) == leave
    qkv = jnp.sum(jnp.where(at_row, qkv, 0.0), axis=0, keepdims=True)
    fresh = fresh_of(qkv, pages.shape[2])
    length = lens_ref[leave]
    for copy in copies:
        copy.wait()
    put_row(pages, length // PAGE, length % PAGE, fresh)
    rows, blocks = blocks_of(pieces, pages.shape[2])
    for piece, at, page, start, column in blocks:
        send_ref[piece, at : at + rows, :] = pages[page, start : start + rows, column : column + LANES]


def pack(leave_slot, target_rep, page_table, req_lengths, qkv_new, kv_pool, pieces):
    cols = kv_pool.shape[2]
    slot_rows = SPAN // pieces * (cols // LANES) + EXTRA
    return pl.pallas_call(
        pack_kernel,
        out_shape=pltpu.VMEM((pieces, slot_rows, LANES), kv_pool.dtype),
        in_specs=[SMEM, SMEM] + [HBM] * 4,
        out_specs=VMEM,
        scratch_shapes=[
            pltpu.SMEM(page_table.shape, page_table.dtype),
            pltpu.SMEM(req_lengths.shape, req_lengths.dtype),
            pltpu.VMEM(qkv_new.shape, qkv_new.dtype),
            pltpu.VMEM((MAXP, PAGE, cols), kv_pool.dtype),
            pltpu.SemaphoreType.DMA((3,)),
            pltpu.SemaphoreType.DMA((MAXP,)),
        ],
        compiler_params=params(),
        name="pack",
    )(leave_slot, target_rep, *map(in_hbm, (page_table, req_lengths, qkv_new, kv_pool)))


def attend_kernel(table_ref, lens_ref, qkv_ref, pool_ref, proj_ref, head_ref, new_ref, stage, sems):
    num_req = qkv_ref.shape[0]
    cols = pool_ref.shape[2]
    heads = cols // LANES
    rows = -(-heads * GROUP // 16) * 16
    width = (GROUP + 2) * HD
    qkv = qkv_ref[...].astype(jnp.float32)
    fresh = fresh_of(qkv, cols)

    writes = []
    for r in range(num_req):
        length = lens_ref[r]
        stage[r] = pool_ref[table_ref[r, length // PAGE]]
        put_row(stage, r, length % PAGE, fresh[r : r + 1, :])
        write = pltpu.make_async_copy(stage.at[r], new_ref.at[r], sems.at[r])
        write.start()
        writes.append(write)

    queries = []
    for r in range(num_req):
        blocks = []
        for h in range(heads):
            block = jnp.concatenate(
                [qkv[r : r + 1, h * width + g * HD : h * width + (g + 2) * HD] for g in range(GROUP)], axis=0
            )
            lane = lax.broadcasted_iota(jnp.int32, block.shape, 1)
            block = jnp.where(lane < HD, block, 0.0)
            parts = [jnp.zeros_like(block)] * heads
            parts[h] = block
            blocks.append(jnp.concatenate(parts, axis=1))
        if rows > heads * GROUP:
            blocks.append(jnp.zeros((rows - heads * GROUP, cols), jnp.float32))
        queries.append(jnp.concatenate(blocks, axis=0))

    scores, masks = [], []
    for r in range(num_req):
        length = lens_ref[r]
        query = queries[r].astype(pool_ref.dtype)
        score = jnp.concatenate(
            [
                lax.dot_general(
                    query, pool_ref[table_ref[r, p]], (((1,), (1,)), ((), ())),
                    preferred_element_type=jnp.float32,
                )
                for p in range(MAXP)
            ],
            axis=1,
        )
        own = jnp.sum(queries[r] * fresh[r : r + 1, :], axis=1, keepdims=True)
        positions = lax.broadcasted_iota(jnp.int32, score.shape, 1)
        score = jnp.where(positions == length, own, score) * (1.0 / math.sqrt(HD))
        scores.append(jnp.where(positions <= length, score, -jnp.inf))
        masks.append(positions == length)
    score = jnp.concatenate(scores, axis=0)
    mask = jnp.concatenate(masks, axis=0)
    weights = jnp.exp(score - jnp.max(score, axis=1, keepdims=True))
    probs = (weights / jnp.sum(weights, axis=1, keepdims=True)).astype(pool_ref.dtype).astype(jnp.float32)
    own = jnp.sum(jnp.where(mask, probs, 0.0), axis=1, keepdims=True)
    probs = jnp.where(mask, 0.0, probs).astype(pool_ref.dtype)

    attn = []
    for r in range(num_req):
        out = own[r * rows : (r + 1) * rows, :] * fresh[r : r + 1, :]
        for p in range(MAXP):
            out = out + jnp.dot(
                probs[r * rows : (r + 1) * rows, p * PAGE : (p + 1) * PAGE], pool_ref[table_ref[r, p]],
                preferred_element_type=jnp.float32,
            )
        attn.append(
            jnp.concatenate(
                [
                    out[i : i + 1, i // GROUP * LANES + HD : (i // GROUP + 1) * LANES]
                    for i in range(heads * GROUP)
                ],
                axis=1,
            )
        )
    attn = jnp.concatenate(attn, axis=0).astype(proj_ref.dtype)
    head_ref[...] = jnp.dot(attn, proj_ref[...], preferred_element_type=jnp.float32)
    for write in writes:
        write.wait()


def attend(page_table, req_lengths, qkv_new, kv_pool, out_proj):
    num_req = qkv_new.shape[0]
    cols = kv_pool.shape[2]
    return pl.pallas_call(
        attend_kernel,
        out_shape=(
            jax.ShapeDtypeStruct((num_req, out_proj.shape[1]), jnp.float32),
            jax.ShapeDtypeStruct((num_req, PAGE, cols), kv_pool.dtype),
        ),
        in_specs=[SMEM, SMEM, VMEM, VMEM, VMEM],
        out_specs=(VMEM, HBM),
        scratch_shapes=[
            pltpu.VMEM((num_req, PAGE, cols), kv_pool.dtype),
            pltpu.SemaphoreType.DMA((num_req,)),
        ],
        compiler_params=params(),
        cost_estimate=pl.CostEstimate(
            flops=2 * num_req * (2 * 16 * SPAN * cols + out_proj.size),
            bytes_accessed=2 * (num_req * SPAN * cols + out_proj.size),
            transcendentals=num_req * 16 * SPAN,
        ),
        name="attend",
    )(page_table, req_lengths, qkv_new, kv_pool, out_proj)


def experts_kernel(
    index_ref, ids_ref, gates_ref, resid_ref, gain_ref, in_ref, down_ref, *parts_refs
):
    *parts_refs, stream_ref, total_ref = parts_refs
    head = parts_refs[0][...]
    for part in parts_refs[1:]:
        head = head + part[...]
    stream = resid_ref[...].astype(jnp.float32) + head
    stream_ref[...] = stream
    mean_sq = jnp.mean(stream * stream, axis=1, keepdims=True)
    normed = (stream * lax.rsqrt(mean_sq + 1e-05) * gain_ref[...]).astype(in_ref.dtype)
    both = jnp.dot(normed, in_ref[0], preferred_element_type=jnp.float32)
    gate = both[:, :FF]
    acted = (gate / (1.0 + jnp.exp(-gate)) * both[:, FF:]).astype(down_ref.dtype)
    chosen = ids_ref[...] == index_ref[0]
    route = jnp.sum(
        jnp.where(chosen, gates_ref[...].astype(jnp.float32), 0.0), axis=1, keepdims=True
    )
    total_ref[...] = route * jnp.dot(acted, down_ref[0], preferred_element_type=jnp.float32)


def experts(tp_index, expert_ids, gate_weights, resid, norm_gain, expert_in, expert_down, parts):
    shape = jax.ShapeDtypeStruct(resid.shape, jnp.float32)
    return pl.pallas_call(
        experts_kernel,
        out_shape=(shape, shape),
        in_specs=[SMEM] + [VMEM] * (6 + len(parts)),
        out_specs=(VMEM, VMEM),
        compiler_params=params(),
        cost_estimate=pl.CostEstimate(
            flops=2 * resid.shape[0] * (expert_in.size + expert_down.size),
            bytes_accessed=2 * (expert_in.size + expert_down.size),
            transcendentals=resid.shape[0] * FF,
        ),
        name="experts",
    )(
        tp_index[None], expert_ids, gate_weights, resid, norm_gain[None, :], expert_in, expert_down, *parts
    )


def forward_kernel(target_ref, landed_ref, extra_ref, send_ref):
    pieces, slot_rows, _ = landed_ref.shape
    body = slot_rows - EXTRA
    send_ref[:, body:, :] = jnp.zeros((pieces, EXTRA, LANES), send_ref.dtype)
    for s in range(pieces):
        target = jnp.max(landed_ref[s, body:, :].astype(jnp.float32)).astype(jnp.int32)
        send_ref[target, :body, :] = landed_ref[s, :body, :]
    send_ref[target_ref[0], body:, :] = extra_ref[...]


def forward(target_rep, landed, extra):
    return pl.pallas_call(
        forward_kernel,
        out_shape=pltpu.VMEM(landed.shape, landed.dtype),
        in_specs=[SMEM, VMEM, VMEM],
        out_specs=VMEM,
        compiler_params=params(),
        name="forward",
    )(target_rep, landed, extra)


def settle_kernel(
    slot_ref, landed_ref, hidden_ref, new_in_ref, hidden_out_ref, new_ref, arrived_ref, pages, sems
):
    del new_in_ref
    pieces, slot_rows, _ = landed_ref.shape
    body = slot_rows - EXTRA
    rows, blocks = blocks_of(pieces, pages.shape[2])
    for piece, at, page, start, column in blocks:
        pages[page, start : start + rows, column : column + LANES] = landed_ref[piece, at : at + rows, :]
    all_pages = pltpu.make_async_copy(pages, arrived_ref, sems.at[0])
    all_pages.start()
    extra = jnp.sum(landed_ref[:, body:, :].astype(jnp.float32), axis=0)
    page = jnp.max(extra[EXTRA - 1 :, :]).astype(jnp.int32)
    leave = jnp.max(slot_ref[...]).astype(jnp.int32)
    new_page = pltpu.make_async_copy(pages.at[page], new_ref.at[leave], sems.at[1])
    new_page.start()
    width = hidden_ref.shape[1]
    row = jnp.concatenate([extra[k : k + 1, :] for k in range(-(-width // LANES))], axis=1)
    hidden = hidden_ref[...].astype(jnp.float32)
    at_row = lax.broadcasted_iota(jnp.int32, hidden.shape, 0) == leave
    hidden_out_ref[...] = jnp.where(at_row, row[:, :width], hidden).astype(hidden_out_ref.dtype)
    all_pages.wait()
    new_page.wait()


def settle(slot, landed, hidden, new_pages):
    arrived = (MAXP,) + new_pages.shape[1:]
    return pl.pallas_call(
        settle_kernel,
        out_shape=(
            jax.ShapeDtypeStruct(hidden.shape, hidden.dtype),
            jax.ShapeDtypeStruct(new_pages.shape, new_pages.dtype),
            jax.ShapeDtypeStruct(arrived, new_pages.dtype),
        ),
        in_specs=[VMEM, VMEM, VMEM, HBM],
        out_specs=(VMEM, HBM, HBM),
        scratch_shapes=[pltpu.VMEM(arrived, new_pages.dtype), pltpu.SemaphoreType.DMA((2,))],
        input_output_aliases={3: 1},
        compiler_params=params(),
        name="settle",
    )(slot, landed, hidden, new_pages)


def local(
    kv_pool,
    page_table,
    req_lengths,
    leave_slot,
    target_rep,
    qkv_new,
    residual_in,
    expert_ids,
    gate_weights,
    norm_gain,
    out_proj,
    expert_in,
    expert_down,
):
    pieces = lax.axis_size("rep")
    tp_size = lax.axis_size("tp")
    tp_index = lax.axis_index("tp")
    assert pieces <= 256

    def exchange(packet):
        return lax.all_to_all(packet, "rep", split_axis=0, concat_axis=0, tiled=True)

    send = pack(leave_slot, target_rep, page_table, req_lengths, qkv_new, kv_pool, pieces)
    send, qkv_new = lax.optimization_barrier((send, qkv_new))
    landed = exchange(send)

    head_part, new_pages = attend(page_table, req_lengths, qkv_new, kv_pool, out_proj)
    shifts = [[(i, (i + k) % tp_size) for i in range(tp_size)] for k in range(1, tp_size)]
    parts = [head_part] + [lax.ppermute(head_part, "tp", shift) for shift in shifts]
    assert expert_in.shape[0] == 1
    stream, total = experts(
        tp_index, expert_ids, gate_weights, residual_in, norm_gain, expert_in, expert_down, parts
    )
    width = stream.shape[1] // tp_size

    def share(values, index):
        return lax.dynamic_slice_in_dim(values, index * width, width, 1)

    mix = share(total, tp_index)
    for k, shift in enumerate(shifts, 1):
        mix = mix + lax.ppermute(share(total, (tp_index + k) % tp_size), "tp", shift)
    hidden = (share(stream, tp_index) + mix).astype(jnp.bfloat16)
    row = lax.dynamic_slice_in_dim(hidden, leave_slot[0], 1, 0)[0]
    row = jnp.pad(row, (0, (EXTRA - 1) * LANES - width)).reshape(EXTRA - 1, LANES)
    page_number = (req_lengths[leave_slot[0]] // PAGE).astype(hidden.dtype)
    extra = jnp.concatenate([row, jnp.full((1, LANES), page_number)], axis=0)
    slot = jnp.full((EXTRA, LANES), leave_slot[0].astype(jnp.float32))

    landed = exchange(forward(target_rep, landed, extra))
    return settle(slot, landed, hidden, new_pages)


def solution(mesh):
    return jax.shard_map(
        local,
        mesh=mesh,
        in_specs=(
            P("rep", None, "tp"),
            P("rep", None),
            P("rep"),
            P("rep"),
            P("rep"),
            P("rep", "tp"),
            P("rep", None),
            P("rep", None),
            P("rep", None),
            P(),
            P("tp", None),
            P("tp", None, None),
            P("tp", None, None),
        ),
        out_specs=(P("rep", "tp"), P("rep", None, "tp"), P("rep", None, "tp")),
        check_vma=False,
    )
```

time: 63.6 us -> 50.9 us (0.80)
  blocking collectives: 20.1 us -> 0 us
  waiting for transfers between devices: 11.7 us -> 20.9 us
  starting transfers between devices: 8.47 us -> 12.6 us
  Pallas kernels: 11.2 us -> 8.06 us
  local copies, waits for them, and re-layouts: 6.48 us -> 3.94 us
    all_to_all x1 -> x0, blocking collectives: 20.1 us -> none  [local(): lax.all_to_all(forward(target_rep, landed, extra), 'rep', split_axis=0, c...]
    all_to_all x1 -> x2, waiting for transfers between devices: 11.7 us -> 19.9 us  [exchange(): lax.all_to_all(packet, 'rep', split_axis=0, concat_axis=0, tiled=True)]
    all_to_all x1 -> x2, starting transfers between devices: 7.84 us -> 12.3 us  [exchange(): lax.all_to_all(packet, 'rep', split_axis=0, concat_axis=0, tiled=True)]
    pallas_call x4, Pallas kernels: 9.52 us -> 6.53 us  [the longest x1 2.76 us: pack(): pl.pallas_call(pack_kernel, out_shape=pltpu.VMEM((pieces, slot_rows, LANE...]
    unnamed x27 -> x24, local copies, waits for them, and re-layouts: 4.74 us -> 3.31 us
    ppermute x1, waiting for transfers between devices: 0.01 us -> 0.94 us  [local(): lax.ppermute(head_part, 'tp', shift)]
    reshape x4 -> x0, local copies, waits for them, and re-layouts: 0.93 us -> none  [the longest x1 0.8 us: attend(): split = qkv_new.reshape(num_req, head_local, GROUP + 2, HD)]
  transfers between devices with their start and end apart: 3 -> 4, of which waited for: 1 -> 3; matrix products, arithmetic and copies ran while one was open for 1% -> 2% of each run, Pallas kernels for 5% -> 6%
where the time goes in v2:
time: 50.9 us; the launch traced here: 50.4 us
  waiting for transfers between devices  20.9 us (41%)
  starting transfers between devices  12.6 us (25%)
  Pallas kernels  8.06 us (16%)
  between operations  4.88 us (10%)
  local copies, waits for them, and re-layouts  3.94 us (8%)
    all_to_all x2, waiting for transfers between devices, exchange(): lax.all_to_all(packet, 'rep', split_axis=0, concat_axis=0, tiled=True)  19.9 us
    all_to_all x2, starting transfers between devices, exchange(): lax.all_to_all(packet, 'rep', split_axis=0, concat_axis=0, tiled=True)  12.3 us
    unnamed x24, local copies, waits for them, and re-layouts  3.31 us
    pallas_call x1, Pallas kernels, pack(): pl.pallas_call(pack_kernel, out_shape=pltpu.VMEM((pieces, slot_rows, LANE...  2.76 us
    pallas_call x1, Pallas kernels, attend(): pl.pallas_call(attend_kernel, out_shape=(jax.ShapeDtypeStruct((num_req, o...  2.22 us
    pallas_call x1, Pallas kernels, settle(): pl.pallas_call(settle_kernel, out_shape=(jax.ShapeDtypeStruct(hidden.shap...  1.53 us
  transfers between devices with their start and end apart: 4, of which 3 were waited for; matrix products, arithmetic and copies ran while one was open for 2% of the time, Pallas kernels for 6%

profile of v2, /device:TPU:0, one launch (start us, length us, event | category | flops | bytes accessed | tf_op | source)
XLA Modules:
  0.0 50.4 jit_solution(1488079765196443079)
XLA Ops:
  0.6 0.0 copy-start.7
  0.6 0.0 copy-start.4
  0.7 0.0 copy-start.6
  0.7 0.0 copy-start
  2.1 2.8 %pack.1 = bf16[16,136,128]{2,1,0:T(8,128)(2,1)} custom-call(s32[1]{0:T(128)} %copy.20.leave_ref, s32[1]{0:T(128)S(6)} %copy.21.target_ref, s32[4,4]{1,0:T(4,128)} %table_ref.1, s32[4]{0:T(128)} %lens_ref.1, bf16[4,1280]{1,0:T(4,128)(2,1)} %qkv_ref, bf16[16,128,512]{2,1,0:T(8,128)(2,1)} %pool_ref.3), custom_call_target="tpu_custom_call" | custom-call | tf_op jit(solution)/shard_map/pack/pallas_call | solution.py:100
  4.9 8.3 %all-to-all-start = ((bf16[16,136,128]{2,1,0:T(8,128)(2,1)}), bf16[16,136,128]{2,1,0:T(8,128)(2,1)S(1)}, u32[]{:S(2)}, u32[]{:S(2)}) async-start(bf16[16,136,128]{2,1,0:T(8,128)(2,1)} %pack.1), calls=%async_computation | async-start | bytes 1114112 | tf_op jit(solution)/shard_map/all_to_all | solution.py:351
  13.2 0.0 copy-done.7
  13.2 0.0 copy-done.4
  13.2 0.0 copy-done.6
  13.2 0.0 copy-done
  13.2 0.0 copy-start.1
  13.3 1.7 %copy-done.1 = bf16[768,1536]{1,0:T(8,128)(2,1)S(1)} copy-done((bf16[768,1536]{1,0:T(8,128)(2,1)S(1)}, bf16[768,1536]{1,0:T(8,128)(2,1)}, u32[]{:S(2)}) %copy-start.1) | copy-done | bytes 2359320
  14.9 0.0 copy-start.10
  14.9 0.0 copy-start.9
  14.9 0.0 copy-start.8
  14.9 0.0 copy-start.3
  14.9 0.0 copy-start.5
  14.9 2.2 %attend.1 = (f32[4,1536]{1,0:T(4,128)S(1)}, bf16[4,128,512]{2,1,0:T(8,128)(2,1)}) custom-call(s32[4,4]{1,0:T(4,128)S(1)} %copy-done.6, s32[4]{0:T(128)S(1)} %copy-done.7, bf16[4,1280]{1,0:T(4,128)(2,1)S(1)} %copy-done.4, bf16[16,128,512]{2,1,0:T(8,128)(2,1)S(1)} %copy-done, bf16[768,1536]{1,0:T(8,128)(2,1)S(1)} %copy-done.1), custom_call_target="tpu_custom_call" | custom-call | flops 76546048 | bytes 4456448 | tf_op jit(solution)/shard_map/attend/pallas_call | solution.py:204
  17.2 0.1 collective-permute-start
  17.3 0.0 copy-done.10
  17.3 0.1 copy.18.gates_ref
  17.4 0.0 copy-done.9
  17.4 0.1 copy.17.ids_ref
  17.5 0.0 copy-done.8
  17.5 0.9 %collective-permute-done.parts_refs_1_ = f32[4,1536]{1,0:T(4,128)S(1)} collective-permute-done((f32[4,1536]{1,0:T(4,128)S(1)}, f32[4,1536]{1,0:T(4,128)S(1)}, u32[]{:S(2)}, u32[]{:S(2)}) %collective-permute-start) | collective-permute-done | bytes 24608 | tf_op jit(solution)/shard_map/ppermute | solution.py:359
  18.4 0.0 copy-done.3
  18.4 0.0 copy-done.5
  18.4 0.0 copy-start.2
  18.4 1.4 %copy-done.2 = bf16[1,1536,512]{2,1,0:T(8,128)(2,1)S(1)} copy-done((bf16[1,1536,512]{2,1,0:T(8,128)(2,1)S(1)}, bf16[1,1536,512]{2,1,0:T(8,128)(2,1)}, u32[]{:S(2)}) %copy-start.2) | copy-done | bytes 1572888
  19.8 0.6 %experts.1 = (f32[4,1536]{1,0:T(4,128)S(1)}, f32[4,1536]{1,0:T(4,128)S(1)}) custom-call(s32[1]{0:T(128)} %bitcast.1.index_ref, s32[4,1]{1,0:T(4,128)S(1)} %copy.17.ids_ref, bf16[4,1]{1,0:T(4,128)(2,1)S(1)} %copy.18.gates_ref, bf16[4,1536]{1,0:T(4,128)(2,1)S(1)} %copy-done.5, f32[1,1536]{1,0:T(1,128)S(1)} %broadcast_in_dim.12.gain_ref, ...), custom_call_target="tpu_custom_call" | custom-call | flops 9437184 | bytes 2359296 | tf_op jit(solution)/shard_map/experts/pallas_call | solution.py:249
  20.4 0.2 collective-permute-start.1
  20.6 0.6 %dynamic_slice.19 = s32[1]{0:T(128)} dynamic-slice(s32[4]{0:T(128)S(1)} %copy-done.7, s32[]{:T(128)S(6)} %select_n.25), dynamic_slice_sizes={1} | dynamic-slice | bytes 12 | tf_op jit(solution)/shard_map/dynamic_slice | solution.py:375
  23.8 0.0 collective-permute-done.1
  23.9 5.0 %all-to-all-done.landed_ref = bf16[16,136,128]{2,1,0:T(8,128)(2,1)S(1)} async-done(((bf16[16,136,128]{2,1,0:T(8,128)(2,1)}), bf16[16,136,128]{2,1,0:T(8,128)(2,1)S(1)}, u32[]{:S(2)}, u32[]{:S(2)}) %all-to-all-start) | async-done | bytes 557088 | tf_op jit(solution)/shard_map/all_to_all | solution.py:351
  28.9 1.0 %forward.1 = bf16[16,136,128]{2,1,0:T(8,128)(2,1)} custom-call(s32[1]{0:T(128)S(6)} %copy.21.target_ref, bf16[16,136,128]{2,1,0:T(8,128)(2,1)S(1)} %all-to-all-done.landed_ref, bf16[8,128]{1,0:T(8,128)(2,1)S(1)} %concatenate.3.extra_ref), custom_call_target="tpu_custom_call" | custom-call | tf_op jit(solution)/shard_map/forward/pallas_call | solution.py:277
  29.9 4.0 %all-to-all-start.1 = ((bf16[16,136,128]{2,1,0:T(8,128)(2,1)}), bf16[16,136,128]{2,1,0:T(8,128)(2,1)S(1)}, u32[]{:S(2)}, u32[]{:S(2)}) async-start(bf16[16,136,128]{2,1,0:T(8,128)(2,1)} %forward.1), calls=%async_computation.1 | async-start | bytes 1114112 | tf_op jit(solution)/shard_map/all_to_all | solution.py:351
  33.9 15.0 %all-to-all-done.1.landed_ref = bf16[16,136,128]{2,1,0:T(8,128)(2,1)S(1)} async-done(((bf16[16,136,128]{2,1,0:T(8,128)(2,1)}), bf16[16,136,128]{2,1,0:T(8,128)(2,1)S(1)}, u32[]{:S(2)}, u32[]{:S(2)}) %all-to-all-start.1) | async-done | bytes 557088 | tf_op jit(solution)/shard_map/all_to_all | solution.py:351
  48.9 1.5 %settle.1 = (bf16[4,768]{1,0:T(4,128)(2,1)}, bf16[4,128,512]{2,1,0:T(8,128)(2,1)}, bf16[4,128,512]{2,1,0:T(8,128)(2,1)}) custom-call(f32[8,128]{1,0:T(8,128)S(1)} %broadcast_in_dim.10.slot_ref, bf16[16,136,128]{2,1,0:T(8,128)(2,1)S(1)} %all-to-all-done.1.landed_ref, bf16[4,768]{1,0:T(4,128)(2,1)S(1)} %add_convert_fusion.hidden_ref, ...), custom_call_target="tpu_custom_call", output_to_operand_aliasing={{1}: (3, {})} | custom-call | tf_op jit(solution)/shard_map/settle/pallas_call | solution.py:314
  (7 shorter events, 0.1 us)
Async XLA Ops:
  0.6 12.6 %copy-start.7 = (s32[4]{0:T(128)S(1)}, s32[4]{0:T(128)}, u32[]{:S(2)}) copy-start(s32[4]{0:T(128)} %lens_ref.1) | copy-start | bytes 52
  0.6 12.6 %copy-start.4 = (bf16[4,1280]{1,0:T(4,128)(2,1)S(1)}, bf16[4,1280]{1,0:T(4,128)(2,1)}, u32[]{:S(2)}) copy-start(bf16[4,1280]{1,0:T(4,128)(2,1)} %qkv_ref) | copy-start | bytes 30724
  0.7 12.6 %copy-start.6 = (s32[4,4]{1,0:T(4,128)S(1)}, s32[4,4]{1,0:T(4,128)}, u32[]{:S(2)}) copy-start(s32[4,4]{1,0:T(4,128)} %table_ref.1) | copy-start | bytes 196
  0.7 12.6 %copy-start = (bf16[16,128,512]{2,1,0:T(8,128)(2,1)S(1)}, bf16[16,128,512]{2,1,0:T(8,128)(2,1)}, u32[]{:S(2)}) copy-start(bf16[16,128,512]{2,1,0:T(8,128)(2,1)} %pool_ref.3) | copy-start | bytes 6291460
  4.9 24.0 %all-to-all-start = ((bf16[16,136,128]{2,1,0:T(8,128)(2,1)}), bf16[16,136,128]{2,1,0:T(8,128)(2,1)S(1)}, u32[]{:S(2)}, u32[]{:S(2)}) async-start(bf16[16,136,128]{2,1,0:T(8,128)(2,1)} %pack.1), calls=%async_computation | async-start | bytes 1114112 | tf_op jit(solution)/shard_map/all_to_all | solution.py:351
  13.2 1.7 %copy-start.1 = (bf16[768,1536]{1,0:T(8,128)(2,1)S(1)}, bf16[768,1536]{1,0:T(8,128)(2,1)}, u32[]{:S(2)}) copy-start(bf16[768,1536]{1,0:T(8,128)(2,1)} %proj_ref.1) | copy-start | bytes 7077892
  14.9 2.4 %copy-start.10 = (bf16[4,1]{0,1:T(2,128)(2,1)S(1)}, bf16[4,1]{0,1:T(2,128)(2,1)}, u32[]{:S(2)}) copy-start(bf16[4,1]{0,1:T(2,128)(2,1)} %param.21) | copy-start | bytes 28
  14.9 2.5 %copy-start.9 = (s32[4,1]{0,1:T(1,128)S(1)}, s32[4,1]{0,1:T(1,128)}, u32[]{:S(2)}) copy-start(s32[4,1]{0,1:T(1,128)} %param.20) | copy-start | bytes 52
  14.9 2.6 %copy-start.8 = (f32[1536]{0:T(1024)S(1)}, f32[1536]{0:T(1024)}, u32[]{:S(2)}) copy-start(f32[1536]{0:T(1024)} %param.22) | copy-start | bytes 18436
  14.9 3.5 %copy-start.3 = (bf16[1,256,1536]{2,1,0:T(8,128)(2,1)S(1)}, bf16[1,256,1536]{2,1,0:T(8,128)(2,1)}, u32[]{:S(2)}) copy-start(bf16[1,256,1536]{2,1,0:T(8,128)(2,1)} %down_ref.1) | copy-start | bytes 2359300
  14.9 3.5 %copy-start.5 = (bf16[4,1536]{1,0:T(4,128)(2,1)S(1)}, bf16[4,1536]{1,0:T(4,128)(2,1)}, u32[]{:S(2)}) copy-start(bf16[4,1536]{1,0:T(4,128)(2,1)} %resid_ref.1) | copy-start | bytes 36868
  17.2 1.3 %collective-permute-start = (f32[4,1536]{1,0:T(4,128)S(1)}, f32[4,1536]{1,0:T(4,128)S(1)}, u32[]{:S(2)}, u32[]{:S(2)}) collective-permute-start(f32[4,1536]{1,0:T(4,128)S(1)} %get-tuple-element.11.parts_refs_0_), channel_id=1, source_target_pairs={{0,1},{1,0},{2,3},{3,2},{4,5},{5,4},{6,7},{7,6},{8,9},{9,8},{10,11... | collective-permute-start | bytes 73736 | tf_op jit(solution)/shard_map/ppermute | solution.py:359
  18.4 1.4 %copy-start.2 = (bf16[1,1536,512]{2,1,0:T(8,128)(2,1)S(1)}, bf16[1,1536,512]{2,1,0:T(8,128)(2,1)}, u32[]{:S(2)}) copy-start(bf16[1,1536,512]{2,1,0:T(8,128)(2,1)} %in_ref.1) | copy-start | bytes 4718596
  20.4 3.4 %collective-permute-start.1 = (f32[4,768]{1,0:T(4,128)S(1)}, f32[4,768]{1,0:T(4,128)S(1)}, u32[]{:S(2)}, u32[]{:S(2)}) collective-permute-start(f32[4,768]{1,0:T(4,128)S(1)} %constant_dynamic-slice_fusion), channel_id=1, source_target_pairs={{0,1},{1,0},{2,3},{3,2},{4,5},{5,4},{6,7},{7,6},{8,9},{9,8},{10,11... | collective-permute-start | bytes 36872 | tf_op jit(solution)/shard_map/ppermute | solution.py:371
  29.9 19.0 %all-to-all-start.1 = ((bf16[16,136,128]{2,1,0:T(8,128)(2,1)}), bf16[16,136,128]{2,1,0:T(8,128)(2,1)S(1)}, u32[]{:S(2)}, u32[]{:S(2)}) async-start(bf16[16,136,128]{2,1,0:T(8,128)(2,1)} %forward.1), calls=%async_computation.1 | async-start | bytes 1114112 | tf_op jit(solution)/shard_map/all_to_all | solution.py:351

commit v3 on v2

--- a/solution.py
+++ b/solution.py
@@ -1,3 +1,4 @@
+import functools
 import math
 
 import jax
@@ -18,6 +19,8 @@
 LANES = 128
 EXTRA = 8
 VMEM_BYTES = 16 * 1024 * 1024
+SPREAD = {16: (11, 8, 3, 14, 13, 12, 4, 10, 9, 7, 1, 0, 2, 15, 5, 6)}
+DELIVER = {16: (10, 9, 3, 13, 12, 7, 2, 8, 14, 15, 4, 0, 6, 11, 1, 5)}
 
 SMEM = pl.BlockSpec(memory_space=pltpu.SMEM)
 VMEM = pl.BlockSpec(memory_space=pltpu.VMEM)
@@ -30,6 +33,17 @@
 
 def params():
     return pltpu.CompilerParams(vmem_limit_bytes=VMEM_BYTES)
+
+
+def peers_of(orders, count):
+    return orders.get(count, tuple(range(count)))
+
+
+def place_of(replica, peers):
+    place = replica
+    for k, peer in enumerate(peers):
+        place = jnp.where(replica == peer, k, place)
+    return place
 
 
 def fresh_of(qkv, cols):
@@ -37,15 +51,6 @@
     return jnp.concatenate(
         [qkv[:, h * width + GROUP * HD : (h + 1) * width] for h in range(cols // LANES)], axis=1
     )
-
-
-def blocks_of(pieces, cols):
-    rows = SPAN // pieces
-    return rows, [
-        (j, c * rows, j * rows // PAGE, j * rows % PAGE, c * LANES)
-        for j in range(pieces)
-        for c in range(cols // LANES)
-    ]
 
 
 def put_row(ref, lead, row, fresh):
@@ -56,8 +61,8 @@
 
 
 def pack_kernel(
-    leave_ref, target_ref, table_hbm, lens_hbm, qkv_hbm, pool_ref, send_ref,
-    table_ref, lens_ref, qkv_ref, pages, small_sems, page_sems,
+    pieces, leave_ref, target_ref, table_hbm, lens_hbm, qkv_hbm, pool_ref, send_ref, taken_ref,
+    table_ref, lens_ref, qkv_ref, pages, small_sems, page_sems, send_sems,
 ):
     smalls = [
         pltpu.make_async_copy(source, target, small_sems.at[i])
@@ -67,10 +72,6 @@
     ]
     for copy in smalls:
         copy.start()
-    pieces, slot_rows, _ = send_ref.shape
-    body = slot_rows - EXTRA
-    ticket = jnp.full((pieces, EXTRA, LANES), target_ref[0].astype(jnp.float32), jnp.float32)
-    send_ref[:, body:, :] = ticket.astype(send_ref.dtype)
     smalls[0].wait()
     leave = leave_ref[0]
     copies = [
@@ -79,29 +80,52 @@
     ]
     for copy in copies:
         copy.start()
+    cols = pages.shape[2]
+    rows = SPAN // pieces
+    ticket = place_of(target_ref[0], peers_of(DELIVER, pieces)).astype(jnp.float32)
     smalls[1].wait()
     smalls[2].wait()
     qkv = qkv_ref[...].astype(jnp.float32)
     at_row = lax.broadcasted_iota(jnp.int32, qkv.shape, 0) == leave
     qkv = jnp.sum(jnp.where(at_row, qkv, 0.0), axis=0, keepdims=True)
-    fresh = fresh_of(qkv, pages.shape[2])
+    fresh = fresh_of(qkv, cols)
     length = lens_ref[leave]
-    for copy in copies:
-        copy.wait()
-    put_row(pages, length // PAGE, length % PAGE, fresh)
-    rows, blocks = blocks_of(pieces, pages.shape[2])
-    for piece, at, page, start, column in blocks:
-        send_ref[piece, at : at + rows, :] = pages[page, start : start + rows, column : column + LANES]
+    taken = jnp.zeros((16, LANES), jnp.float32)
+    row_in = lax.broadcasted_iota(jnp.int32, taken.shape, 0)
+    lane = lax.broadcasted_iota(jnp.int32, taken.shape, 1)
+    sends = []
+    for p in range(MAXP):
+        copies[p].wait()
+
+        @pl.when(length // PAGE == p)
+        def _():
+            put_row(pages, p, length % PAGE, fresh)
+
+        for j in range(p * pieces // MAXP, (p + 1) * pieces // MAXP):
+            last = (j + 1) * rows - 1 - p * PAGE
+            start = last // 16 * 16
+            block = pages[p, start : start + 16, :LANES].astype(jnp.float32)
+            at = jnp.logical_and(row_in == last - start, lane == j)
+            taken = taken + jnp.where(at, block, 0.0)
+            pages[p, start : start + 16, :LANES] = jnp.where(at, ticket, block).astype(pages.dtype)
+        sends.append(pltpu.make_async_copy(pages.at[p], send_ref.at[p], send_sems.at[p]))
+        sends[p].start()
+    taken_ref[...] = jnp.sum(taken, axis=0, keepdims=True)
+    for send in sends:
+        send.wait()
 
 
 def pack(leave_slot, target_rep, page_table, req_lengths, qkv_new, kv_pool, pieces):
     cols = kv_pool.shape[2]
-    slot_rows = SPAN // pieces * (cols // LANES) + EXTRA
+    assert pieces % MAXP == 0 and pieces <= LANES
     return pl.pallas_call(
-        pack_kernel,
-        out_shape=pltpu.VMEM((pieces, slot_rows, LANES), kv_pool.dtype),
+        functools.partial(pack_kernel, pieces),
+        out_shape=(
+            pltpu.HBM((MAXP, PAGE, cols), kv_pool.dtype),
+            jax.ShapeDtypeStruct((1, LANES), jnp.float32),
+        ),
         in_specs=[SMEM, SMEM] + [HBM] * 4,
-        out_specs=VMEM,
+        out_specs=(HBM, VMEM),
         scratch_shapes=[
             pltpu.SMEM(page_table.shape, page_table.dtype),
             pltpu.SMEM(req_lengths.shape, req_lengths.dtype),
@@ -109,13 +133,21 @@
             pltpu.VMEM((MAXP, PAGE, cols), kv_pool.dtype),
             pltpu.SemaphoreType.DMA((3,)),
             pltpu.SemaphoreType.DMA((MAXP,)),
+            pltpu.SemaphoreType.DMA((MAXP,)),
         ],
         compiler_params=params(),
         name="pack",
     )(leave_slot, target_rep, *map(in_hbm, (page_table, req_lengths, qkv_new, kv_pool)))
 
 
-def attend_kernel(table_ref, lens_ref, qkv_ref, pool_ref, proj_ref, head_ref, new_ref, stage, sems):
+def attend_kernel(
+    leave_ref, table_ref, lens_ref, qkv_ref, pool_ref, proj_hbm, head_ref, new_ref, note_ref,
+    stage, proj_ref, sems, proj_sem,
+):
+    proj_read = pltpu.make_async_copy(proj_hbm, proj_ref, proj_sem)
+    proj_read.start()
+    note = (lens_ref[leave_ref[0]] // PAGE).astype(jnp.float32)
+    note_ref[...] = jnp.full(note_ref.shape, note, jnp.float32)
     num_req = qkv_ref.shape[0]
     cols = pool_ref.shape[2]
     heads = cols // LANES
@@ -193,12 +225,13 @@
             )
         )
     attn = jnp.concatenate(attn, axis=0).astype(proj_ref.dtype)
+    proj_read.wait()
     head_ref[...] = jnp.dot(attn, proj_ref[...], preferred_element_type=jnp.float32)
     for write in writes:
         write.wait()
 
 
-def attend(page_table, req_lengths, qkv_new, kv_pool, out_proj):
+def attend(leave_slot, page_table, req_lengths, qkv_new, kv_pool, out_proj):
     num_req = qkv_new.shape[0]
     cols = kv_pool.shape[2]
     return pl.pallas_call(
@@ -206,12 +239,15 @@
         out_shape=(
             jax.ShapeDtypeStruct((num_req, out_proj.shape[1]), jnp.float32),
             jax.ShapeDtypeStruct((num_req, PAGE, cols), kv_pool.dtype),
-        ),
-        in_specs=[SMEM, SMEM, VMEM, VMEM, VMEM],
-        out_specs=(VMEM, HBM),
+            jax.ShapeDtypeStruct((1, LANES), jnp.float32),
+        ),
+        in_specs=[SMEM, SMEM, SMEM, VMEM, VMEM, HBM],
+        out_specs=(VMEM, HBM, VMEM),
         scratch_shapes=[
             pltpu.VMEM((num_req, PAGE, cols), kv_pool.dtype),
+            pltpu.VMEM(out_proj.shape, out_proj.dtype),
             pltpu.SemaphoreType.DMA((num_req,)),
+            pltpu.SemaphoreType.DMA,
         ],
         compiler_params=params(),
         cost_estimate=pl.CostEstimate(
@@ -220,7 +256,7 @@
             transcendentals=num_req * 16 * SPAN,
         ),
         name="attend",
-    )(page_table, req_lengths, qkv_new, kv_pool, out_proj)
+    )(leave_slot, page_table, req_lengths, qkv_new, kv_pool, in_hbm(out_proj))
 
 
 def experts_kernel(
@@ -263,53 +299,86 @@
     )
 
 
-def forward_kernel(target_ref, landed_ref, extra_ref, send_ref):
-    pieces, slot_rows, _ = landed_ref.shape
-    body = slot_rows - EXTRA
+def forward_kernel(
+    leave_ref, target_ref, index_ref, landed_ref, hidden_ref, note_ref, taken_ref, send_ref
+):
+    pieces, rows, cols = landed_ref.shape
+    body = rows * cols // LANES
     send_ref[:, body:, :] = jnp.zeros((pieces, EXTRA, LANES), send_ref.dtype)
+    own = place_of(index_ref[0], peers_of(SPREAD, pieces))
+    lane = lax.broadcasted_iota(jnp.int32, (1, LANES), 1)
     for s in range(pieces):
-        target = jnp.max(landed_ref[s, body:, :].astype(jnp.float32)).astype(jnp.int32)
-        send_ref[target, :body, :] = landed_ref[s, :body, :]
-    send_ref[target_ref[0], body:, :] = extra_ref[...]
-
-
-def forward(target_rep, landed, extra):
+        last = landed_ref[s, rows - 1 :, :LANES].astype(jnp.float32)
+        place = jnp.max(jnp.where(lane == own, last, 0.0)).astype(jnp.int32)
+        for c in range(cols // LANES):
+            send_ref[place, c * rows : (c + 1) * rows, :] = landed_ref[s, :, c * LANES : (c + 1) * LANES]
+    hidden = hidden_ref[...].astype(jnp.float32)
+    at_row = lax.broadcasted_iota(jnp.int32, hidden.shape, 0) == leave_ref[0]
+    row = jnp.sum(jnp.where(at_row, hidden, 0.0), axis=0, keepdims=True)
+    spare = (EXTRA - 2) * LANES - row.shape[1]
+    if spare:
+        row = jnp.concatenate([row, jnp.zeros((1, spare), jnp.float32)], axis=1)
+    lines = [row[:, k * LANES : (k + 1) * LANES] for k in range(EXTRA - 2)]
+    place = place_of(target_ref[0], peers_of(DELIVER, pieces))
+    extra = jnp.concatenate(lines + [taken_ref[...], note_ref[...]], axis=0)
+    send_ref[place, body:, :] = extra.astype(send_ref.dtype)
+
+
+def forward(leave_slot, target_rep, rep_index, landed, hidden, note, taken):
+    pieces, rows, cols = landed.shape
     return pl.pallas_call(
         forward_kernel,
-        out_shape=pltpu.VMEM(landed.shape, landed.dtype),
-        in_specs=[SMEM, VMEM, VMEM],
+        out_shape=jax.ShapeDtypeStruct((pieces, rows * cols // LANES + EXTRA, LANES), landed.dtype),
+        in_specs=[SMEM, SMEM, SMEM, VMEM, VMEM, VMEM, VMEM],
         out_specs=VMEM,
         compiler_params=params(),
         name="forward",
-    )(target_rep, landed, extra)
+    )(leave_slot, target_rep, rep_index, landed, hidden, note, taken)
 
 
 def settle_kernel(
-    slot_ref, landed_ref, hidden_ref, new_in_ref, hidden_out_ref, new_ref, arrived_ref, pages, sems
+    leave_ref, landed_ref, hidden_ref, new_in_ref, hidden_out_ref, new_ref, arrived_ref,
+    pages, mixed, page_sems, new_sem, hidden_sem,
 ):
     del new_in_ref
     pieces, slot_rows, _ = landed_ref.shape
     body = slot_rows - EXTRA
-    rows, blocks = blocks_of(pieces, pages.shape[2])
-    for piece, at, page, start, column in blocks:
-        pages[page, start : start + rows, column : column + LANES] = landed_ref[piece, at : at + rows, :]
-    all_pages = pltpu.make_async_copy(pages, arrived_ref, sems.at[0])
-    all_pages.start()
+    cols = pages.shape[2]
+    rows = SPAN // pieces
+    leave = leave_ref[0]
     extra = jnp.sum(landed_ref[:, body:, :].astype(jnp.float32), axis=0)
+    taken = extra[EXTRA - 2 : EXTRA - 1, :]
+    spread, deliver = peers_of(SPREAD, pieces), peers_of(DELIVER, pieces)
+    row_in = lax.broadcasted_iota(jnp.int32, (rows, LANES), 0)
+    lane = lax.broadcasted_iota(jnp.int32, (rows, LANES), 1)
+    writes = []
+    for p in range(MAXP):
+        for j in range(p * pieces // MAXP, (p + 1) * pieces // MAXP):
+            slot = deliver.index(spread[j])
+            start = j * rows - p * PAGE
+            for c in range(cols // LANES):
+                block = landed_ref[slot, c * rows : (c + 1) * rows, :]
+                if c == 0:
+                    at = jnp.logical_and(row_in == rows - 1, lane == j)
+                    block = jnp.where(at, taken, block.astype(jnp.float32)).astype(pages.dtype)
+                pages[p, start : start + rows, c * LANES : (c + 1) * LANES] = block
+        writes.append(pltpu.make_async_copy(pages.at[p], arrived_ref.at[p], page_sems.at[p]))
+        writes[p].start()
     page = jnp.max(extra[EXTRA - 1 :, :]).astype(jnp.int32)
-    leave = jnp.max(slot_ref[...]).astype(jnp.int32)
-    new_page = pltpu.make_async_copy(pages.at[page], new_ref.at[leave], sems.at[1])
-    new_page.start()
+    writes.append(pltpu.make_async_copy(pages.at[page], new_ref.at[leave], new_sem))
+    writes[-1].start()
     width = hidden_ref.shape[1]
     row = jnp.concatenate([extra[k : k + 1, :] for k in range(-(-width // LANES))], axis=1)
     hidden = hidden_ref[...].astype(jnp.float32)
     at_row = lax.broadcasted_iota(jnp.int32, hidden.shape, 0) == leave
-    hidden_out_ref[...] = jnp.where(at_row, row[:, :width], hidden).astype(hidden_out_ref.dtype)
-    all_pages.wait()
-    new_page.wait()
-
-
-def settle(slot, landed, hidden, new_pages):
+    mixed[...] = jnp.where(at_row, row[:, :width], hidden).astype(mixed.dtype)
+    writes.append(pltpu.make_async_copy(mixed, hidden_out_ref, hidden_sem))
+    writes[-1].start()
+    for write in writes:
+        write.wait()
+
+
+def settle(leave_slot, landed, hidden, new_pages):
     arrived = (MAXP,) + new_pages.shape[1:]
     return pl.pallas_call(
         settle_kernel,
@@ -318,13 +387,19 @@
             jax.ShapeDtypeStruct(new_pages.shape, new_pages.dtype),
             jax.ShapeDtypeStruct(arrived, new_pages.dtype),
         ),
-        in_specs=[VMEM, VMEM, VMEM, HBM],
-        out_specs=(VMEM, HBM, HBM),
-        scratch_shapes=[pltpu.VMEM(arrived, new_pages.dtype), pltpu.SemaphoreType.DMA((2,))],
+        in_specs=[SMEM, VMEM, VMEM, HBM],
+        out_specs=(HBM, HBM, HBM),
+        scratch_shapes=[
+            pltpu.VMEM(arrived, new_pages.dtype),
+            pltpu.VMEM(hidden.shape, hidden.dtype),
+            pltpu.SemaphoreType.DMA((MAXP,)),
+            pltpu.SemaphoreType.DMA,
+            pltpu.SemaphoreType.DMA,
+        ],
         input_output_aliases={3: 1},
         compiler_params=params(),
         name="settle",
-    )(slot, landed, hidden, new_pages)
+    )(leave_slot, landed, hidden, new_pages)
 
 
 def local(
@@ -345,16 +420,20 @@
     pieces = lax.axis_size("rep")
     tp_size = lax.axis_size("tp")
     tp_index = lax.axis_index("tp")
-    assert pieces <= 256
-
-    def exchange(packet):
-        return lax.all_to_all(packet, "rep", split_axis=0, concat_axis=0, tiled=True)
-
-    send = pack(leave_slot, target_rep, page_table, req_lengths, qkv_new, kv_pool, pieces)
+
+    def exchange(packet, orders):
+        return lax.all_to_all(
+            packet, "rep", split_axis=0, concat_axis=0, tiled=True,
+            axis_index_groups=[peers_of(orders, pieces)],
+        )
+
+    send, taken = pack(leave_slot, target_rep, page_table, req_lengths, qkv_new, kv_pool, pieces)
     send, qkv_new = lax.optimization_barrier((send, qkv_new))
-    landed = exchange(send)
-
-    head_part, new_pages = attend(page_table, req_lengths, qkv_new, kv_pool, out_proj)
+    landed = exchange(send.reshape(pieces, SPAN // pieces, kv_pool.shape[2]), SPREAD)
+
+    head_part, new_pages, note = attend(
+        leave_slot, page_table, req_lengths, qkv_new, kv_pool, out_proj
+    )
     shifts = [[(i, (i + k) % tp_size) for i in range(tp_size)] for k in range(1, tp_size)]
     parts = [head_part] + [lax.ppermute(head_part, "tp", shift) for shift in shifts]
     assert expert_in.shape[0] == 1
@@ -370,14 +449,11 @@
     for k, shift in enumerate(shifts, 1):
         mix = mix + lax.ppermute(share(total, (tp_index + k) % tp_size), "tp", shift)
     hidden = (share(stream, tp_index) + mix).astype(jnp.bfloat16)
-    row = lax.dynamic_slice_in_dim(hidden, leave_slot[0], 1, 0)[0]
-    row = jnp.pad(row, (0, (EXTRA - 1) * LANES - width)).reshape(EXTRA - 1, LANES)
-    page_number = (req_lengths[leave_slot[0]] // PAGE).astype(hidden.dtype)
-    extra = jnp.concatenate([row, jnp.full((1, LANES), page_number)], axis=0)
-    slot = jnp.full((EXTRA, LANES), leave_slot[0].astype(jnp.float32))
-
-    landed = exchange(forward(target_rep, landed, extra))
-    return settle(slot, landed, hidden, new_pages)
+    rep_index = lax.axis_index("rep")[None]
+    landed = exchange(
+        forward(leave_slot, target_rep, rep_index, landed, hidden, note, taken), DELIVER
+    )
+    return settle(leave_slot, landed, hidden, new_pages)
 
 
 def solution(mesh):

time: 50.9 us -> 45.7 us (0.90)
  blocking collectives: 0 us -> 18.4 us
  waiting for transfers between devices: 20.9 us -> 5.46 us
  starting transfers between devices: 12.6 us -> 9.64 us
  between operations: 4.88 us -> 2.25 us
  local copies, waits for them, and re-layouts: 3.94 us -> 1.67 us
    all_to_all x0 -> x1, blocking collectives: none -> 18.4 us  [exchange(): lax.all_to_all(packet, 'rep', split_axis=0, concat_axis=0, tiled=True, ax...]
    all_to_all x2 -> x1, waiting for transfers between devices: 19.9 us -> 3.51 us  [exchange(): lax.all_to_all(packet, 'rep', split_axis=0, concat_axis=0, tiled=True, ax...]
    all_to_all x2 -> x1, starting transfers between devices: 12.3 us -> 9.36 us  [exchange(): lax.all_to_all(packet, 'rep', split_axis=0, concat_axis=0, tiled=True, ax...]
    unnamed x24 -> x22, local copies, waits for them, and re-layouts: 3.31 us -> 1.66 us
    pallas_call x1, Pallas kernels: 2.22 us -> 3.57 us  [attend(): pl.pallas_call(attend_kernel, out_shape=(jax.ShapeDtypeStruct((num_req, o...]
    ppermute x1, waiting for transfers between devices: 0.01 us -> 1.01 us  [local(): lax.ppermute(share(total, (tp_index + k) % tp_size), 'tp', shift)]
    pallas_call x2, Pallas kernels: 3.72 us -> 2.76 us  [the longest x1 2.55 us: pack(): pl.pallas_call(functools.partial(pack_kernel, pieces), out_shape=(pltpu.H...]
    pallas_call x1, Pallas kernels: 1.53 us -> 0.91 us  [settle(): pl.pallas_call(settle_kernel, out_shape=(jax.ShapeDtypeStruct(hidden.shap...]
  transfers between devices with their start and end apart: 4 -> 3, of which waited for: 3 -> 3; matrix products, arithmetic and copies ran while one was open for 2% -> 0% of each run, Pallas kernels for 6% -> 9%
where the time goes in v3:
time: 45.7 us; the launch traced here: 45.2 us
  blocking collectives  18.4 us (40%)
  starting transfers between devices  9.64 us (21%)
  Pallas kernels  7.82 us (17%)
  waiting for transfers between devices  5.46 us (12%)
  between operations  2.25 us (5%)
  local copies, waits for them, and re-layouts  1.67 us (4%)
    all_to_all x1, blocking collectives, exchange(): lax.all_to_all(packet, 'rep', split_axis=0, concat_axis=0, tiled=True, ax...  18.4 us
    all_to_all x1, starting transfers between devices, exchange(): lax.all_to_all(packet, 'rep', split_axis=0, concat_axis=0, tiled=True, ax...  9.36 us
    pallas_call x1, Pallas kernels, attend(): pl.pallas_call(attend_kernel, out_shape=(jax.ShapeDtypeStruct((num_req, o...  3.57 us
    all_to_all x1, waiting for transfers between devices, exchange(): lax.all_to_all(packet, 'rep', split_axis=0, concat_axis=0, tiled=True, ax...  3.51 us
    pallas_call x1, Pallas kernels, pack(): pl.pallas_call(functools.partial(pack_kernel, pieces), out_shape=(pltpu.H...  2.55 us
    unnamed x22, local copies, waits for them, and re-layouts  1.66 us
    ppermute x1, waiting for transfers between devices, local(): lax.ppermute(share(total, (tp_index + k) % tp_size), 'tp', shift)  1.01 us
    ppermute x1, waiting for transfers between devices, local(): lax.ppermute(head_part, 'tp', shift)  0.94 us
  transfers between devices with their start and end apart: 3, of which 3 were waited for; matrix products, arithmetic and copies ran while one was open for 0% of the time, Pallas kernels for 9%

profile of v3, /device:TPU:0, one launch (start us, length us, event | category | flops | bytes accessed | tf_op | source)
XLA Modules:
  0.0 45.2 jit_solution(7079607487774461789)
XLA Ops:
  0.6 0.0 copy-start.3
  0.6 0.0 copy-start.6
  0.7 0.0 copy-start.5
  0.7 0.0 copy-start
  2.1 2.5 %pack.1 = (bf16[4,128,512]{2,1,0:T(8,128)(2,1)}, f32[1,128]{1,0:T(1,128)S(1)}) custom-call(s32[1]{0:T(128)S(6)} %copy.20.leave_ref, s32[1]{0:T(128)S(6)} %copy.21.target_ref, s32[4,4]{1,0:T(4,128)} %table_ref.1, s32[4]{0:T(128)} %lens_ref.1, bf16[4,1280]{1,0:T(4,128)(2,1)} %qkv_ref, bf16[16,128,512]{2,1,0:T(8,128)(2,1)} %pool_ref.3), custom_call_target="tpu_custom_call" | custom-call | tf_op jit(solution)/shard_map/pack/pallas_call | solution.py:121
  4.7 9.4 %all-to-all-start = ((bf16[16,32,512]{2,1,0:T(8,128)(2,1)}), bf16[16,32,512]{2,1,0:T(8,128)(2,1)S(1)}, u32[]{:S(2)}, u32[]{:S(2)}) async-start(bf16[16,32,512]{2,1,0:T(8,128)(2,1)} %bitcast.3), calls=%async_computation | async-start | bytes 1048576 | tf_op jit(solution)/shard_map/all_to_all | solution.py:425
  14.0 0.0 copy-done.3
  14.0 0.0 copy-done.6
  14.0 0.0 copy-done.5
  14.1 0.0 copy-done
  14.1 0.0 copy-start.9
  14.1 0.0 copy-start.8
  14.1 0.0 copy-start.7
  14.1 0.0 copy-start.2
  14.1 0.0 copy-start.4
  14.1 3.6 %attend.1 = (f32[4,1536]{1,0:T(4,128)S(1)}, bf16[4,128,512]{2,1,0:T(8,128)(2,1)}, f32[1,128]{1,0:T(1,128)S(1)}) custom-call(s32[1]{0:T(128)S(6)} %copy.20.leave_ref, s32[4,4]{1,0:T(4,128)S(1)} %copy-done.5, s32[4]{0:T(128)S(1)} %copy-done.6, bf16[4,1280]{1,0:T(4,128)(2,1)S(1)} %copy-done.3, bf16[16,128,512]{2,1,0:T(8,128)(2,1)S(1)} %copy-done, ...), custom_call_target="tpu_custom_call" | custom-call | flops 76546048 | bytes 4456448 | tf_op jit(solution)/shard_map/attend/pallas_call | solution.py:237
  17.7 0.1 collective-permute-start
  17.8 0.0 copy-done.9
  17.8 0.1 copy.18.gates_ref
  17.9 0.0 copy-done.8
  17.9 0.1 copy.17.ids_ref
  18.0 0.0 copy-done.7
  18.0 0.9 %collective-permute-done.parts_refs_1_ = f32[4,1536]{1,0:T(4,128)S(1)} collective-permute-done((f32[4,1536]{1,0:T(4,128)S(1)}, f32[4,1536]{1,0:T(4,128)S(1)}, u32[]{:S(2)}, u32[]{:S(2)}) %collective-permute-start) | collective-permute-done | bytes 24608 | tf_op jit(solution)/shard_map/ppermute | solution.py:438
  19.0 0.0 copy-done.2
  19.0 0.0 copy-done.4
  19.0 0.0 copy-start.1
  19.0 1.4 %copy-done.1 = bf16[1,1536,512]{2,1,0:T(8,128)(2,1)S(1)} copy-done((bf16[1,1536,512]{2,1,0:T(8,128)(2,1)S(1)}, bf16[1,1536,512]{2,1,0:T(8,128)(2,1)}, u32[]{:S(2)}) %copy-start.1) | copy-done | bytes 1572888
  20.4 0.6 %experts.1 = (f32[4,1536]{1,0:T(4,128)S(1)}, f32[4,1536]{1,0:T(4,128)S(1)}) custom-call(s32[1]{0:T(128)} %bitcast.2.index_ref, s32[4,1]{1,0:T(4,128)S(1)} %copy.17.ids_ref, bf16[4,1]{1,0:T(4,128)(2,1)S(1)} %copy.18.gates_ref, bf16[4,1536]{1,0:T(4,128)(2,1)S(1)} %copy-done.4, f32[1,1536]{1,0:T(1,128)S(1)} %broadcast_in_dim.11.gain_ref, ...), custom_call_target="tpu_custom_call" | custom-call | flops 9437184 | bytes 2359296 | tf_op jit(solution)/shard_map/experts/pallas_call | solution.py:285
  21.0 0.2 collective-permute-start.1
  21.2 1.0 %collective-permute-done.1 = f32[4,768]{1,0:T(4,128)S(1)} collective-permute-done((f32[4,768]{1,0:T(4,128)S(1)}, f32[4,768]{1,0:T(4,128)S(1)}, u32[]{:S(2)}, u32[]{:S(2)}) %collective-permute-start.1) | collective-permute-done | bytes 12320 | tf_op jit(solution)/shard_map/ppermute | solution.py:450
  22.2 3.5 %all-to-all-done.landed_ref = bf16[16,32,512]{2,1,0:T(8,128)(2,1)S(1)} async-done(((bf16[16,32,512]{2,1,0:T(8,128)(2,1)}), bf16[16,32,512]{2,1,0:T(8,128)(2,1)S(1)}, u32[]{:S(2)}, u32[]{:S(2)}) %all-to-all-start) | async-done | bytes 524320 | tf_op jit(solution)/shard_map/all_to_all | solution.py:425
  25.7 0.2 forward.1
  25.9 18.4 %all_to_all.10.landed_ref = bf16[16,136,128]{2,1,0:T(8,128)(2,1)S(1)} all-to-all(bf16[16,136,128]{2,1,0:T(8,128)(2,1)S(1)} %forward.1), channel_id=1, replica_groups={{20,18,6,26,24,14,4,16,28,30,8,0,12,22,2,10},{21,19,7,27,25,15,5,17,29,..., dimensions={0} | all-to-all | bytes 1114112 | tf_op jit(solution)/shard_map/all_to_all | solution.py:425
  44.3 0.9 %settle.1 = (bf16[4,768]{1,0:T(4,128)(2,1)}, bf16[4,128,512]{2,1,0:T(8,128)(2,1)}, bf16[4,128,512]{2,1,0:T(8,128)(2,1)}) custom-call(s32[1]{0:T(128)S(6)} %copy.20.leave_ref, bf16[16,136,128]{2,1,0:T(8,128)(2,1)S(1)} %all_to_all.10.landed_ref, bf16[4,768]{1,0:T(4,128)(2,1)S(1)} %add_convert_fusion.hidden_ref, ...), custom_call_target="tpu_custom_call", output_to_operand_aliasing={{1}: (3, {})} | custom-call | tf_op jit(solution)/shard_map/settle/pallas_call | solution.py:383
  (3 shorter events, 0.0 us)
Async XLA Ops:
  0.6 13.4 %copy-start.3 = (bf16[4,1280]{1,0:T(4,128)(2,1)S(1)}, bf16[4,1280]{1,0:T(4,128)(2,1)}, u32[]{:S(2)}) copy-start(bf16[4,1280]{1,0:T(4,128)(2,1)} %qkv_ref) | copy-start | bytes 30724
  0.6 13.4 %copy-start.6 = (s32[4]{0:T(128)S(1)}, s32[4]{0:T(128)}, u32[]{:S(2)}) copy-start(s32[4]{0:T(128)} %lens_ref.1) | copy-start | bytes 52
  0.7 13.4 %copy-start.5 = (s32[4,4]{1,0:T(4,128)S(1)}, s32[4,4]{1,0:T(4,128)}, u32[]{:S(2)}) copy-start(s32[4,4]{1,0:T(4,128)} %table_ref.1) | copy-start | bytes 196
  0.7 13.4 %copy-start = (bf16[16,128,512]{2,1,0:T(8,128)(2,1)S(1)}, bf16[16,128,512]{2,1,0:T(8,128)(2,1)}, u32[]{:S(2)}) copy-start(bf16[16,128,512]{2,1,0:T(8,128)(2,1)} %pool_ref.3) | copy-start | bytes 6291460
  4.7 21.0 %all-to-all-start = ((bf16[16,32,512]{2,1,0:T(8,128)(2,1)}), bf16[16,32,512]{2,1,0:T(8,128)(2,1)S(1)}, u32[]{:S(2)}, u32[]{:S(2)}) async-start(bf16[16,32,512]{2,1,0:T(8,128)(2,1)} %bitcast.3), calls=%async_computation | async-start | bytes 1048576 | tf_op jit(solution)/shard_map/all_to_all | solution.py:425
  14.1 3.7 %copy-start.9 = (bf16[4,1]{0,1:T(2,128)(2,1)S(1)}, bf16[4,1]{0,1:T(2,128)(2,1)}, u32[]{:S(2)}) copy-start(bf16[4,1]{0,1:T(2,128)(2,1)} %param.21) | copy-start | bytes 28
  14.1 3.8 %copy-start.8 = (s32[4,1]{0,1:T(1,128)S(1)}, s32[4,1]{0,1:T(1,128)}, u32[]{:S(2)}) copy-start(s32[4,1]{0,1:T(1,128)} %param.20) | copy-start | bytes 52
  14.1 3.9 %copy-start.7 = (f32[1536]{0:T(1024)S(1)}, f32[1536]{0:T(1024)}, u32[]{:S(2)}) copy-start(f32[1536]{0:T(1024)} %param.22) | copy-start | bytes 18436
  14.1 4.9 %copy-start.2 = (bf16[1,256,1536]{2,1,0:T(8,128)(2,1)S(1)}, bf16[1,256,1536]{2,1,0:T(8,128)(2,1)}, u32[]{:S(2)}) copy-start(bf16[1,256,1536]{2,1,0:T(8,128)(2,1)} %down_ref.1) | copy-start | bytes 2359300
  14.1 4.9 %copy-start.4 = (bf16[4,1536]{1,0:T(4,128)(2,1)S(1)}, bf16[4,1536]{1,0:T(4,128)(2,1)}, u32[]{:S(2)}) copy-start(bf16[4,1536]{1,0:T(4,128)(2,1)} %resid_ref.1) | copy-start | bytes 36868
  17.7 1.3 %collective-permute-start = (f32[4,1536]{1,0:T(4,128)S(1)}, f32[4,1536]{1,0:T(4,128)S(1)}, u32[]{:S(2)}, u32[]{:S(2)}) collective-permute-start(f32[4,1536]{1,0:T(4,128)S(1)} %get-tuple-element.15.parts_refs_0_), channel_id=1, source_target_pairs={{0,1},{1,0},{2,3},{3,2},{4,5},{5,4},{6,7},{7,6},{8,9},{9,8},{10,11... | collective-permute-start | bytes 73736 | tf_op jit(solution)/shard_map/ppermute | solution.py:438
  19.0 1.4 %copy-start.1 = (bf16[1,1536,512]{2,1,0:T(8,128)(2,1)S(1)}, bf16[1,1536,512]{2,1,0:T(8,128)(2,1)}, u32[]{:S(2)}) copy-start(bf16[1,1536,512]{2,1,0:T(8,128)(2,1)} %in_ref.1) | copy-start | bytes 4718596
  21.0 1.2 %collective-permute-start.1 = (f32[4,768]{1,0:T(4,128)S(1)}, f32[4,768]{1,0:T(4,128)S(1)}, u32[]{:S(2)}, u32[]{:S(2)}) collective-permute-start(f32[4,768]{1,0:T(4,128)S(1)} %constant_dynamic-slice_fusion), channel_id=1, source_target_pairs={{0,1},{1,0},{2,3},{3,2},{4,5},{5,4},{6,7},{7,6},{8,9},{9,8},{10,11... | collective-permute-start | bytes 36872 | tf_op jit(solution)/shard_map/ppermute | solution.py:450

commit v4 on v3

--- a/solution.py
+++ b/solution.py
@@ -19,8 +19,10 @@
 LANES = 128
 EXTRA = 8
 VMEM_BYTES = 16 * 1024 * 1024
-SPREAD = {16: (11, 8, 3, 14, 13, 12, 4, 10, 9, 7, 1, 0, 2, 15, 5, 6)}
-DELIVER = {16: (10, 9, 3, 13, 12, 7, 2, 8, 14, 15, 4, 0, 6, 11, 1, 5)}
+ORDERS = {(16, 2): (
+    (0, 8, 2, 3, 4, 5, 6, 13, 1, 15, 10, 11, 14, 7, 12, 9),
+    (10, 9, 8, 11, 4, 15, 12, 0, 2, 3, 1, 13, 14, 7, 6, 5),
+)}
 
 SMEM = pl.BlockSpec(memory_space=pltpu.SMEM)
 VMEM = pl.BlockSpec(memory_space=pltpu.VMEM)
@@ -35,14 +37,12 @@
     return pltpu.CompilerParams(vmem_limit_bytes=VMEM_BYTES)
 
 
-def peers_of(orders, count):
-    return orders.get(count, tuple(range(count)))
-
-
-def place_of(replica, peers):
+def place_of(replica, tp_index, mesh_shape):
     place = replica
-    for k, peer in enumerate(peers):
-        place = jnp.where(replica == peer, k, place)
+    for core, peers in enumerate(ORDERS.get(mesh_shape, ())):
+        for k, peer in enumerate(peers):
+            hit = jnp.logical_and(replica == peer, tp_index == core)
+            place = jnp.where(hit, k, place)
     return place
 
 
@@ -61,7 +61,7 @@
 
 
 def pack_kernel(
-    pieces, leave_ref, target_ref, table_hbm, lens_hbm, qkv_hbm, pool_ref, send_ref, taken_ref,
+    mesh_shape, leave_ref, target_ref, tp_ref, table_hbm, lens_hbm, qkv_hbm, pool_ref, send_ref, taken_ref,
     table_ref, lens_ref, qkv_ref, pages, small_sems, page_sems, send_sems,
 ):
     smalls = [
@@ -81,8 +81,9 @@
     for copy in copies:
         copy.start()
     cols = pages.shape[2]
+    pieces = mesh_shape[0]
     rows = SPAN // pieces
-    ticket = place_of(target_ref[0], peers_of(DELIVER, pieces)).astype(jnp.float32)
+    ticket = place_of(target_ref[0], tp_ref[0], mesh_shape).astype(jnp.float32)
     smalls[1].wait()
     smalls[2].wait()
     qkv = qkv_ref[...].astype(jnp.float32)
@@ -115,16 +116,17 @@
         send.wait()
 
 
-def pack(leave_slot, target_rep, page_table, req_lengths, qkv_new, kv_pool, pieces):
+def pack(mesh_shape, leave_slot, target_rep, tp_index, page_table, req_lengths, qkv_new, kv_pool):
     cols = kv_pool.shape[2]
+    pieces = mesh_shape[0]
     assert pieces % MAXP == 0 and pieces <= LANES
     return pl.pallas_call(
-        functools.partial(pack_kernel, pieces),
+        functools.partial(pack_kernel, mesh_shape),
         out_shape=(
             pltpu.HBM((MAXP, PAGE, cols), kv_pool.dtype),
             jax.ShapeDtypeStruct((1, LANES), jnp.float32),
         ),
-        in_specs=[SMEM, SMEM] + [HBM] * 4,
+        in_specs=[SMEM] * 3 + [HBM] * 4,
         out_specs=(HBM, VMEM),
         scratch_shapes=[
             pltpu.SMEM(page_table.shape, page_table.dtype),
@@ -137,7 +139,7 @@
         ],
         compiler_params=params(),
         name="pack",
-    )(leave_slot, target_rep, *map(in_hbm, (page_table, req_lengths, qkv_new, kv_pool)))
+    )(leave_slot, target_rep, tp_index, *map(in_hbm, (page_table, req_lengths, qkv_new, kv_pool)))
 
 
 def attend_kernel(
@@ -295,17 +297,17 @@
         ),
         name="experts",
     )(
-        tp_index[None], expert_ids, gate_weights, resid, norm_gain[None, :], expert_in, expert_down, *parts
+        tp_index, expert_ids, gate_weights, resid, norm_gain[None, :], expert_in, expert_down, *parts
     )
 
 
 def forward_kernel(
-    leave_ref, target_ref, index_ref, landed_ref, hidden_ref, note_ref, taken_ref, send_ref
+    mesh_shape, leave_ref, target_ref, tp_ref, index_ref, landed_ref, hidden_ref, note_ref, taken_ref, send_ref
 ):
     pieces, rows, cols = landed_ref.shape
     body = rows * cols // LANES
     send_ref[:, body:, :] = jnp.zeros((pieces, EXTRA, LANES), send_ref.dtype)
-    own = place_of(index_ref[0], peers_of(SPREAD, pieces))
+    own = place_of(index_ref[0], tp_ref[0], mesh_shape)
     lane = lax.broadcasted_iota(jnp.int32, (1, LANES), 1)
     for s in range(pieces):
         last = landed_ref[s, rows - 1 :, :LANES].astype(jnp.float32)
@@ -319,21 +321,21 @@
     if spare:
         row = jnp.concatenate([row, jnp.zeros((1, spare), jnp.float32)], axis=1)
     lines = [row[:, k * LANES : (k + 1) * LANES] for k in range(EXTRA - 2)]
-    place = place_of(target_ref[0], peers_of(DELIVER, pieces))
+    place = place_of(target_ref[0], tp_ref[0], mesh_shape)
     extra = jnp.concatenate(lines + [taken_ref[...], note_ref[...]], axis=0)
     send_ref[place, body:, :] = extra.astype(send_ref.dtype)
 
 
-def forward(leave_slot, target_rep, rep_index, landed, hidden, note, taken):
+def forward(mesh_shape, leave_slot, target_rep, tp_index, rep_index, landed, hidden, note, taken):
     pieces, rows, cols = landed.shape
     return pl.pallas_call(
-        forward_kernel,
+        functools.partial(forward_kernel, mesh_shape),
         out_shape=jax.ShapeDtypeStruct((pieces, rows * cols // LANES + EXTRA, LANES), landed.dtype),
-        in_specs=[SMEM, SMEM, SMEM, VMEM, VMEM, VMEM, VMEM],
+        in_specs=[SMEM] * 4 + [VMEM] * 4,
         out_specs=VMEM,
         compiler_params=params(),
         name="forward",
-    )(leave_slot, target_rep, rep_index, landed, hidden, note, taken)
+    )(leave_slot, target_rep, tp_index, rep_index, landed, hidden, note, taken)
 
 
 def settle_kernel(
@@ -348,16 +350,14 @@
     leave = leave_ref[0]
     extra = jnp.sum(landed_ref[:, body:, :].astype(jnp.float32), axis=0)
     taken = extra[EXTRA - 2 : EXTRA - 1, :]
-    spread, deliver = peers_of(SPREAD, pieces), peers_of(DELIVER, pieces)
     row_in = lax.broadcasted_iota(jnp.int32, (rows, LANES), 0)
     lane = lax.broadcasted_iota(jnp.int32, (rows, LANES), 1)
     writes = []
     for p in range(MAXP):
         for j in range(p * pieces // MAXP, (p + 1) * pieces // MAXP):
-            slot = deliver.index(spread[j])
             start = j * rows - p * PAGE
             for c in range(cols // LANES):
-                block = landed_ref[slot, c * rows : (c + 1) * rows, :]
+                block = landed_ref[j, c * rows : (c + 1) * rows, :]
                 if c == 0:
                     at = jnp.logical_and(row_in == rows - 1, lane == j)
                     block = jnp.where(at, taken, block.astype(jnp.float32)).astype(pages.dtype)
@@ -417,19 +417,21 @@
     expert_in,
     expert_down,
 ):
-    pieces = lax.axis_size("rep")
-    tp_size = lax.axis_size("tp")
-    tp_index = lax.axis_index("tp")
-
-    def exchange(packet, orders):
+    pieces, tp_size = mesh_shape = lax.axis_size("rep"), lax.axis_size("tp")
+    rep_index, tp_index = lax.axis_index("rep")[None], lax.axis_index("tp")[None]
+    orders = ORDERS.get(mesh_shape, (tuple(range(pieces)),) * tp_size)
+    groups = [[peer * tp_size + core for peer in peers] for core, peers in enumerate(orders)]
+
+    def exchange(packet):
         return lax.all_to_all(
-            packet, "rep", split_axis=0, concat_axis=0, tiled=True,
-            axis_index_groups=[peers_of(orders, pieces)],
+            packet, ("rep", "tp"), split_axis=0, concat_axis=0, tiled=True, axis_index_groups=groups
         )
 
-    send, taken = pack(leave_slot, target_rep, page_table, req_lengths, qkv_new, kv_pool, pieces)
+    send, taken = pack(
+        mesh_shape, leave_slot, target_rep, tp_index, page_table, req_lengths, qkv_new, kv_pool
+    )
     send, qkv_new = lax.optimization_barrier((send, qkv_new))
-    landed = exchange(send.reshape(pieces, SPAN // pieces, kv_pool.shape[2]), SPREAD)
+    landed = exchange(send.reshape(pieces, SPAN // pieces, kv_pool.shape[2]))
 
     head_part, new_pages, note = attend(
         leave_slot, page_table, req_lengths, qkv_new, kv_pool, out_proj
@@ -445,13 +447,12 @@
     def share(values, index):
         return lax.dynamic_slice_in_dim(values, index * width, width, 1)
 
-    mix = share(total, tp_index)
+    mix = share(total, tp_index[0])
     for k, shift in enumerate(shifts, 1):
-        mix = mix + lax.ppermute(share(total, (tp_index + k) % tp_size), "tp", shift)
-    hidden = (share(stream, tp_index) + mix).astype(jnp.bfloat16)
-    rep_index = lax.axis_index("rep")[None]
+        mix = mix + lax.ppermute(share(total, (tp_index[0] + k) % tp_size), "tp", shift)
+    hidden = (share(stream, tp_index[0]) + mix).astype(jnp.bfloat16)
     landed = exchange(
-        forward(leave_slot, target_rep, rep_index, landed, hidden, note, taken), DELIVER
+        forward(mesh_shape, leave_slot, target_rep, tp_index, rep_index, landed, hidden, note, taken)
     )
     return settle(leave_slot, landed, hidden, new_pages)
 

time: 45.7 us -> 44.1 us (0.965)
  blocking collectives: 18.4 us -> 17.3 us
  starting transfers between devices: 9.64 us -> 8.59 us
  waiting for transfers between devices: 5.46 us -> 6.01 us
    all_to_all x1, blocking collectives: 18.4 us -> 17.3 us  [exchange(): lax.all_to_all(packet, ('rep', 'tp'), split_axis=0, concat_axis=0, tiled=...]
    all_to_all x1, starting transfers between devices: 9.36 us -> 8.32 us  [exchange(): lax.all_to_all(packet, ('rep', 'tp'), split_axis=0, concat_axis=0, tiled=...]
    all_to_all x1, waiting for transfers between devices: 3.51 us -> 4.06 us  [exchange(): lax.all_to_all(packet, ('rep', 'tp'), split_axis=0, concat_axis=0, tiled=...]
  transfers between devices with their start and end apart: 3 -> 3, of which waited for: 3 -> 3; matrix products, arithmetic and copies ran while one was open for 0% -> 1% of each run, Pallas kernels for 9% -> 10%
where the time goes in v4:
time: 44.1 us; the launch traced here: 43.7 us
  blocking collectives  17.3 us (39%)
  starting transfers between devices  8.59 us (19%)
  Pallas kernels  7.84 us (18%)
  waiting for transfers between devices  6.01 us (14%)
  between operations  2.26 us (5%)
  local copies, waits for them, and re-layouts  1.67 us (4%)
    all_to_all x1, blocking collectives, exchange(): lax.all_to_all(packet, ('rep', 'tp'), split_axis=0, concat_axis=0, tiled=...  17.3 us
    all_to_all x1, starting transfers between devices, exchange(): lax.all_to_all(packet, ('rep', 'tp'), split_axis=0, concat_axis=0, tiled=...  8.32 us
    all_to_all x1, waiting for transfers between devices, exchange(): lax.all_to_all(packet, ('rep', 'tp'), split_axis=0, concat_axis=0, tiled=...  4.06 us
    pallas_call x1, Pallas kernels, attend(): pl.pallas_call(attend_kernel, out_shape=(jax.ShapeDtypeStruct((num_req, o...  3.57 us
    pallas_call x1, Pallas kernels, pack(): pl.pallas_call(functools.partial(pack_kernel, mesh_shape), out_shape=(plt...  2.55 us
    unnamed x22, local copies, waits for them, and re-layouts  1.66 us
    ppermute x1, waiting for transfers between devices, local(): lax.ppermute(share(total, (tp_index[0] + k) % tp_size), 'tp', shift)  1.01 us
    ppermute x1, waiting for transfers between devices, local(): lax.ppermute(head_part, 'tp', shift)  0.94 us
  transfers between devices with their start and end apart: 3, of which 3 were waited for; matrix products, arithmetic and copies ran while one was open for 1% of the time, Pallas kernels for 10%

profile of v4, /device:TPU:0, one launch (start us, length us, event | category | flops | bytes accessed | tf_op | source)
XLA Modules:
  0.0 43.7 jit_solution(9093742821549776748)
XLA Ops:
  0.6 0.0 copy-start.3
  0.6 0.0 copy-start.6
  0.7 0.0 copy-start.5
  0.7 0.0 copy-start
  2.1 2.6 %pack.1 = (bf16[4,128,512]{2,1,0:T(8,128)(2,1)}, f32[1,128]{1,0:T(1,128)S(1)}) custom-call(s32[1]{0:T(128)S(6)} %copy.20.leave_ref, s32[1]{0:T(128)S(6)} %copy.21.target_ref, s32[1]{0:T(128)} %bitcast.tp_ref.index_ref, s32[4,4]{1,0:T(4,128)} %table_ref.1, s32[4]{0:T(128)} %lens_ref.1, bf16[4,1280]{1,0:T(4,128)(2,1)} %qkv_ref, bf16[16,128,512]{2,1,0:T(8,128)(2,1)} %pool_ref.3), custom_call_target="tpu_custom_call" | custom-call | tf_op jit(solution)/shard_map/pack/pallas_call | solution.py:123
  4.7 8.3 %all-to-all-start = ((bf16[16,32,512]{2,1,0:T(8,128)(2,1)}), bf16[16,32,512]{2,1,0:T(8,128)(2,1)S(1)}, u32[]{:S(2)}, u32[]{:S(2)}) async-start(bf16[16,32,512]{2,1,0:T(8,128)(2,1)} %bitcast.3), calls=%async_computation | async-start | bytes 1048576 | tf_op jit(solution)/shard_map/all_to_all | solution.py:426
  13.0 0.0 copy-done.3
  13.0 0.0 copy-done.6
  13.0 0.0 copy-done.5
  13.0 0.0 copy-done
  13.0 0.0 copy-start.9
  13.1 0.0 copy-start.8
  13.1 0.0 copy-start.7
  13.1 0.0 copy-start.2
  13.1 0.0 copy-start.4
  13.1 3.6 %attend.1 = (f32[4,1536]{1,0:T(4,128)S(1)}, bf16[4,128,512]{2,1,0:T(8,128)(2,1)}, f32[1,128]{1,0:T(1,128)S(1)}) custom-call(s32[1]{0:T(128)S(6)} %copy.20.leave_ref, s32[4,4]{1,0:T(4,128)S(1)} %copy-done.5, s32[4]{0:T(128)S(1)} %copy-done.6, bf16[4,1280]{1,0:T(4,128)(2,1)S(1)} %copy-done.3, bf16[16,128,512]{2,1,0:T(8,128)(2,1)S(1)} %copy-done, ...), custom_call_target="tpu_custom_call" | custom-call | flops 76546048 | bytes 4456448 | tf_op jit(solution)/shard_map/attend/pallas_call | solution.py:239
  16.7 0.1 collective-permute-start
  16.8 0.0 copy-done.9
  16.8 0.1 copy.18.gates_ref
  16.9 0.0 copy-done.8
  16.9 0.1 copy.17.ids_ref
  17.0 0.0 copy-done.7
  17.0 0.9 %collective-permute-done.parts_refs_1_ = f32[4,1536]{1,0:T(4,128)S(1)} collective-permute-done((f32[4,1536]{1,0:T(4,128)S(1)}, f32[4,1536]{1,0:T(4,128)S(1)}, u32[]{:S(2)}, u32[]{:S(2)}) %collective-permute-start) | collective-permute-done | bytes 24608 | tf_op jit(solution)/shard_map/ppermute | solution.py:440
  17.9 0.0 copy-done.2
  17.9 0.0 copy-done.4
  17.9 0.0 copy-start.1
  18.0 1.4 %copy-done.1 = bf16[1,1536,512]{2,1,0:T(8,128)(2,1)S(1)} copy-done((bf16[1,1536,512]{2,1,0:T(8,128)(2,1)S(1)}, bf16[1,1536,512]{2,1,0:T(8,128)(2,1)}, u32[]{:S(2)}) %copy-start.1) | copy-done | bytes 1572888
  19.4 0.6 %experts.1 = (f32[4,1536]{1,0:T(4,128)S(1)}, f32[4,1536]{1,0:T(4,128)S(1)}) custom-call(s32[1]{0:T(128)} %bitcast.tp_ref.index_ref, s32[4,1]{1,0:T(4,128)S(1)} %copy.17.ids_ref, bf16[4,1]{1,0:T(4,128)(2,1)S(1)} %copy.18.gates_ref, bf16[4,1536]{1,0:T(4,128)(2,1)S(1)} %copy-done.4, f32[1,1536]{1,0:T(1,128)S(1)} %broadcast_in_dim.11.gain_ref, ...), custom_call_target="tpu_custom_call" | custom-call | flops 9437184 | bytes 2359296 | tf_op jit(solution)/shard_map/experts/pallas_call | solution.py:287
  19.9 0.2 collective-permute-start.1
  20.2 1.0 %collective-permute-done.1 = f32[4,768]{1,0:T(4,128)S(1)} collective-permute-done((f32[4,768]{1,0:T(4,128)S(1)}, f32[4,768]{1,0:T(4,128)S(1)}, u32[]{:S(2)}, u32[]{:S(2)}) %collective-permute-start.1) | collective-permute-done | bytes 12320 | tf_op jit(solution)/shard_map/ppermute | solution.py:452
  21.2 4.1 %all-to-all-done.landed_ref = bf16[16,32,512]{2,1,0:T(8,128)(2,1)S(1)} async-done(((bf16[16,32,512]{2,1,0:T(8,128)(2,1)}), bf16[16,32,512]{2,1,0:T(8,128)(2,1)S(1)}, u32[]{:S(2)}, u32[]{:S(2)}) %all-to-all-start) | async-done | bytes 524320 | tf_op jit(solution)/shard_map/all_to_all | solution.py:426
  25.2 0.2 forward.1
  25.5 17.3 %all_to_all.10.landed_ref = bf16[16,136,128]{2,1,0:T(8,128)(2,1)S(1)} all-to-all(bf16[16,136,128]{2,1,0:T(8,128)(2,1)S(1)} %forward.1), channel_id=1, replica_groups={{0,16,4,6,8,10,12,26,2,30,20,22,28,14,24,18},{21,19,17,23,9,31,25,1,5,7..., dimensions={0} | all-to-all | bytes 1114112 | tf_op jit(solution)/shard_map/all_to_all | solution.py:426
  42.8 0.9 %settle.1 = (bf16[4,768]{1,0:T(4,128)(2,1)}, bf16[4,128,512]{2,1,0:T(8,128)(2,1)}, bf16[4,128,512]{2,1,0:T(8,128)(2,1)}) custom-call(s32[1]{0:T(128)S(6)} %copy.20.leave_ref, bf16[16,136,128]{2,1,0:T(8,128)(2,1)S(1)} %all_to_all.10.landed_ref, bf16[4,768]{1,0:T(4,128)(2,1)S(1)} %add_convert_fusion.hidden_ref, ...), custom_call_target="tpu_custom_call", output_to_operand_aliasing={{1}: (3, {})} | custom-call | tf_op jit(solution)/shard_map/settle/pallas_call | solution.py:383
  (3 shorter events, 0.0 us)
Async XLA Ops:
  0.6 12.4 %copy-start.3 = (bf16[4,1280]{1,0:T(4,128)(2,1)S(1)}, bf16[4,1280]{1,0:T(4,128)(2,1)}, u32[]{:S(2)}) copy-start(bf16[4,1280]{1,0:T(4,128)(2,1)} %qkv_ref) | copy-start | bytes 30724
  0.6 12.4 %copy-start.6 = (s32[4]{0:T(128)S(1)}, s32[4]{0:T(128)}, u32[]{:S(2)}) copy-start(s32[4]{0:T(128)} %lens_ref.1) | copy-start | bytes 52
  0.7 12.4 %copy-start.5 = (s32[4,4]{1,0:T(4,128)S(1)}, s32[4,4]{1,0:T(4,128)}, u32[]{:S(2)}) copy-start(s32[4,4]{1,0:T(4,128)} %table_ref.1) | copy-start | bytes 196
  0.7 12.4 %copy-start = (bf16[16,128,512]{2,1,0:T(8,128)(2,1)S(1)}, bf16[16,128,512]{2,1,0:T(8,128)(2,1)}, u32[]{:S(2)}) copy-start(bf16[16,128,512]{2,1,0:T(8,128)(2,1)} %pool_ref.3) | copy-start | bytes 6291460
  4.7 20.6 %all-to-all-start = ((bf16[16,32,512]{2,1,0:T(8,128)(2,1)}), bf16[16,32,512]{2,1,0:T(8,128)(2,1)S(1)}, u32[]{:S(2)}, u32[]{:S(2)}) async-start(bf16[16,32,512]{2,1,0:T(8,128)(2,1)} %bitcast.3), calls=%async_computation | async-start | bytes 1048576 | tf_op jit(solution)/shard_map/all_to_all | solution.py:426
  13.0 3.7 %copy-start.9 = (bf16[4,1]{0,1:T(2,128)(2,1)S(1)}, bf16[4,1]{0,1:T(2,128)(2,1)}, u32[]{:S(2)}) copy-start(bf16[4,1]{0,1:T(2,128)(2,1)} %param.21) | copy-start | bytes 28
  13.1 3.8 %copy-start.8 = (s32[4,1]{0,1:T(1,128)S(1)}, s32[4,1]{0,1:T(1,128)}, u32[]{:S(2)}) copy-start(s32[4,1]{0,1:T(1,128)} %param.20) | copy-start | bytes 52
  13.1 3.9 %copy-start.7 = (f32[1536]{0:T(1024)S(1)}, f32[1536]{0:T(1024)}, u32[]{:S(2)}) copy-start(f32[1536]{0:T(1024)} %param.22) | copy-start | bytes 18436
  13.1 4.9 %copy-start.2 = (bf16[1,256,1536]{2,1,0:T(8,128)(2,1)S(1)}, bf16[1,256,1536]{2,1,0:T(8,128)(2,1)}, u32[]{:S(2)}) copy-start(bf16[1,256,1536]{2,1,0:T(8,128)(2,1)} %down_ref.1) | copy-start | bytes 2359300
  13.1 4.9 %copy-start.4 = (bf16[4,1536]{1,0:T(4,128)(2,1)S(1)}, bf16[4,1536]{1,0:T(4,128)(2,1)}, u32[]{:S(2)}) copy-start(bf16[4,1536]{1,0:T(4,128)(2,1)} %resid_ref.1) | copy-start | bytes 36868
  16.7 1.3 %collective-permute-start = (f32[4,1536]{1,0:T(4,128)S(1)}, f32[4,1536]{1,0:T(4,128)S(1)}, u32[]{:S(2)}, u32[]{:S(2)}) collective-permute-start(f32[4,1536]{1,0:T(4,128)S(1)} %get-tuple-element.15.parts_refs_0_), channel_id=1, source_target_pairs={{0,1},{1,0},{2,3},{3,2},{4,5},{5,4},{6,7},{7,6},{8,9},{9,8},{10,11... | collective-permute-start | bytes 73736 | tf_op jit(solution)/shard_map/ppermute | solution.py:440
  17.9 1.4 %copy-start.1 = (bf16[1,1536,512]{2,1,0:T(8,128)(2,1)S(1)}, bf16[1,1536,512]{2,1,0:T(8,128)(2,1)}, u32[]{:S(2)}) copy-start(bf16[1,1536,512]{2,1,0:T(8,128)(2,1)} %in_ref.1) | copy-start | bytes 4718596
  19.9 1.2 %collective-permute-start.1 = (f32[4,768]{1,0:T(4,128)S(1)}, f32[4,768]{1,0:T(4,128)S(1)}, u32[]{:S(2)}, u32[]{:S(2)}) collective-permute-start(f32[4,768]{1,0:T(4,128)S(1)} %constant_dynamic-slice_fusion), channel_id=1, source_target_pairs={{0,1},{1,0},{2,3},{3,2},{4,5},{5,4},{6,7},{7,6},{8,9},{9,8},{10,11... | collective-permute-start | bytes 36872 | tf_op jit(solution)/shard_map/ppermute | solution.py:452

commit v5 on v4

--- a/solution.py
+++ b/solution.py
@@ -19,10 +19,14 @@
 LANES = 128
 EXTRA = 8
 VMEM_BYTES = 16 * 1024 * 1024
-ORDERS = {(16, 2): (
+SPREAD = {(16, 2): (
     (0, 8, 2, 3, 4, 5, 6, 13, 1, 15, 10, 11, 14, 7, 12, 9),
     (10, 9, 8, 11, 4, 15, 12, 0, 2, 3, 1, 13, 14, 7, 6, 5),
 )}
+DELIVER = {(16, 2): (
+    (3, 8, 2, 0, 4, 5, 6, 13, 1, 15, 10, 11, 14, 7, 12, 9),
+    (10, 9, 12, 11, 4, 15, 8, 6, 2, 3, 5, 13, 14, 7, 0, 1),
+)}
 
 SMEM = pl.BlockSpec(memory_space=pltpu.SMEM)
 VMEM = pl.BlockSpec(memory_space=pltpu.VMEM)
@@ -37,9 +41,9 @@
     return pltpu.CompilerParams(vmem_limit_bytes=VMEM_BYTES)
 
 
-def place_of(replica, tp_index, mesh_shape):
+def place_of(replica, tp_index, orders):
     place = replica
-    for core, peers in enumerate(ORDERS.get(mesh_shape, ())):
+    for core, peers in enumerate(orders):
         for k, peer in enumerate(peers):
             hit = jnp.logical_and(replica == peer, tp_index == core)
             place = jnp.where(hit, k, place)
@@ -83,7 +87,7 @@
     cols = pages.shape[2]
     pieces = mesh_shape[0]
     rows = SPAN // pieces
-    ticket = place_of(target_ref[0], tp_ref[0], mesh_shape).astype(jnp.float32)
+    ticket = place_of(target_ref[0], tp_ref[0], DELIVER.get(mesh_shape, ())).astype(jnp.float32)
     smalls[1].wait()
     smalls[2].wait()
     qkv = qkv_ref[...].astype(jnp.float32)
@@ -307,7 +311,7 @@
     pieces, rows, cols = landed_ref.shape
     body = rows * cols // LANES
     send_ref[:, body:, :] = jnp.zeros((pieces, EXTRA, LANES), send_ref.dtype)
-    own = place_of(index_ref[0], tp_ref[0], mesh_shape)
+    own = place_of(index_ref[0], tp_ref[0], SPREAD.get(mesh_shape, ()))
     lane = lax.broadcasted_iota(jnp.int32, (1, LANES), 1)
     for s in range(pieces):
         last = landed_ref[s, rows - 1 :, :LANES].astype(jnp.float32)
@@ -321,7 +325,7 @@
     if spare:
         row = jnp.concatenate([row, jnp.zeros((1, spare), jnp.float32)], axis=1)
     lines = [row[:, k * LANES : (k + 1) * LANES] for k in range(EXTRA - 2)]
-    place = place_of(target_ref[0], tp_ref[0], mesh_shape)
+    place = place_of(target_ref[0], tp_ref[0], DELIVER.get(mesh_shape, ()))
     extra = jnp.concatenate(lines + [taken_ref[...], note_ref[...]], axis=0)
     send_ref[place, body:, :] = extra.astype(send_ref.dtype)
 
@@ -339,7 +343,7 @@
 
 
 def settle_kernel(
-    leave_ref, landed_ref, hidden_ref, new_in_ref, hidden_out_ref, new_ref, arrived_ref,
+    mesh_shape, leave_ref, tp_ref, landed_ref, hidden_ref, new_in_ref, hidden_out_ref, new_ref, arrived_ref,
     pages, mixed, page_sems, new_sem, hidden_sem,
 ):
     del new_in_ref
@@ -348,6 +352,7 @@
     cols = pages.shape[2]
     rows = SPAN // pieces
     leave = leave_ref[0]
+    orders = list(zip(SPREAD.get(mesh_shape, ()), DELIVER.get(mesh_shape, ())))
     extra = jnp.sum(landed_ref[:, body:, :].astype(jnp.float32), axis=0)
     taken = extra[EXTRA - 2 : EXTRA - 1, :]
     row_in = lax.broadcasted_iota(jnp.int32, (rows, LANES), 0)
@@ -356,8 +361,11 @@
     for p in range(MAXP):
         for j in range(p * pieces // MAXP, (p + 1) * pieces // MAXP):
             start = j * rows - p * PAGE
+            slot = j
+            for core, (spread, deliver) in enumerate(orders):
+                slot = jnp.where(tp_ref[0] == core, deliver.index(spread[j]), slot)
             for c in range(cols // LANES):
-                block = landed_ref[j, c * rows : (c + 1) * rows, :]
+                block = landed_ref[slot, c * rows : (c + 1) * rows, :]
                 if c == 0:
                     at = jnp.logical_and(row_in == rows - 1, lane == j)
                     block = jnp.where(at, taken, block.astype(jnp.float32)).astype(pages.dtype)
@@ -378,16 +386,16 @@
         write.wait()
 
 
-def settle(leave_slot, landed, hidden, new_pages):
+def settle(mesh_shape, leave_slot, tp_index, landed, hidden, new_pages):
     arrived = (MAXP,) + new_pages.shape[1:]
     return pl.pallas_call(
-        settle_kernel,
+        functools.partial(settle_kernel, mesh_shape),
         out_shape=(
             jax.ShapeDtypeStruct(hidden.shape, hidden.dtype),
             jax.ShapeDtypeStruct(new_pages.shape, new_pages.dtype),
             jax.ShapeDtypeStruct(arrived, new_pages.dtype),
         ),
-        in_specs=[SMEM, VMEM, VMEM, HBM],
+        in_specs=[SMEM, SMEM, VMEM, VMEM, HBM],
         out_specs=(HBM, HBM, HBM),
         scratch_shapes=[
             pltpu.VMEM(arrived, new_pages.dtype),
@@ -396,10 +404,10 @@
             pltpu.SemaphoreType.DMA,
             pltpu.SemaphoreType.DMA,
         ],
-        input_output_aliases={3: 1},
+        input_output_aliases={4: 1},
         compiler_params=params(),
         name="settle",
-    )(leave_slot, landed, hidden, new_pages)
+    )(leave_slot, tp_index, landed, hidden, new_pages)
 
 
 def local(
@@ -419,10 +427,10 @@
 ):
     pieces, tp_size = mesh_shape = lax.axis_size("rep"), lax.axis_size("tp")
     rep_index, tp_index = lax.axis_index("rep")[None], lax.axis_index("tp")[None]
-    orders = ORDERS.get(mesh_shape, (tuple(range(pieces)),) * tp_size)
-    groups = [[peer * tp_size + core for peer in peers] for core, peers in enumerate(orders)]
-
-    def exchange(packet):
+
+    def exchange(packet, orders):
+        orders = orders.get(mesh_shape, (tuple(range(pieces)),) * tp_size)
+        groups = [[peer * tp_size + core for peer in peers] for core, peers in enumerate(orders)]
         return lax.all_to_all(
             packet, ("rep", "tp"), split_axis=0, concat_axis=0, tiled=True, axis_index_groups=groups
         )
@@ -431,7 +439,7 @@
         mesh_shape, leave_slot, target_rep, tp_index, page_table, req_lengths, qkv_new, kv_pool
     )
     send, qkv_new = lax.optimization_barrier((send, qkv_new))
-    landed = exchange(send.reshape(pieces, SPAN // pieces, kv_pool.shape[2]))
+    landed = exchange(send.reshape(pieces, SPAN // pieces, kv_pool.shape[2]), SPREAD)
 
     head_part, new_pages, note = attend(
         leave_slot, page_table, req_lengths, qkv_new, kv_pool, out_proj
@@ -452,9 +460,10 @@
         mix = mix + lax.ppermute(share(total, (tp_index[0] + k) % tp_size), "tp", shift)
     hidden = (share(stream, tp_index[0]) + mix).astype(jnp.bfloat16)
     landed = exchange(
-        forward(mesh_shape, leave_slot, target_rep, tp_index, rep_index, landed, hidden, note, taken)
-    )
-    return settle(leave_slot, landed, hidden, new_pages)
+        forward(mesh_shape, leave_slot, target_rep, tp_index, rep_index, landed, hidden, note, taken),
+        DELIVER,
+    )
+    return settle(mesh_shape, leave_slot, tp_index, landed, hidden, new_pages)
 
 
 def solution(mesh):

time: 44.1 us -> 44.1 us (level)
  no operation moved by 1% of the time
where the time goes in v5:
time: 44.1 us; the launch traced here: 43.6 us
  blocking collectives  17.2 us (39%)
  starting transfers between devices  8.6 us (20%)
  Pallas kernels  7.84 us (18%)
  waiting for transfers between devices  6.01 us (14%)
  between operations  2.26 us (5%)
  local copies, waits for them, and re-layouts  1.67 us (4%)
    all_to_all x1, blocking collectives, exchange(): lax.all_to_all(packet, ('rep', 'tp'), split_axis=0, concat_axis=0, tiled=...  17.2 us
    all_to_all x1, starting transfers between devices, exchange(): lax.all_to_all(packet, ('rep', 'tp'), split_axis=0, concat_axis=0, tiled=...  8.32 us
    all_to_all x1, waiting for transfers between devices, exchange(): lax.all_to_all(packet, ('rep', 'tp'), split_axis=0, concat_axis=0, tiled=...  4.06 us
    pallas_call x1, Pallas kernels, attend(): pl.pallas_call(attend_kernel, out_shape=(jax.ShapeDtypeStruct((num_req, o...  3.57 us
    pallas_call x1, Pallas kernels, pack(): pl.pallas_call(functools.partial(pack_kernel, mesh_shape), out_shape=(plt...  2.55 us
    unnamed x22, local copies, waits for them, and re-layouts  1.66 us
    ppermute x1, waiting for transfers between devices, local(): lax.ppermute(share(total, (tp_index[0] + k) % tp_size), 'tp', shift)  1.01 us
    ppermute x1, waiting for transfers between devices, local(): lax.ppermute(head_part, 'tp', shift)  0.94 us
  transfers between devices with their start and end apart: 3, of which 3 were waited for; matrix products, arithmetic and copies ran while one was open for 1% of the time, Pallas kernels for 10%

profile of v5, /device:TPU:0, one launch (start us, length us, event | category | flops | bytes accessed | tf_op | source)
XLA Modules:
  0.0 43.6 jit_solution(9359512396781222944)
XLA Ops:
  0.6 0.0 copy-start.3
  0.6 0.0 copy-start.6
  0.7 0.0 copy-start.5
  0.7 0.0 copy-start
  2.1 2.5 %pack.1 = (bf16[4,128,512]{2,1,0:T(8,128)(2,1)}, f32[1,128]{1,0:T(1,128)S(1)}) custom-call(s32[1]{0:T(128)S(6)} %copy.20.leave_ref, s32[1]{0:T(128)S(6)} %copy.21.target_ref, s32[1]{0:T(128)} %bitcast.tp_ref.index_ref, s32[4,4]{1,0:T(4,128)} %table_ref.1, s32[4]{0:T(128)} %lens_ref.1, bf16[4,1280]{1,0:T(4,128)(2,1)} %qkv_ref, bf16[16,128,512]{2,1,0:T(8,128)(2,1)} %pool_ref.3), custom_call_target="tpu_custom_call" | custom-call | tf_op jit(solution)/shard_map/pack/pallas_call | solution.py:127
  4.7 8.3 %all-to-all-start = ((bf16[16,32,512]{2,1,0:T(8,128)(2,1)}), bf16[16,32,512]{2,1,0:T(8,128)(2,1)S(1)}, u32[]{:S(2)}, u32[]{:S(2)}) async-start(bf16[16,32,512]{2,1,0:T(8,128)(2,1)} %bitcast.3), calls=%async_computation | async-start | bytes 1048576 | tf_op jit(solution)/shard_map/all_to_all | solution.py:434
  13.0 0.0 copy-done.3
  13.0 0.0 copy-done.6
  13.0 0.0 copy-done.5
  13.0 0.0 copy-done
  13.0 0.0 copy-start.9
  13.1 0.0 copy-start.8
  13.1 0.0 copy-start.7
  13.1 0.0 copy-start.2
  13.1 0.0 copy-start.4
  13.1 3.6 %attend.1 = (f32[4,1536]{1,0:T(4,128)S(1)}, bf16[4,128,512]{2,1,0:T(8,128)(2,1)}, f32[1,128]{1,0:T(1,128)S(1)}) custom-call(s32[1]{0:T(128)S(6)} %copy.20.leave_ref, s32[4,4]{1,0:T(4,128)S(1)} %copy-done.5, s32[4]{0:T(128)S(1)} %copy-done.6, bf16[4,1280]{1,0:T(4,128)(2,1)S(1)} %copy-done.3, bf16[16,128,512]{2,1,0:T(8,128)(2,1)S(1)} %copy-done, ...), custom_call_target="tpu_custom_call" | custom-call | flops 76546048 | bytes 4456448 | tf_op jit(solution)/shard_map/attend/pallas_call | solution.py:243
  16.7 0.1 collective-permute-start
  16.8 0.0 copy-done.9
  16.8 0.1 copy.18.gates_ref
  16.9 0.0 copy-done.8
  16.9 0.1 copy.17.ids_ref
  17.0 0.0 copy-done.7
  17.0 0.9 %collective-permute-done.parts_refs_1_ = f32[4,1536]{1,0:T(4,128)S(1)} collective-permute-done((f32[4,1536]{1,0:T(4,128)S(1)}, f32[4,1536]{1,0:T(4,128)S(1)}, u32[]{:S(2)}, u32[]{:S(2)}) %collective-permute-start) | collective-permute-done | bytes 24608 | tf_op jit(solution)/shard_map/ppermute | solution.py:448
  17.9 0.0 copy-done.2
  17.9 0.0 copy-done.4
  17.9 0.0 copy-start.1
  18.0 1.4 %copy-done.1 = bf16[1,1536,512]{2,1,0:T(8,128)(2,1)S(1)} copy-done((bf16[1,1536,512]{2,1,0:T(8,128)(2,1)S(1)}, bf16[1,1536,512]{2,1,0:T(8,128)(2,1)}, u32[]{:S(2)}) %copy-start.1) | copy-done | bytes 1572888
  19.4 0.6 %experts.1 = (f32[4,1536]{1,0:T(4,128)S(1)}, f32[4,1536]{1,0:T(4,128)S(1)}) custom-call(s32[1]{0:T(128)} %bitcast.tp_ref.index_ref, s32[4,1]{1,0:T(4,128)S(1)} %copy.17.ids_ref, bf16[4,1]{1,0:T(4,128)(2,1)S(1)} %copy.18.gates_ref, bf16[4,1536]{1,0:T(4,128)(2,1)S(1)} %copy-done.4, f32[1,1536]{1,0:T(1,128)S(1)} %broadcast_in_dim.11.gain_ref, ...), custom_call_target="tpu_custom_call" | custom-call | flops 9437184 | bytes 2359296 | tf_op jit(solution)/shard_map/experts/pallas_call | solution.py:291
  19.9 0.2 collective-permute-start.1
  20.2 1.0 %collective-permute-done.1 = f32[4,768]{1,0:T(4,128)S(1)} collective-permute-done((f32[4,768]{1,0:T(4,128)S(1)}, f32[4,768]{1,0:T(4,128)S(1)}, u32[]{:S(2)}, u32[]{:S(2)}) %collective-permute-start.1) | collective-permute-done | bytes 12320 | tf_op jit(solution)/shard_map/ppermute | solution.py:460
  21.2 4.1 %all-to-all-done.landed_ref = bf16[16,32,512]{2,1,0:T(8,128)(2,1)S(1)} async-done(((bf16[16,32,512]{2,1,0:T(8,128)(2,1)}), bf16[16,32,512]{2,1,0:T(8,128)(2,1)S(1)}, u32[]{:S(2)}, u32[]{:S(2)}) %all-to-all-start) | async-done | bytes 524320 | tf_op jit(solution)/shard_map/all_to_all | solution.py:434
  25.2 0.2 forward.1
  25.5 17.2 %all_to_all.10.landed_ref = bf16[16,136,128]{2,1,0:T(8,128)(2,1)S(1)} all-to-all(bf16[16,136,128]{2,1,0:T(8,128)(2,1)S(1)} %forward.1), channel_id=1, replica_groups={{6,16,4,0,8,10,12,26,2,30,20,22,28,14,24,18},{21,19,25,23,9,31,17,13,5,..., dimensions={0} | all-to-all | bytes 1114112 | tf_op jit(solution)/shard_map/all_to_all | solution.py:434
  42.7 0.9 %settle.1 = (bf16[4,768]{1,0:T(4,128)(2,1)}, bf16[4,128,512]{2,1,0:T(8,128)(2,1)}, bf16[4,128,512]{2,1,0:T(8,128)(2,1)}) custom-call(s32[1]{0:T(128)S(6)} %copy.20.leave_ref, s32[1]{0:T(128)} %bitcast.tp_ref.index_ref, bf16[16,136,128]{2,1,0:T(8,128)(2,1)S(1)} %all_to_all.10.landed_ref, ...), custom_call_target="tpu_custom_call", output_to_operand_aliasing={{1}: (4, {})} | custom-call | tf_op jit(solution)/shard_map/settle/pallas_call | solution.py:391
  (3 shorter events, 0.0 us)
Async XLA Ops:
  0.6 12.4 %copy-start.3 = (bf16[4,1280]{1,0:T(4,128)(2,1)S(1)}, bf16[4,1280]{1,0:T(4,128)(2,1)}, u32[]{:S(2)}) copy-start(bf16[4,1280]{1,0:T(4,128)(2,1)} %qkv_ref) | copy-start | bytes 30724
  0.6 12.4 %copy-start.6 = (s32[4]{0:T(128)S(1)}, s32[4]{0:T(128)}, u32[]{:S(2)}) copy-start(s32[4]{0:T(128)} %lens_ref.1) | copy-start | bytes 52
  0.7 12.4 %copy-start.5 = (s32[4,4]{1,0:T(4,128)S(1)}, s32[4,4]{1,0:T(4,128)}, u32[]{:S(2)}) copy-start(s32[4,4]{1,0:T(4,128)} %table_ref.1) | copy-start | bytes 196
  0.7 12.4 %copy-start = (bf16[16,128,512]{2,1,0:T(8,128)(2,1)S(1)}, bf16[16,128,512]{2,1,0:T(8,128)(2,1)}, u32[]{:S(2)}) copy-start(bf16[16,128,512]{2,1,0:T(8,128)(2,1)} %pool_ref.3) | copy-start | bytes 6291460
  4.7 20.6 %all-to-all-start = ((bf16[16,32,512]{2,1,0:T(8,128)(2,1)}), bf16[16,32,512]{2,1,0:T(8,128)(2,1)S(1)}, u32[]{:S(2)}, u32[]{:S(2)}) async-start(bf16[16,32,512]{2,1,0:T(8,128)(2,1)} %bitcast.3), calls=%async_computation | async-start | bytes 1048576 | tf_op jit(solution)/shard_map/all_to_all | solution.py:434
  13.0 3.7 %copy-start.9 = (bf16[4,1]{0,1:T(2,128)(2,1)S(1)}, bf16[4,1]{0,1:T(2,128)(2,1)}, u32[]{:S(2)}) copy-start(bf16[4,1]{0,1:T(2,128)(2,1)} %param.21) | copy-start | bytes 28
  13.1 3.8 %copy-start.8 = (s32[4,1]{0,1:T(1,128)S(1)}, s32[4,1]{0,1:T(1,128)}, u32[]{:S(2)}) copy-start(s32[4,1]{0,1:T(1,128)} %param.20) | copy-start | bytes 52
  13.1 3.9 %copy-start.7 = (f32[1536]{0:T(1024)S(1)}, f32[1536]{0:T(1024)}, u32[]{:S(2)}) copy-start(f32[1536]{0:T(1024)} %param.22) | copy-start | bytes 18436
  13.1 4.9 %copy-start.2 = (bf16[1,256,1536]{2,1,0:T(8,128)(2,1)S(1)}, bf16[1,256,1536]{2,1,0:T(8,128)(2,1)}, u32[]{:S(2)}) copy-start(bf16[1,256,1536]{2,1,0:T(8,128)(2,1)} %down_ref.1) | copy-start | bytes 2359300
  13.1 4.9 %copy-start.4 = (bf16[4,1536]{1,0:T(4,128)(2,1)S(1)}, bf16[4,1536]{1,0:T(4,128)(2,1)}, u32[]{:S(2)}) copy-start(bf16[4,1536]{1,0:T(4,128)(2,1)} %resid_ref.1) | copy-start | bytes 36868
  16.7 1.3 %collective-permute-start = (f32[4,1536]{1,0:T(4,128)S(1)}, f32[4,1536]{1,0:T(4,128)S(1)}, u32[]{:S(2)}, u32[]{:S(2)}) collective-permute-start(f32[4,1536]{1,0:T(4,128)S(1)} %get-tuple-element.15.parts_refs_0_), channel_id=1, source_target_pairs={{0,1},{1,0},{2,3},{3,2},{4,5},{5,4},{6,7},{7,6},{8,9},{9,8},{10,11... | collective-permute-start | bytes 73736 | tf_op jit(solution)/shard_map/ppermute | solution.py:448
  17.9 1.4 %copy-start.1 = (bf16[1,1536,512]{2,1,0:T(8,128)(2,1)S(1)}, bf16[1,1536,512]{2,1,0:T(8,128)(2,1)}, u32[]{:S(2)}) copy-start(bf16[1,1536,512]{2,1,0:T(8,128)(2,1)} %in_ref.1) | copy-start | bytes 4718596
  19.9 1.2 %collective-permute-start.1 = (f32[4,768]{1,0:T(4,128)S(1)}, f32[4,768]{1,0:T(4,128)S(1)}, u32[]{:S(2)}, u32[]{:S(2)}) collective-permute-start(f32[4,768]{1,0:T(4,128)S(1)} %constant_dynamic-slice_fusion), channel_id=1, source_target_pairs={{0,1},{1,0},{2,3},{3,2},{4,5},{5,4},{6,7},{7,6},{8,9},{9,8},{10,11... | collective-permute-start | bytes 36872 | tf_op jit(solution)/shard_map/ppermute | solution.py:460

commit v6 on v5

--- a/solution.py
+++ b/solution.py
@@ -438,7 +438,7 @@
     send, taken = pack(
         mesh_shape, leave_slot, target_rep, tp_index, page_table, req_lengths, qkv_new, kv_pool
     )
-    send, qkv_new = lax.optimization_barrier((send, qkv_new))
+    send, qkv_new, kv_pool = lax.optimization_barrier((send, qkv_new, kv_pool))
     landed = exchange(send.reshape(pieces, SPAN // pieces, kv_pool.shape[2]), SPREAD)
 
     head_part, new_pages, note = attend(

time: 44.1 us -> 44 us (level)
  no operation moved by 1% of the time
where the time goes in v6:
time: 44 us; the launch traced here: 43.6 us
  blocking collectives  17.2 us (39%)
  starting transfers between devices  8.6 us (20%)
  Pallas kernels  7.84 us (18%)
  waiting for transfers between devices  6.01 us (14%)
  between operations  2.26 us (5%)
  local copies, waits for them, and re-layouts  1.67 us (4%)
    all_to_all x1, blocking collectives, exchange(): lax.all_to_all(packet, ('rep', 'tp'), split_axis=0, concat_axis=0, tiled=...  17.2 us
    all_to_all x1, starting transfers between devices, exchange(): lax.all_to_all(packet, ('rep', 'tp'), split_axis=0, concat_axis=0, tiled=...  8.32 us
    all_to_all x1, waiting for transfers between devices, exchange(): lax.all_to_all(packet, ('rep', 'tp'), split_axis=0, concat_axis=0, tiled=...  4.06 us
    pallas_call x1, Pallas kernels, attend(): pl.pallas_call(attend_kernel, out_shape=(jax.ShapeDtypeStruct((num_req, o...  3.57 us
    pallas_call x1, Pallas kernels, pack(): pl.pallas_call(functools.partial(pack_kernel, mesh_shape), out_shape=(plt...  2.55 us
    unnamed x22, local copies, waits for them, and re-layouts  1.66 us
    ppermute x1, waiting for transfers between devices, local(): lax.ppermute(share(total, (tp_index[0] + k) % tp_size), 'tp', shift)  1.01 us
    ppermute x1, waiting for transfers between devices, local(): lax.ppermute(head_part, 'tp', shift)  0.94 us
  transfers between devices with their start and end apart: 3, of which 3 were waited for; matrix products, arithmetic and copies ran while one was open for 1% of the time, Pallas kernels for 10%

profile of v6, /device:TPU:0, one launch (start us, length us, event | category | flops | bytes accessed | tf_op | source)
XLA Modules:
  0.0 43.6 jit_solution(9359512396781222944)
XLA Ops:
  0.6 0.0 copy-start.3
  0.6 0.0 copy-start.6
  0.7 0.0 copy-start.5
  0.7 0.0 copy-start
  2.1 2.5 %pack.1 = (bf16[4,128,512]{2,1,0:T(8,128)(2,1)}, f32[1,128]{1,0:T(1,128)S(1)}) custom-call(s32[1]{0:T(128)S(6)} %copy.20.leave_ref, s32[1]{0:T(128)S(6)} %copy.21.target_ref, s32[1]{0:T(128)} %bitcast.tp_ref.index_ref, s32[4,4]{1,0:T(4,128)} %table_ref.1, s32[4]{0:T(128)} %lens_ref.1, bf16[4,1280]{1,0:T(4,128)(2,1)} %qkv_ref, bf16[16,128,512]{2,1,0:T(8,128)(2,1)} %pool_ref.2), custom_call_target="tpu_custom_call" | custom-call | tf_op jit(solution)/shard_map/pack/pallas_call | solution.py:127
  4.7 8.3 %all-to-all-start = ((bf16[16,32,512]{2,1,0:T(8,128)(2,1)}), bf16[16,32,512]{2,1,0:T(8,128)(2,1)S(1)}, u32[]{:S(2)}, u32[]{:S(2)}) async-start(bf16[16,32,512]{2,1,0:T(8,128)(2,1)} %bitcast.3), calls=%async_computation | async-start | bytes 1048576 | tf_op jit(solution)/shard_map/all_to_all | solution.py:434
  13.0 0.0 copy-done.3
  13.0 0.0 copy-done.6
  13.0 0.0 copy-done.5
  13.0 0.0 copy-done
  13.0 0.0 copy-start.9
  13.1 0.0 copy-start.8
  13.1 0.0 copy-start.7
  13.1 0.0 copy-start.2
  13.1 0.0 copy-start.4
  13.1 3.6 %attend.1 = (f32[4,1536]{1,0:T(4,128)S(1)}, bf16[4,128,512]{2,1,0:T(8,128)(2,1)}, f32[1,128]{1,0:T(1,128)S(1)}) custom-call(s32[1]{0:T(128)S(6)} %copy.20.leave_ref, s32[4,4]{1,0:T(4,128)S(1)} %copy-done.5, s32[4]{0:T(128)S(1)} %copy-done.6, bf16[4,1280]{1,0:T(4,128)(2,1)S(1)} %copy-done.3, bf16[16,128,512]{2,1,0:T(8,128)(2,1)S(1)} %copy-done, ...), custom_call_target="tpu_custom_call" | custom-call | flops 76546048 | bytes 4456448 | tf_op jit(solution)/shard_map/attend/pallas_call | solution.py:243
  16.7 0.1 collective-permute-start
  16.8 0.0 copy-done.9
  16.8 0.1 copy.18.gates_ref
  16.9 0.0 copy-done.8
  16.9 0.1 copy.17.ids_ref
  17.0 0.0 copy-done.7
  17.0 0.9 %collective-permute-done.parts_refs_1_ = f32[4,1536]{1,0:T(4,128)S(1)} collective-permute-done((f32[4,1536]{1,0:T(4,128)S(1)}, f32[4,1536]{1,0:T(4,128)S(1)}, u32[]{:S(2)}, u32[]{:S(2)}) %collective-permute-start) | collective-permute-done | bytes 24608 | tf_op jit(solution)/shard_map/ppermute | solution.py:448
  17.9 0.0 copy-done.2
  17.9 0.0 copy-done.4
  17.9 0.0 copy-start.1
  18.0 1.4 %copy-done.1 = bf16[1,1536,512]{2,1,0:T(8,128)(2,1)S(1)} copy-done((bf16[1,1536,512]{2,1,0:T(8,128)(2,1)S(1)}, bf16[1,1536,512]{2,1,0:T(8,128)(2,1)}, u32[]{:S(2)}) %copy-start.1) | copy-done | bytes 1572888
  19.4 0.6 %experts.1 = (f32[4,1536]{1,0:T(4,128)S(1)}, f32[4,1536]{1,0:T(4,128)S(1)}) custom-call(s32[1]{0:T(128)} %bitcast.tp_ref.index_ref, s32[4,1]{1,0:T(4,128)S(1)} %copy.17.ids_ref, bf16[4,1]{1,0:T(4,128)(2,1)S(1)} %copy.18.gates_ref, bf16[4,1536]{1,0:T(4,128)(2,1)S(1)} %copy-done.4, f32[1,1536]{1,0:T(1,128)S(1)} %broadcast_in_dim.11.gain_ref, ...), custom_call_target="tpu_custom_call" | custom-call | flops 9437184 | bytes 2359296 | tf_op jit(solution)/shard_map/experts/pallas_call | solution.py:291
  19.9 0.2 collective-permute-start.1
  20.2 1.0 %collective-permute-done.1 = f32[4,768]{1,0:T(4,128)S(1)} collective-permute-done((f32[4,768]{1,0:T(4,128)S(1)}, f32[4,768]{1,0:T(4,128)S(1)}, u32[]{:S(2)}, u32[]{:S(2)}) %collective-permute-start.1) | collective-permute-done | bytes 12320 | tf_op jit(solution)/shard_map/ppermute | solution.py:460
  21.2 4.1 %all-to-all-done.landed_ref = bf16[16,32,512]{2,1,0:T(8,128)(2,1)S(1)} async-done(((bf16[16,32,512]{2,1,0:T(8,128)(2,1)}), bf16[16,32,512]{2,1,0:T(8,128)(2,1)S(1)}, u32[]{:S(2)}, u32[]{:S(2)}) %all-to-all-start) | async-done | bytes 524320 | tf_op jit(solution)/shard_map/all_to_all | solution.py:434
  25.2 0.2 forward.1
  25.5 17.2 %all_to_all.10.landed_ref = bf16[16,136,128]{2,1,0:T(8,128)(2,1)S(1)} all-to-all(bf16[16,136,128]{2,1,0:T(8,128)(2,1)S(1)} %forward.1), channel_id=1, replica_groups={{6,16,4,0,8,10,12,26,2,30,20,22,28,14,24,18},{21,19,25,23,9,31,17,13,5,..., dimensions={0} | all-to-all | bytes 1114112 | tf_op jit(solution)/shard_map/all_to_all | solution.py:434
  42.7 0.9 %settle.1 = (bf16[4,768]{1,0:T(4,128)(2,1)}, bf16[4,128,512]{2,1,0:T(8,128)(2,1)}, bf16[4,128,512]{2,1,0:T(8,128)(2,1)}) custom-call(s32[1]{0:T(128)S(6)} %copy.20.leave_ref, s32[1]{0:T(128)} %bitcast.tp_ref.index_ref, bf16[16,136,128]{2,1,0:T(8,128)(2,1)S(1)} %all_to_all.10.landed_ref, ...), custom_call_target="tpu_custom_call", output_to_operand_aliasing={{1}: (4, {})} | custom-call | tf_op jit(solution)/shard_map/settle/pallas_call | solution.py:391
  (3 shorter events, 0.0 us)
Async XLA Ops:
  0.6 12.4 %copy-start.3 = (bf16[4,1280]{1,0:T(4,128)(2,1)S(1)}, bf16[4,1280]{1,0:T(4,128)(2,1)}, u32[]{:S(2)}) copy-start(bf16[4,1280]{1,0:T(4,128)(2,1)} %qkv_ref) | copy-start | bytes 30724
  0.6 12.4 %copy-start.6 = (s32[4]{0:T(128)S(1)}, s32[4]{0:T(128)}, u32[]{:S(2)}) copy-start(s32[4]{0:T(128)} %lens_ref.1) | copy-start | bytes 52
  0.7 12.4 %copy-start.5 = (s32[4,4]{1,0:T(4,128)S(1)}, s32[4,4]{1,0:T(4,128)}, u32[]{:S(2)}) copy-start(s32[4,4]{1,0:T(4,128)} %table_ref.1) | copy-start | bytes 196
  0.7 12.4 %copy-start = (bf16[16,128,512]{2,1,0:T(8,128)(2,1)S(1)}, bf16[16,128,512]{2,1,0:T(8,128)(2,1)}, u32[]{:S(2)}) copy-start(bf16[16,128,512]{2,1,0:T(8,128)(2,1)} %pool_ref.2) | copy-start | bytes 6291460
  4.7 20.6 %all-to-all-start = ((bf16[16,32,512]{2,1,0:T(8,128)(2,1)}), bf16[16,32,512]{2,1,0:T(8,128)(2,1)S(1)}, u32[]{:S(2)}, u32[]{:S(2)}) async-start(bf16[16,32,512]{2,1,0:T(8,128)(2,1)} %bitcast.3), calls=%async_computation | async-start | bytes 1048576 | tf_op jit(solution)/shard_map/all_to_all | solution.py:434
  13.0 3.7 %copy-start.9 = (bf16[4,1]{0,1:T(2,128)(2,1)S(1)}, bf16[4,1]{0,1:T(2,128)(2,1)}, u32[]{:S(2)}) copy-start(bf16[4,1]{0,1:T(2,128)(2,1)} %param.21) | copy-start | bytes 28
  13.1 3.8 %copy-start.8 = (s32[4,1]{0,1:T(1,128)S(1)}, s32[4,1]{0,1:T(1,128)}, u32[]{:S(2)}) copy-start(s32[4,1]{0,1:T(1,128)} %param.20) | copy-start | bytes 52
  13.1 3.9 %copy-start.7 = (f32[1536]{0:T(1024)S(1)}, f32[1536]{0:T(1024)}, u32[]{:S(2)}) copy-start(f32[1536]{0:T(1024)} %param.22) | copy-start | bytes 18436
  13.1 4.9 %copy-start.2 = (bf16[1,256,1536]{2,1,0:T(8,128)(2,1)S(1)}, bf16[1,256,1536]{2,1,0:T(8,128)(2,1)}, u32[]{:S(2)}) copy-start(bf16[1,256,1536]{2,1,0:T(8,128)(2,1)} %down_ref.1) | copy-start | bytes 2359300
  13.1 4.9 %copy-start.4 = (bf16[4,1536]{1,0:T(4,128)(2,1)S(1)}, bf16[4,1536]{1,0:T(4,128)(2,1)}, u32[]{:S(2)}) copy-start(bf16[4,1536]{1,0:T(4,128)(2,1)} %resid_ref.1) | copy-start | bytes 36868
  16.7 1.3 %collective-permute-start = (f32[4,1536]{1,0:T(4,128)S(1)}, f32[4,1536]{1,0:T(4,128)S(1)}, u32[]{:S(2)}, u32[]{:S(2)}) collective-permute-start(f32[4,1536]{1,0:T(4,128)S(1)} %get-tuple-element.17.parts_refs_0_), channel_id=1, source_target_pairs={{0,1},{1,0},{2,3},{3,2},{4,5},{5,4},{6,7},{7,6},{8,9},{9,8},{10,11... | collective-permute-start | bytes 73736 | tf_op jit(solution)/shard_map/ppermute | solution.py:448
  17.9 1.4 %copy-start.1 = (bf16[1,1536,512]{2,1,0:T(8,128)(2,1)S(1)}, bf16[1,1536,512]{2,1,0:T(8,128)(2,1)}, u32[]{:S(2)}) copy-start(bf16[1,1536,512]{2,1,0:T(8,128)(2,1)} %in_ref.1) | copy-start | bytes 4718596
  19.9 1.2 %collective-permute-start.1 = (f32[4,768]{1,0:T(4,128)S(1)}, f32[4,768]{1,0:T(4,128)S(1)}, u32[]{:S(2)}, u32[]{:S(2)}) collective-permute-start(f32[4,768]{1,0:T(4,128)S(1)} %constant_dynamic-slice_fusion), channel_id=1, source_target_pairs={{0,1},{1,0},{2,3},{3,2},{4,5},{5,4},{6,7},{7,6},{8,9},{9,8},{10,11... | collective-permute-start | bytes 36872 | tf_op jit(solution)/shard_map/ppermute | solution.py:460

commit v7 on v6

--- a/solution.py
+++ b/solution.py
@@ -17,6 +17,7 @@
 GROUP = QH // KVH
 SPAN = MAXP * PAGE
 LANES = 128
+HALF = PAGE // 2
 EXTRA = 8
 VMEM_BYTES = 16 * 1024 * 1024
 SPREAD = {(16, 2): (
@@ -370,8 +371,14 @@
                     at = jnp.logical_and(row_in == rows - 1, lane == j)
                     block = jnp.where(at, taken, block.astype(jnp.float32)).astype(pages.dtype)
                 pages[p, start : start + rows, c * LANES : (c + 1) * LANES] = block
-        writes.append(pltpu.make_async_copy(pages.at[p], arrived_ref.at[p], page_sems.at[p]))
-        writes[p].start()
+            if (start + rows) % HALF == 0:
+                span = pl.ds(start + rows - HALF, HALF)
+                writes.append(
+                    pltpu.make_async_copy(
+                        pages.at[p, span], arrived_ref.at[p, span], page_sems.at[len(writes)]
+                    )
+                )
+                writes[-1].start()
     page = jnp.max(extra[EXTRA - 1 :, :]).astype(jnp.int32)
     writes.append(pltpu.make_async_copy(pages.at[page], new_ref.at[leave], new_sem))
     writes[-1].start()
@@ -400,7 +407,7 @@
         scratch_shapes=[
             pltpu.VMEM(arrived, new_pages.dtype),
             pltpu.VMEM(hidden.shape, hidden.dtype),
-            pltpu.SemaphoreType.DMA((MAXP,)),
+            pltpu.SemaphoreType.DMA((SPAN // HALF,)),
             pltpu.SemaphoreType.DMA,
             pltpu.SemaphoreType.DMA,
         ],

time: 44 us -> 44.1 us (level)
  no operation moved by 1% of the time
where the time goes in v7:
time: 44.1 us; the launch traced here: 43.7 us
  blocking collectives  17.2 us (39%)
  starting transfers between devices  8.6 us (20%)
  Pallas kernels  7.87 us (18%)
  waiting for transfers between devices  6.01 us (14%)
  between operations  2.26 us (5%)
  local copies, waits for them, and re-layouts  1.67 us (4%)
    all_to_all x1, blocking collectives, exchange(): lax.all_to_all(packet, ('rep', 'tp'), split_axis=0, concat_axis=0, tiled=...  17.2 us
    all_to_all x1, starting transfers between devices, exchange(): lax.all_to_all(packet, ('rep', 'tp'), split_axis=0, concat_axis=0, tiled=...  8.32 us
    all_to_all x1, waiting for transfers between devices, exchange(): lax.all_to_all(packet, ('rep', 'tp'), split_axis=0, concat_axis=0, tiled=...  4.06 us
    pallas_call x1, Pallas kernels, attend(): pl.pallas_call(attend_kernel, out_shape=(jax.ShapeDtypeStruct((num_req, o...  3.57 us
    pallas_call x1, Pallas kernels, pack(): pl.pallas_call(functools.partial(pack_kernel, mesh_shape), out_shape=(plt...  2.55 us
    unnamed x22, local copies, waits for them, and re-layouts  1.66 us
    ppermute x1, waiting for transfers between devices, local(): lax.ppermute(share(total, (tp_index[0] + k) % tp_size), 'tp', shift)  1.01 us
    pallas_call x1, Pallas kernels, settle(): pl.pallas_call(functools.partial(settle_kernel, mesh_shape), out_shape=(j...  0.95 us
  transfers between devices with their start and end apart: 3, of which 3 were waited for; matrix products, arithmetic and copies ran while one was open for 1% of the time, Pallas kernels for 10%

profile of v7, /device:TPU:0, one launch (start us, length us, event | category | flops | bytes accessed | tf_op | source)
XLA Modules:
  0.0 43.7 jit_solution(14012807613056593264)
XLA Ops:
  0.6 0.0 copy-start.3
  0.6 0.0 copy-start.6
  0.7 0.0 copy-start.5
  0.7 0.0 copy-start
  2.1 2.5 %pack.1 = (bf16[4,128,512]{2,1,0:T(8,128)(2,1)}, f32[1,128]{1,0:T(1,128)S(1)}) custom-call(s32[1]{0:T(128)S(6)} %copy.20.leave_ref, s32[1]{0:T(128)S(6)} %copy.21.target_ref, s32[1]{0:T(128)} %bitcast.tp_ref.index_ref, s32[4,4]{1,0:T(4,128)} %table_ref.1, s32[4]{0:T(128)} %lens_ref.1, bf16[4,1280]{1,0:T(4,128)(2,1)} %qkv_ref, bf16[16,128,512]{2,1,0:T(8,128)(2,1)} %pool_ref.2), custom_call_target="tpu_custom_call" | custom-call | tf_op jit(solution)/shard_map/pack/pallas_call | solution.py:128
  4.7 8.3 %all-to-all-start = ((bf16[16,32,512]{2,1,0:T(8,128)(2,1)}), bf16[16,32,512]{2,1,0:T(8,128)(2,1)S(1)}, u32[]{:S(2)}, u32[]{:S(2)}) async-start(bf16[16,32,512]{2,1,0:T(8,128)(2,1)} %bitcast.3), calls=%async_computation | async-start | bytes 1048576 | tf_op jit(solution)/shard_map/all_to_all | solution.py:441
  13.0 0.0 copy-done.3
  13.0 0.0 copy-done.6
  13.0 0.0 copy-done.5
  13.0 0.0 copy-done
  13.0 0.0 copy-start.9
  13.1 0.0 copy-start.8
  13.1 0.0 copy-start.7
  13.1 0.0 copy-start.2
  13.1 0.0 copy-start.4
  13.1 3.6 %attend.1 = (f32[4,1536]{1,0:T(4,128)S(1)}, bf16[4,128,512]{2,1,0:T(8,128)(2,1)}, f32[1,128]{1,0:T(1,128)S(1)}) custom-call(s32[1]{0:T(128)S(6)} %copy.20.leave_ref, s32[4,4]{1,0:T(4,128)S(1)} %copy-done.5, s32[4]{0:T(128)S(1)} %copy-done.6, bf16[4,1280]{1,0:T(4,128)(2,1)S(1)} %copy-done.3, bf16[16,128,512]{2,1,0:T(8,128)(2,1)S(1)} %copy-done, ...), custom_call_target="tpu_custom_call" | custom-call | flops 76546048 | bytes 4456448 | tf_op jit(solution)/shard_map/attend/pallas_call | solution.py:244
  16.7 0.1 collective-permute-start
  16.8 0.0 copy-done.9
  16.8 0.1 copy.18.gates_ref
  16.9 0.0 copy-done.8
  16.9 0.1 copy.17.ids_ref
  17.0 0.0 copy-done.7
  17.0 0.9 %collective-permute-done.parts_refs_1_ = f32[4,1536]{1,0:T(4,128)S(1)} collective-permute-done((f32[4,1536]{1,0:T(4,128)S(1)}, f32[4,1536]{1,0:T(4,128)S(1)}, u32[]{:S(2)}, u32[]{:S(2)}) %collective-permute-start) | collective-permute-done | bytes 24608 | tf_op jit(solution)/shard_map/ppermute | solution.py:455
  17.9 0.0 copy-done.2
  17.9 0.0 copy-done.4
  17.9 0.0 copy-start.1
  18.0 1.4 %copy-done.1 = bf16[1,1536,512]{2,1,0:T(8,128)(2,1)S(1)} copy-done((bf16[1,1536,512]{2,1,0:T(8,128)(2,1)S(1)}, bf16[1,1536,512]{2,1,0:T(8,128)(2,1)}, u32[]{:S(2)}) %copy-start.1) | copy-done | bytes 1572888
  19.4 0.6 %experts.1 = (f32[4,1536]{1,0:T(4,128)S(1)}, f32[4,1536]{1,0:T(4,128)S(1)}) custom-call(s32[1]{0:T(128)} %bitcast.tp_ref.index_ref, s32[4,1]{1,0:T(4,128)S(1)} %copy.17.ids_ref, bf16[4,1]{1,0:T(4,128)(2,1)S(1)} %copy.18.gates_ref, bf16[4,1536]{1,0:T(4,128)(2,1)S(1)} %copy-done.4, f32[1,1536]{1,0:T(1,128)S(1)} %broadcast_in_dim.11.gain_ref, ...), custom_call_target="tpu_custom_call" | custom-call | flops 9437184 | bytes 2359296 | tf_op jit(solution)/shard_map/experts/pallas_call | solution.py:292
  19.9 0.2 collective-permute-start.1
  20.2 1.0 %collective-permute-done.1 = f32[4,768]{1,0:T(4,128)S(1)} collective-permute-done((f32[4,768]{1,0:T(4,128)S(1)}, f32[4,768]{1,0:T(4,128)S(1)}, u32[]{:S(2)}, u32[]{:S(2)}) %collective-permute-start.1) | collective-permute-done | bytes 12320 | tf_op jit(solution)/shard_map/ppermute | solution.py:467
  21.2 4.1 %all-to-all-done.landed_ref = bf16[16,32,512]{2,1,0:T(8,128)(2,1)S(1)} async-done(((bf16[16,32,512]{2,1,0:T(8,128)(2,1)}), bf16[16,32,512]{2,1,0:T(8,128)(2,1)S(1)}, u32[]{:S(2)}, u32[]{:S(2)}) %all-to-all-start) | async-done | bytes 524320 | tf_op jit(solution)/shard_map/all_to_all | solution.py:441
  25.2 0.2 forward.1
  25.5 17.2 %all_to_all.10.landed_ref = bf16[16,136,128]{2,1,0:T(8,128)(2,1)S(1)} all-to-all(bf16[16,136,128]{2,1,0:T(8,128)(2,1)S(1)} %forward.1), channel_id=1, replica_groups={{6,16,4,0,8,10,12,26,2,30,20,22,28,14,24,18},{21,19,25,23,9,31,17,13,5,..., dimensions={0} | all-to-all | bytes 1114112 | tf_op jit(solution)/shard_map/all_to_all | solution.py:441
  42.7 0.9 %settle.1 = (bf16[4,768]{1,0:T(4,128)(2,1)}, bf16[4,128,512]{2,1,0:T(8,128)(2,1)}, bf16[4,128,512]{2,1,0:T(8,128)(2,1)}) custom-call(s32[1]{0:T(128)S(6)} %copy.20.leave_ref, s32[1]{0:T(128)} %bitcast.tp_ref.index_ref, bf16[16,136,128]{2,1,0:T(8,128)(2,1)S(1)} %all_to_all.10.landed_ref, ...), custom_call_target="tpu_custom_call", output_to_operand_aliasing={{1}: (4, {})} | custom-call | tf_op jit(solution)/shard_map/settle/pallas_call | solution.py:398
  (3 shorter events, 0.0 us)
Async XLA Ops:
  0.6 12.4 %copy-start.3 = (bf16[4,1280]{1,0:T(4,128)(2,1)S(1)}, bf16[4,1280]{1,0:T(4,128)(2,1)}, u32[]{:S(2)}) copy-start(bf16[4,1280]{1,0:T(4,128)(2,1)} %qkv_ref) | copy-start | bytes 30724
  0.6 12.4 %copy-start.6 = (s32[4]{0:T(128)S(1)}, s32[4]{0:T(128)}, u32[]{:S(2)}) copy-start(s32[4]{0:T(128)} %lens_ref.1) | copy-start | bytes 52
  0.7 12.4 %copy-start.5 = (s32[4,4]{1,0:T(4,128)S(1)}, s32[4,4]{1,0:T(4,128)}, u32[]{:S(2)}) copy-start(s32[4,4]{1,0:T(4,128)} %table_ref.1) | copy-start | bytes 196
  0.7 12.4 %copy-start = (bf16[16,128,512]{2,1,0:T(8,128)(2,1)S(1)}, bf16[16,128,512]{2,1,0:T(8,128)(2,1)}, u32[]{:S(2)}) copy-start(bf16[16,128,512]{2,1,0:T(8,128)(2,1)} %pool_ref.2) | copy-start | bytes 6291460
  4.7 20.6 %all-to-all-start = ((bf16[16,32,512]{2,1,0:T(8,128)(2,1)}), bf16[16,32,512]{2,1,0:T(8,128)(2,1)S(1)}, u32[]{:S(2)}, u32[]{:S(2)}) async-start(bf16[16,32,512]{2,1,0:T(8,128)(2,1)} %bitcast.3), calls=%async_computation | async-start | bytes 1048576 | tf_op jit(solution)/shard_map/all_to_all | solution.py:441
  13.0 3.7 %copy-start.9 = (bf16[4,1]{0,1:T(2,128)(2,1)S(1)}, bf16[4,1]{0,1:T(2,128)(2,1)}, u32[]{:S(2)}) copy-start(bf16[4,1]{0,1:T(2,128)(2,1)} %param.21) | copy-start | bytes 28
  13.1 3.8 %copy-start.8 = (s32[4,1]{0,1:T(1,128)S(1)}, s32[4,1]{0,1:T(1,128)}, u32[]{:S(2)}) copy-start(s32[4,1]{0,1:T(1,128)} %param.20) | copy-start | bytes 52
  13.1 3.9 %copy-start.7 = (f32[1536]{0:T(1024)S(1)}, f32[1536]{0:T(1024)}, u32[]{:S(2)}) copy-start(f32[1536]{0:T(1024)} %param.22) | copy-start | bytes 18436
  13.1 4.9 %copy-start.2 = (bf16[1,256,1536]{2,1,0:T(8,128)(2,1)S(1)}, bf16[1,256,1536]{2,1,0:T(8,128)(2,1)}, u32[]{:S(2)}) copy-start(bf16[1,256,1536]{2,1,0:T(8,128)(2,1)} %down_ref.1) | copy-start | bytes 2359300
  13.1 4.9 %copy-start.4 = (bf16[4,1536]{1,0:T(4,128)(2,1)S(1)}, bf16[4,1536]{1,0:T(4,128)(2,1)}, u32[]{:S(2)}) copy-start(bf16[4,1536]{1,0:T(4,128)(2,1)} %resid_ref.1) | copy-start | bytes 36868
  16.7 1.3 %collective-permute-start = (f32[4,1536]{1,0:T(4,128)S(1)}, f32[4,1536]{1,0:T(4,128)S(1)}, u32[]{:S(2)}, u32[]{:S(2)}) collective-permute-start(f32[4,1536]{1,0:T(4,128)S(1)} %get-tuple-element.17.parts_refs_0_), channel_id=1, source_target_pairs={{0,1},{1,0},{2,3},{3,2},{4,5},{5,4},{6,7},{7,6},{8,9},{9,8},{10,11... | collective-permute-start | bytes 73736 | tf_op jit(solution)/shard_map/ppermute | solution.py:455
  17.9 1.4 %copy-start.1 = (bf16[1,1536,512]{2,1,0:T(8,128)(2,1)S(1)}, bf16[1,1536,512]{2,1,0:T(8,128)(2,1)}, u32[]{:S(2)}) copy-start(bf16[1,1536,512]{2,1,0:T(8,128)(2,1)} %in_ref.1) | copy-start | bytes 4718596
  19.9 1.2 %collective-permute-start.1 = (f32[4,768]{1,0:T(4,128)S(1)}, f32[4,768]{1,0:T(4,128)S(1)}, u32[]{:S(2)}, u32[]{:S(2)}) collective-permute-start(f32[4,768]{1,0:T(4,128)S(1)} %constant_dynamic-slice_fusion), channel_id=1, source_target_pairs={{0,1},{1,0},{2,3},{3,2},{4,5},{5,4},{6,7},{7,6},{8,9},{9,8},{10,11... | collective-permute-start | bytes 36872 | tf_op jit(solution)/shard_map/ppermute | solution.py:467
